TPU v7x, 32 devices: a whole 2x2x4 slice. The times are simulated.
32 devices in a mesh: fsdp: 4 (over x, core), ctx: 4 (over z), tp: 2 (over y).
Axes of the slice: x: 2, y: 2, z: 4, core: 2. Of those that a mesh axis runs over, the one named last changes fastest.
Arguments:
- tokens: bfloat16 [16384, 2560], P(('fsdp', 'ctx')), may hold values from -6 to 6
- query_weight: bfloat16 [2560, 2560], P(('fsdp', 'ctx'), 'tp'), may hold values from -0.125 to 0.125
- keyval_weight: bfloat16 [2560, 512], P(('fsdp', 'ctx')), may hold values from -0.125 to 0.125
- out_weight: bfloat16 [2560, 2560], P(('fsdp', 'ctx'), 'tp'), may hold values from -3.5 to 3.5
- gate_weight: bfloat16 [2560, 7680], P(('fsdp', 'ctx'), 'tp'), may hold values from -0.125 to 0.125
- up_weight: bfloat16 [2560, 7680], P(('fsdp', 'ctx'), 'tp'), may hold values from -0.125 to 0.125
- down_weight: bfloat16 [2560, 7680], P(('fsdp', 'ctx'), 'tp'), may hold values from -0.125 to 0.125
- first_gain: bfloat16 [2560], P(('fsdp', 'ctx')), may hold values from -0.8984375 to 0.8984375
- second_gain: bfloat16 [2560], P(('fsdp', 'ctx')), may hold values from -0.8984375 to 0.8984375
- cotangent: bfloat16 [16384, 2560], P(('fsdp', 'ctx')), may hold values from -6 to 6
Outputs:
- output: bfloat16 [16384, 2560], P(('fsdp', 'ctx'))
- input_grad: bfloat16 [16384, 2560], P(('fsdp', 'ctx'))
- query_grad: float32 [2560, 2560], P(('fsdp', 'ctx'), 'tp')
- keyval_grad: float32 [2560, 512], P(('fsdp', 'ctx'))
- out_grad: float32 [2560, 2560], P(('fsdp', 'ctx'), 'tp')
- gate_grad: float32 [2560, 7680], P(('fsdp', 'ctx'), 'tp')
- up_grad: float32 [2560, 7680], P(('fsdp', 'ctx'), 'tp')
- down_grad: float32 [2560, 7680], P(('fsdp', 'ctx'), 'tp')
- first_grad: float32 [2560], P(('fsdp', 'ctx'))
- second_grad: float32 [2560], P(('fsdp', 'ctx'))
All inputs are finite; a program needn't handle non-finite values.
Results may differ from a plain program's by a relative error of at most 0.018.
Values may be sent and summed in bfloat16 or wider, within the bound.
A program may use at most 448 MiB of HBM per device.

v0:
```python
import jax
import jax.numpy as jnp
from jax import lax
from jax.sharding import PartitionSpec as P

HD = 256
W = 2048


EPS = 1e-06
FAR = -1e30
CONTRACT_ROWS = (((0,), (0,)), ((), ()))
CONTRACT_LAST = (((1,), (1,)), ((), ()))


def shifted(array, axis, by):
    count = lax.axis_size(axis)
    pairs = [(i, i + by) for i in range(count) if 0 <= i + by < count]
    return lax.ppermute(array, axis, pairs)


def rms_parts(values, gain):
    inverse = lax.rsqrt(jnp.mean(values * values, axis=-1, keepdims=True) + EPS)
    return (values * inverse * (1.0 + gain.astype(jnp.float32)), inverse)


def rms_back(values, gain, inverse, grad_out):
    scaled = grad_out * (1.0 + gain.astype(jnp.float32))
    along = jnp.mean(scaled * values, axis=-1, keepdims=True)
    grad_in = inverse * scaled - values * inverse * inverse * inverse * along
    grad_gain = jnp.sum(grad_out * values * inverse, axis=0)
    return (grad_in, grad_gain)


def matmul(left, right):
    return jnp.dot(left, right, preferred_element_type=jnp.float32)


def rows_product(left, right):
    return lax.dot_general(left, right, CONTRACT_ROWS, preferred_element_type=jnp.float32)


def right_transposed(left, right):
    return lax.dot_general(left, right, CONTRACT_LAST, preferred_element_type=jnp.float32)


def geglu(gate, upward):
    return jax.nn.gelu(gate, approximate=True) * upward


def window_live(place, rows, hops):
    query_pos = place * rows + jnp.arange(rows, dtype=jnp.int32)
    key_pos = (place - hops) * rows + jnp.arange((hops + 1) * rows, dtype=jnp.int32)
    gap = query_pos[:, None] - key_pos[None, :]
    return (gap >= 0) & (gap < W) & (key_pos[None, :] >= 0)


def masked_scores(queries3, keys, live):
    scores = jnp.einsum("qhd,kd->hqk", queries3, keys, preferred_element_type=jnp.float32)
    return jnp.where(live[None], scores, FAR)


def on_device(
    tokens,
    query_weight,
    keyval_weight,
    out_weight,
    gate_weight,
    up_weight,
    down_weight,
    first_gain,
    second_gain,
    cotangent,
):
    rows = tokens.shape[0]
    heads = query_weight.shape[1] // HD
    scale = HD ** (-0.5)
    hops = min(-(-W // rows), lax.axis_size("ctx") - 1)
    place = lax.axis_index("ctx")
    plan = []
    have = 1
    while have < hops + 1:
        count = min(have, hops + 1 - have)
        plan.append((have, count))
        have = have + count
    shards = (
        query_weight,
        keyval_weight,
        out_weight,
        gate_weight,
        up_weight,
        down_weight,
        first_gain,
        second_gain,
    )
    gathered = (
        lax.all_gather(shards[0], ("fsdp", "ctx"), axis=0, tiled=True),
        lax.all_gather(shards[1], ("fsdp", "ctx"), axis=0, tiled=True),
        lax.all_gather(shards[2], ("fsdp", "ctx"), axis=0, tiled=True),
        lax.all_gather(shards[3], ("fsdp", "ctx"), axis=0, tiled=True),
        lax.all_gather(shards[4], ("fsdp", "ctx"), axis=0, tiled=True),
        lax.all_gather(shards[5], ("fsdp", "ctx"), axis=0, tiled=True),
        lax.all_gather(shards[6], ("fsdp", "ctx"), axis=0, tiled=True),
        lax.all_gather(shards[7], ("fsdp", "ctx"), axis=0, tiled=True),
    )
    query_full, keyval_full, out_full, gate_full, up_full, down_full, gain_one, gain_two = gathered
    source = tokens.astype(jnp.float32)
    first_norm, first_inverse = rms_parts(source, gain_one)
    first_low = first_norm.astype(jnp.bfloat16)
    queries = (matmul(first_low, query_full) * scale).astype(jnp.bfloat16)
    keyval = matmul(first_low, keyval_full).astype(jnp.bfloat16)

    def carry_back(step, state):
        moving, window = state
        moving = shifted(moving, "ctx", 1)
        window = lax.dynamic_update_slice_in_dim(window, moving, (hops - 1 - step) * rows, 0)
        return (moving, window)

    window = jnp.zeros(((hops + 1) * rows, keyval.shape[1]), jnp.bfloat16)
    window = lax.dynamic_update_slice_in_dim(window, keyval, hops * rows, 0)
    moving, window = lax.fori_loop(0, hops, carry_back, (keyval, window))
    keys = window[:, :HD]
    values = window[:, HD:]
    live = window_live(place, rows, hops)
    queries3 = queries.reshape(rows, heads, HD)
    scores = masked_scores(queries3, keys, live)
    top = jnp.max(scores, axis=-1, keepdims=True)
    weights = jnp.exp(scores - top)
    total = jnp.sum(weights, axis=-1, keepdims=True)
    probs = weights / total
    log_total = top + jnp.log(total)
    attended = jnp.einsum(
        "hqk,kd->qhd", probs.astype(jnp.bfloat16), values, preferred_element_type=jnp.float32
    )
    attended = attended.reshape(rows, heads * HD).astype(jnp.bfloat16)
    branch = lax.psum(right_transposed(attended, out_full), "tp")
    middle = source + branch
    second_norm, second_inverse = rms_parts(middle, gain_two)
    second_low = second_norm.astype(jnp.bfloat16)
    gate = matmul(second_low, gate_full)
    upward = matmul(second_low, up_full)
    hidden = geglu(gate, upward).astype(jnp.bfloat16)
    feed = lax.psum(right_transposed(hidden, down_full).astype(jnp.bfloat16), "tp").astype(
        jnp.float32
    )
    output = (middle + feed).astype(jnp.bfloat16)
    regathered = (
        lax.all_gather(shards[0], ("fsdp", "ctx"), axis=0, tiled=True),
        lax.all_gather(shards[1], ("fsdp", "ctx"), axis=0, tiled=True),
        lax.all_gather(shards[2], ("fsdp", "ctx"), axis=0, tiled=True),
        lax.all_gather(shards[3], ("fsdp", "ctx"), axis=0, tiled=True),
        lax.all_gather(shards[4], ("fsdp", "ctx"), axis=0, tiled=True),
        lax.all_gather(shards[5], ("fsdp", "ctx"), axis=0, tiled=True),
        lax.all_gather(shards[6], ("fsdp", "ctx"), axis=0, tiled=True),
        lax.all_gather(shards[7], ("fsdp", "ctx"), axis=0, tiled=True),
    )
    query_full, keyval_full, out_full, gate_full, up_full, down_full, gain_one, gain_two = (
        regathered
    )
    down_grad = rows_product(cotangent, hidden)
    grad_hidden = matmul(cotangent, down_full)
    unused, geglu_back = jax.vjp(geglu, gate, upward)
    gate_part, up_part = geglu_back(grad_hidden)
    gate_back = gate_part.astype(jnp.bfloat16)
    up_back = up_part.astype(jnp.bfloat16)
    gate_grad = rows_product(second_low, gate_back)
    up_grad = rows_product(second_low, up_back)
    grad_second = lax.psum(
        (right_transposed(gate_back, gate_full) + right_transposed(up_back, up_full)).astype(
            jnp.bfloat16
        ),
        "tp",
    ).astype(jnp.float32)
    middle_part, second_grad = rms_back(middle, gain_two, second_inverse, grad_second)
    grad_middle = cotangent.astype(jnp.float32) + middle_part
    gate_grad, up_grad, down_grad, second_grad = (
        lax.psum_scatter(gate_grad, ("fsdp", "ctx"), scatter_dimension=0, tiled=True),
        lax.psum_scatter(up_grad, ("fsdp", "ctx"), scatter_dimension=0, tiled=True),
        lax.psum_scatter(down_grad, ("fsdp", "ctx"), scatter_dimension=0, tiled=True),
        lax.psum_scatter(second_grad, ("fsdp", "ctx"), scatter_dimension=0, tiled=True),
    )
    middle_low = grad_middle.astype(jnp.bfloat16)
    out_grad = rows_product(middle_low, attended)
    grad_attended = matmul(middle_low, out_full).astype(jnp.bfloat16).reshape(rows, heads, HD)
    again_scores = masked_scores(queries3, keys, live)
    again_probs = jnp.exp(again_scores - log_total)
    grad_probs = jnp.einsum(
        "qhd,kd->hqk", grad_attended, values, preferred_element_type=jnp.float32
    )
    value_back = jnp.einsum(
        "hqk,qhd->kd",
        again_probs.astype(jnp.bfloat16),
        grad_attended,
        preferred_element_type=jnp.float32,
    )
    grad_scores = again_probs * (
        grad_probs - jnp.sum(again_probs * grad_probs, axis=-1, keepdims=True)
    )
    grad_scores = grad_scores.astype(jnp.bfloat16)
    query_part = jnp.einsum("hqk,kd->qhd", grad_scores, keys, preferred_element_type=jnp.float32)
    query_back = (query_part.astype(jnp.bfloat16) * scale).reshape(rows, heads * HD)
    key_back = jnp.einsum("hqk,qhd->kd", grad_scores, queries3, preferred_element_type=jnp.float32)
    window_grad = jnp.concatenate([key_back, value_back], 1)

    def send_back(step, moving):
        moving = shifted(moving.astype(jnp.bfloat16), "ctx", -1).astype(moving.dtype)
        return moving + lax.dynamic_slice_in_dim(window_grad, (step + 1) * rows, rows, 0)

    own_grad = lax.fori_loop(0, hops, send_back, window_grad[:rows])
    keyval_total = lax.psum(own_grad.astype(jnp.bfloat16), "tp")
    query_grad = rows_product(first_low, query_back)
    keyval_grad = rows_product(first_low, keyval_total)
    query_share = lax.psum(
        right_transposed(query_back, query_full).astype(jnp.bfloat16), "tp"
    ).astype(jnp.float32)
    grad_first = query_share + right_transposed(keyval_total, keyval_full)
    source_part, first_grad = rms_back(source, gain_one, first_inverse, grad_first)
    input_grad = (grad_middle + source_part).astype(jnp.bfloat16)
    query_grad, keyval_grad, out_grad, first_grad = (
        lax.psum_scatter(query_grad, ("fsdp", "ctx"), scatter_dimension=0, tiled=True),
        lax.psum_scatter(keyval_grad, ("fsdp", "ctx"), scatter_dimension=0, tiled=True),
        lax.psum_scatter(out_grad, ("fsdp", "ctx"), scatter_dimension=0, tiled=True),
        lax.psum_scatter(first_grad, ("fsdp", "ctx"), scatter_dimension=0, tiled=True),
    )
    return (
        output,
        input_grad,
        query_grad,
        keyval_grad,
        out_grad,
        gate_grad,
        up_grad,
        down_grad,
        first_grad,
        second_grad,
    )


def solution(mesh):
    in_specs = (
        P(("fsdp", "ctx"), None),
        P(("fsdp", "ctx"), "tp"),
        P(("fsdp", "ctx"), None),
        P(("fsdp", "ctx"), "tp"),
        P(("fsdp", "ctx"), "tp"),
        P(("fsdp", "ctx"), "tp"),
        P(("fsdp", "ctx"), "tp"),
        P(("fsdp", "ctx")),
        P(("fsdp", "ctx")),
        P(("fsdp", "ctx"), None),
    )
    out_specs = (
        P(("fsdp", "ctx"), None),
        P(("fsdp", "ctx"), None),
        P(("fsdp", "ctx"), "tp"),
        P(("fsdp", "ctx"), None),
        P(("fsdp", "ctx"), "tp"),
        P(("fsdp", "ctx"), "tp"),
        P(("fsdp", "ctx"), "tp"),
        P(("fsdp", "ctx"), "tp"),
        P(("fsdp", "ctx")),
        P(("fsdp", "ctx")),
    )
    return jax.shard_map(
        on_device, mesh=mesh, in_specs=in_specs, out_specs=out_specs, check_vma=False
    )
```

profile of v0, /device:TPU:0, one launch (start us, length us, event | category | flops | bytes accessed | tf_op | source)
XLA Modules:
  0.0 3154.8 jit_solution(3085243546189729101)
XLA Ops:
  16.8 64.1 %all-reduce.6 = (bf16[2560]{0:T(1024)(128)(2,1)S(1)}, bf16[2560]{0:T(1024)(128)(2,1)}) all-reduce(bf16[2560]{0:T(1024)(128)(2,1)S(1)} %dynamic-update-slice, bf16[2560]{0:T(1024)(128)(2,1)S(1)} %dynamic-update-slice.1), channel_id=1, replica_groups=mesh['fsdp'=4,'ctx'=4,'tp'=2] {'fsdp','ctx'}, use_global_device_ids=true, to_apply=%add.1 | all-reduce | flops 5120 | bytes 20480
  95.5 90.3 %while.28 = (s32[]{:T(128)}, bf16[1024,512]{1,0:T(8,128)(2,1)}, bf16[3072,512]{1,0:T(8,128)(2,1)}, s32[]{:T(128)}, s32[]{:T(128)}, /*index=5*/s32[]{:T(128)}, s32[]{:T(128)}) while((s32[]{:T(128)}, bf16[1024,512]{1,0:T(8,128)(2,1)}, bf16[3072,512]{1,0:T(8,128)(2,1)}, s32[]{:T(128)}, s32[]{:T(128)}, /*index=5*/s32[]{:T(128)}, s32[]{:T(128)}) %tuple.109), condition=%wide.region_2.0_spmd, body=%wide.region_1.0_spmd.sunk | while | flops 7 | bytes 8388787 | solution.py:121
  97.7 38.8 %collective-permute-done = bf16[1024,512]{1,0:T(8,128)(2,1)} collective-permute-done((bf16[1024,512]{1,0:T(8,128)(2,1)}, bf16[1024,512]{1,0:T(8,128)(2,1)}, u32[]{:S(2)}, u32[]{:S(2)}) %collective-permute-start) | collective-permute-done | bytes 1048608 | tf_op jit(solution)/shard_map/while/body/eval_jaxpr/ppermute | solution.py:19
  146.5 34.7 %collective-permute-done = bf16[1024,512]{1,0:T(8,128)(2,1)} collective-permute-done((bf16[1024,512]{1,0:T(8,128)(2,1)}, bf16[1024,512]{1,0:T(8,128)(2,1)}, u32[]{:S(2)}, u32[]{:S(2)}) %collective-permute-start) | collective-permute-done | bytes 1048608 | tf_op jit(solution)/shard_map/while/body/eval_jaxpr/ppermute | solution.py:19
  207.0 24.9 fusion.4
  252.3 26.3 fusion.45
  293.5 248.0 %all-reduce.12.cloned.1.call-done = f32[1024,2560]{1,0:T(8,128)} async-done(((f32[1024,2560]{1,0:T(8,128)}), f32[1024,2560]{1,0:T(8,128)}) %all-reduce.12.cloned.1.call-update) | async-done | bytes 10485776 | tf_op jit(solution)/shard_map/psum | solution.py:136
  560.2 91.7 %all-gather.15.cloned.1.call-done = bf16[2560,3840]{1,0:T(8,128)(2,1)} async-done(((bf16[160,3840]{1,0:T(8,128)(2,1)}), bf16[2560,3840]{1,0:T(8,128)(2,1)}) %all-gather.15.cloned.1.call-update) | async-done | bytes 19660816 | tf_op jit(solution)/shard_map/all_gather | solution.py:101
  651.9 27.0 fusion.63
  678.9 82.7 %all-gather.13.cloned.1.call-done = bf16[2560,3840]{1,0:T(8,128)(2,1)} async-done(((bf16[160,3840]{1,0:T(8,128)(2,1)}), bf16[2560,3840]{1,0:T(8,128)(2,1)}) %all-gather.13.cloned.1.call-update) | async-done | bytes 19660816 | tf_op jit(solution)/shard_map/all_gather | solution.py:100
  761.5 26.6 fusion.62
  788.1 83.2 %all-gather.17.cloned.1.call-done = bf16[2560,3840]{1,0:T(8,128)(2,1)} async-done(((bf16[160,3840]{1,0:T(8,128)(2,1)}), bf16[2560,3840]{1,0:T(8,128)(2,1)}) %all-gather.17.cloned.1.call-update) | async-done | bytes 19660816 | tf_op jit(solution)/shard_map/all_gather | solution.py:102
  871.3 42.4 %multiply_convert_fusion = (bf16[1024,3840]{1,0:T(8,128)(2,1)}, bf16[1024,3840]{1,0:T(8,128)(2,1)}, bf16[1024,3840]{1,0:T(8,128)(2,1)}) fusion(f32[1024,3840]{1,0:T(8,128)} %fusion.62, f32[1024,3840]{1,0:T(8,128)} %fusion.63, bf16[1024,2560]{1,0:T(8,128)(2,1)} %param.23, bf16[2560,3840]{1,0:T(8,128)(2,1)} %all-gather.17.cloned.1.call-done), kind=kOutput, calls=%fused_computation.35 | convolution fusion | flops 20234895360 | bytes 79953920 | tf_op jit(solution)/shard_map/dot_general | solution.py:36
  913.8 24.9 fusion.64
  938.7 24.4 add_convert_fusion
  963.2 26.8 convolution_convert_fusion.1
  990.0 103.8 %all-reduce.14.cloned.1.call-done = bf16[1024,2560]{1,0:T(8,128)(2,1)} async-done(((bf16[1024,2560]{1,0:T(8,128)(2,1)}), bf16[1024,2560]{1,0:T(8,128)(2,1)}) %all-reduce.14.cloned.1.call-update) | async-done | bytes 5242896 | tf_op jit(solution)/shard_map/psum | solution.py:168
  1130.9 26.6 fusion.38
  1157.5 47.6 %fusion = (f32[5,1024]{1,0:T(8,128)S(1)}, f32[3072,1024,5]{1,0,2:T(8,128)}) fusion(f32[3072,1024,5]{1,0,2:T(8,128)} %get-tuple-element.210, f32[5,1024]{1,0:T(8,128)S(1)} %log_add_fusion, pred[1024,3072]{0,1:T(8,128)(4,1)S(1)} %copy-done.1, bf16[1024,5,256]{0,2,1:T(8,128)(2,1)} %bitcast.105, bf16[3072,512]{0,1:T(8,128)(2,1)} %copy.48), kind=kOutput, calls=%fused_computation.5 | convolution fusion | flops 8115973120 | bytes 133210112 | tf_op jit(solution)/shard_map/qhd,kd->hqk/dot_general | solution.py:187
  1205.0 50.2 %fusion.2 = bf16[5,1024,3072]{1,2,0:T(8,128)(2,1)} fusion(f32[3072,1024,5]{1,0,2:T(8,128)} %get-tuple-element.212, f32[3072,1024,5]{1,0,2:T(8,128)} %get-tuple-element.210, f32[5,1024]{1,0:T(8,128)S(1)} %get-tuple-element.211, f32[5,1024]{1,0:T(8,128)S(1)} %log_add_fusion, pred[1024,3072]{0,1:T(8,128)(4,1)S(1)} %copy-done.1), kind=kLoop, calls=%fused_computation.7 | loop fusion | flops 78643200 | bytes 160473088 | tf_op jit(solution)/shard_map/convert_element_type | solution.py:199
  1302.0 55.7 %while.29 = (s32[]{:T(128)}, bf16[1024,512]{1,0:T(8,128)(2,1)}, f32[3072,512]{0,1:T(8,128)}, s32[]{:T(128)}, s32[]{:T(128)}, /*index=5*/s32[]{:T(128)}, s32[]{:T(128)}) while((s32[]{:T(128)}, bf16[1024,512]{1,0:T(8,128)(2,1)}, f32[3072,512]{0,1:T(8,128)}, s32[]{:T(128)}, s32[]{:T(128)}, /*index=5*/s32[]{:T(128)}, s32[]{:T(128)}) %tuple.75), condition=%wide.region_13.14_spmd, body=%wide.region_12.13_spmd.sunk | while | flops 1572870 | bytes 16777384 | solution.py:209
  1358.0 265.8 %all-reduce.16.cloned.1.call-done = (bf16[1024,2560]{1,0:T(8,128)(2,1)}, bf16[1024,2560]{1,0:T(8,128)(2,1)}, bf16[1024,512]{1,0:T(8,128)(2,1)}) async-done(((bf16[1024,2560]{1,0:T(8,128)(2,1)}, bf16[1024,2560]{1,0:T(8,128)(2,1)}, bf16[1024,512]{1,0:T(8,128)(2,1)}), (bf16[1024,2560]{1,0:T(8,128)(2,1)}, bf16[1024,2560]{1,0:T(8,128)(2,1)}, bf16[1024,512]{1,0:T(8,128)(2,1)})) %all-reduce.16.cloned.1.call-update) | async-done | bytes 11534352 | tf_op jit(solution)/shard_map/psum | solution.py:143
  1659.7 29.5 convolution_bitcast_fusion
  1689.3 40.1 %copy.72 = f32[2560,3840]{1,0:T(8,128)} copy(f32[2560,3840]{0,1:T(8,128)} %convolution_bitcast_fusion) | data formatting | bytes 78643200
  1729.5 30.5 fusion.66
  1760.2 29.2 fusion.65
  1800.9 63.4 %all-reduce.5 = (f32[2560]{0:T(1024)S(1)}, f32[2560]{0:T(1024)S(1)}) all-reduce(f32[2560]{0:T(1024)S(1)} %get-tuple-element.181, f32[2560]{0:T(1024)S(1)} %copy-done.17), channel_id=8, replica_groups=mesh['fsdp'=4,'ctx'=4,'tp'=2] {'fsdp','ctx'}, use_global_device_ids=true, to_apply=%region_23.24.clone | all-reduce | flops 5120 | bytes 40960
  1865.6 24.6 fusion.28
  1890.2 106.9 %reduce-scatter.9.cloned.1.call-done = f32[160,1280]{1,0:T(8,128)} async-done(((f32[2560,1280]{1,0:T(8,128)}), f32[160,1280]{1,0:T(8,128)}) %reduce-scatter.9.cloned.1.call-update) | async-done | bytes 819216 | tf_op jit(solution)/shard_map/reduce_scatter | solution.py:220
  1997.1 383.7 %reduce-scatter.19.cloned.1.call-done = f32[160,3840]{1,0:T(8,128)} async-done(((f32[2560,3840]{1,0:T(8,128)}), f32[160,3840]{1,0:T(8,128)}) %reduce-scatter.19.cloned.1.call-update) | async-done | bytes 2457616
  2380.8 383.7 %reduce-scatter.17.cloned.1.call-done = f32[160,3840]{1,0:T(8,128)} async-done(((f32[2560,3840]{1,0:T(8,128)}), f32[160,3840]{1,0:T(8,128)}) %reduce-scatter.17.cloned.1.call-update) | async-done | bytes 2457616 | tf_op jit(solution)/shard_map/reduce_scatter | solution.py:178
  2764.5 383.6 %reduce-scatter.15.cloned.1.call-done = f32[160,3840]{1,0:T(8,128)} async-done(((f32[2560,3840]{1,0:T(8,128)}), f32[160,3840]{1,0:T(8,128)}) %reduce-scatter.15.cloned.1.call-update) | async-done | bytes 2457616 | tf_op jit(solution)/shard_map/reduce_scatter | solution.py:177
  (143 shorter events, 303.1 us)
Async XLA Ops:
  7.2 78.1 %all-gather.7.cloned.1.call-start = ((), (), s32[]{:S(2)}) async-start(), calls=%async_computation.6 | async-start | bytes 2785280 | tf_op jit(solution)/shard_map/all_gather | solution.py:98
  7.9 182.5 %all-gather.9.cloned.1.call-start = ((), (), s32[]{:S(2)}) async-start(), calls=%async_computation.7 | async-start | bytes 6963200 | tf_op jit(solution)/shard_map/all_gather | solution.py:97
  8.7 269.9 %all-gather.11.cloned.1.call-start = ((), (), s32[]{:S(2)}) async-start(), calls=%async_computation.8 | async-start | bytes 6963200 | tf_op jit(solution)/shard_map/all_gather | solution.py:99
  9.4 532.2 %all-reduce.12.cloned.1.call-start = ((), (), s32[]{:S(2)}) async-start(), calls=%async_computation.9 | async-start | bytes 20971520 | tf_op jit(solution)/shard_map/psum | solution.py:136
  13.1 177.3 %copy-start.18 = (f32[1024]{0:T(1024)}, f32[1024]{0:T(1024)S(1)}, u32[]{:S(2)}) copy-start(f32[1024]{0:T(1024)S(1)} %add_rsqrt_fusion.1) | copy-start | bytes 12292
  80.9 109.5 %copy-start.15 = (f32[2560]{0:T(1024)}, f32[2560]{0:T(1024)S(1)}, u32[]{:S(2)}) copy-start(f32[2560]{0:T(1024)S(1)} %convert_add_fusion.4) | copy-start | bytes 30724
  85.3 167.0 %copy-start = (pred[1024,3072]{0,1:T(8,128)(4,1)}, pred[1024,3072]{0,1:T(8,128)(4,1)S(1)}, u32[]{:S(2)}) copy-start(pred[1024,3072]{0,1:T(8,128)(4,1)S(1)} %fusion.18) | copy-start | bytes 9437188
  95.5 41.1 %collective-permute-start = (bf16[1024,512]{1,0:T(8,128)(2,1)}, bf16[1024,512]{1,0:T(8,128)(2,1)}, u32[]{:S(2)}, u32[]{:S(2)}) collective-permute-start(bf16[1024,512]{1,0:T(8,128)(2,1)} %get-tuple-element.262), channel_id=1, source_target_pairs={{0,2},{2,4},{4,6},{1,3},{3,5},{5,7},{8,10},{10,12},{12,14},{9,11},... | collective-permute-start | bytes 3145736 | tf_op jit(solution)/shard_map/while/body/eval_jaxpr/ppermute | solution.py:19
  141.1 40.1 %collective-permute-start = (bf16[1024,512]{1,0:T(8,128)(2,1)}, bf16[1024,512]{1,0:T(8,128)(2,1)}, u32[]{:S(2)}, u32[]{:S(2)}) collective-permute-start(bf16[1024,512]{1,0:T(8,128)(2,1)} %get-tuple-element.262), channel_id=1, source_target_pairs={{0,2},{2,4},{4,6},{1,3},{3,5},{5,7},{8,10},{10,12},{12,14},{9,11},... | collective-permute-start | bytes 3145736 | tf_op jit(solution)/shard_map/while/body/eval_jaxpr/ppermute | solution.py:19
  232.0 20.3 copy-start.9
  252.2 26.3 copy-start.11
  291.5 360.4 %all-gather.15.cloned.1.call-start = ((), (), s32[]{:S(2)}) async-start(), calls=%async_computation.11 | async-start | bytes 20889600 | tf_op jit(solution)/shard_map/all_gather | solution.py:101
  292.1 469.4 %all-gather.13.cloned.1.call-start = ((), (), s32[]{:S(2)}) async-start(), calls=%async_computation.10 | async-start | bytes 20889600 | tf_op jit(solution)/shard_map/all_gather | solution.py:100
  292.7 578.7 %all-gather.17.cloned.1.call-start = ((), (), s32[]{:S(2)}) async-start(), calls=%async_computation.12 | async-start | bytes 20889600 | tf_op jit(solution)/shard_map/all_gather | solution.py:102
  293.4 800.4 %all-reduce.14.cloned.1.call-start = ((), (), s32[]{:S(2)}) async-start(), calls=%async_computation.13 | async-start | bytes 10485760 | tf_op jit(solution)/shard_map/psum | solution.py:168
  293.5 258.7 %copy-start.7 = (f32[2560]{0:T(1024)}, f32[2560]{0:T(1024)S(1)}, u32[]{:S(2)}) copy-start(f32[2560]{0:T(1024)S(1)} %convert_add_fusion.3) | copy-start | bytes 30724
  913.8 24.9 copy-start.24
  938.7 24.5 copy-start.10
  938.7 24.5 copy-start.12
  963.1 660.7 %all-reduce.16.cloned.1.call-start = ((), (), s32[]{:S(2)}) async-start(), calls=%async_computation.20 | async-start | bytes 23068672 | tf_op jit(solution)/shard_map/psum | solution.py:143
  963.2 130.6 %copy-start.8 = (f32[2560]{0:T(1024)S(1)}, f32[2560]{0:T(1024)}, u32[]{:S(2)}) copy-start(f32[2560]{0:T(1024)} %copy-done.7) | copy-start | bytes 30724
  963.2 130.6 %copy-start.14 = (f32[1024]{0:T(1024)S(1)}, f32[1024]{0:T(1024)}, u32[]{:S(2)}) copy-start(f32[1024]{0:T(1024)} %copy-done.13) | copy-start | bytes 12292
  1302.0 27.0 collective-permute-start.1
  1330.3 26.1 collective-permute-start.1
  1357.7 266.1 %copy-start.16 = (f32[2560]{0:T(1024)S(1)}, f32[2560]{0:T(1024)}, u32[]{:S(2)}) copy-start(f32[2560]{0:T(1024)} %copy-done.15) | copy-start | bytes 30724
  1357.7 266.1 %copy-start.19 = (f32[1024]{0:T(1024)S(1)}, f32[1024]{0:T(1024)}, u32[]{:S(2)}) copy-start(f32[1024]{0:T(1024)} %copy-done.18) | copy-start | bytes 12292
  1357.7 532.4 %reduce-scatter.11.cloned.1.call-start = ((), (), s32[]{:S(2)}) async-start(), calls=%async_computation.15 | async-start | bytes 5570560 | tf_op jit(solution)/shard_map/reduce_scatter | solution.py:221
  1632.2 257.9 %reduce-scatter.13.cloned.1.call-start = ((), (), s32[]{:S(2)}) async-start(), calls=%async_computation.16 | async-start | bytes 13926400 | tf_op jit(solution)/shard_map/reduce_scatter | solution.py:222
  1644.9 352.1 %reduce-scatter.9.cloned.1.call-start = ((), (), s32[]{:S(2)}) async-start(), calls=%async_computation.14 | async-start | bytes 13926400 | tf_op jit(solution)/shard_map/reduce_scatter | solution.py:220
  1659.3 721.5 %reduce-scatter.19.cloned.1.call-start = ((), (), s32[]{:S(2)}) async-start(), calls=%async_computation.19 | async-start | bytes 41779200
  1729.4 1035.0 %reduce-scatter.17.cloned.1.call-start = ((), (), s32[]{:S(2)}) async-start(), calls=%async_computation.18 | async-start | bytes 41779200 | tf_op jit(solution)/shard_map/reduce_scatter | solution.py:178
  1760.0 1388.2 %reduce-scatter.15.cloned.1.call-start = ((), (), s32[]{:S(2)}) async-start(), calls=%async_computation.17 | async-start | bytes 41779200 | tf_op jit(solution)/shard_map/reduce_scatter | solution.py:177
  (12 other events, 85.7 us)
Sparse Core Ops, SparseCore 0:
  10.3 46.0 all-gather.6
  58.8 73.9 all-gather.8
  135.0 78.1 all-gather.10
  291.6 249.8 all-reduce.11
  543.0 108.8 all-gather.14
  653.4 108.1 all-gather.12
  763.2 108.1 all-gather.16
  963.2 130.5 all-reduce.13
  1357.9 265.9 all-reduce.15
  1632.3 78.7 reduce-scatter.10
  1715.8 138.6 reduce-scatter.12
  1859.6 137.4 reduce-scatter.8
  2001.9 378.8 reduce-scatter.18
  2385.5 378.9 reduce-scatter.16
  2769.2 378.8 reduce-scatter.14
where the time goes:
time: 3170 us; the launch traced here: 3150 us
  waiting for transfers between devices  2250 us (71%)
  matrix products  516 us (16%)
  other arithmetic  144 us (5%)
  blocking collectives  127 us (4%)
  local copies, waits for them, and re-layouts  88 us (3%)
    unnamed x16, waiting for transfers between devices  388 us
    reduce_scatter x1, waiting for transfers between devices, on_device(): lax.psum_scatter(up_grad, ('fsdp', 'ctx'), scatter_dimension=0, tiled=True)  384 us
    reduce_scatter x1, waiting for transfers between devices, on_device(): lax.psum_scatter(gate_grad, ('fsdp', 'ctx'), scatter_dimension=0, tiled=T...  384 us
    psum x1, waiting for transfers between devices, on_device(): lax.psum(right_transposed(hidden, down_full).astype(jnp.bfloat16), 'tp')  266 us
    psum x1, waiting for transfers between devices, on_device(): branch = lax.psum(right_transposed(attended, out_full), 'tp')  248 us
    dot_general x6, matrix products, matmul(): return jnp.dot(left, right, preferred_element_type=jnp.float32)  128 us
    unnamed x2, blocking collectives  127 us
    dot_general x6, matrix products, rows_product(): lax.dot_general(left, right, CONTRACT_ROWS, preferred_element_type=jnp.fl...  123 us
  transfers between devices with their start and end apart: 19, of which 14 were waited for; matrix products, arithmetic and copies ran while one was open for 13% of the time, Pallas kernels for 0%

commit v1 on v0

v1 whole, which is shorter than its diff:
```python
import functools

import jax
import jax.numpy as jnp
from jax import lax
from jax.experimental import pallas as pl
from jax.experimental.pallas import tpu as pltpu
from jax.sharding import PartitionSpec as P

HD = 256
W = 2048
EPS = 1e-06
FAR = -1e30
LOW = jnp.bfloat16
WIDE = jnp.float32
CONTRACT_ROWS = (((0,), (0,)), ((), ()))
CONTRACT_LAST = (((1,), (1,)), ((), ()))
VMEM = 56 * 1024 * 1024


def matmul(left, right):
    return jnp.dot(left, right, preferred_element_type=WIDE)


def rows_product(left, right):
    return lax.dot_general(left, right, CONTRACT_ROWS, preferred_element_type=WIDE)


def right_transposed(left, right):
    return lax.dot_general(left, right, CONTRACT_LAST, preferred_element_type=WIDE)


def gelu_parts(gate):
    c = 0.7978845608028654
    inner = c * (gate + 0.044715 * gate * gate * gate)
    t = jnp.tanh(inner)
    value = 0.5 * gate * (1.0 + t)
    slope = 0.5 * (1.0 + t) + 0.5 * gate * (1.0 - t * t) * c * (1.0 + 3 * 0.044715 * gate * gate)
    return value, slope


def attend_kernel(place_ref, q_ref, win_ref, out_ref, probs_ref, bias_ref, *, heads, hops, rows, block):
    span = W + block
    start = pl.program_id(0) * block
    first = (hops - place_ref[0]) * rows - start
    row = lax.broadcasted_iota(jnp.int32, (block, span), 0)
    col = lax.broadcasted_iota(jnp.int32, (block, span), 1)
    live = (col > row) & (col <= row + W) & (col >= first)
    bias_ref[...] = jnp.where(live, 0.0, FAR)
    window = pl.ds(pl.multiple_of(start, block), span)
    for h in range(heads):
        cols = slice(h * HD, (h + 1) * HD)
        scores = right_transposed(q_ref[:, cols], win_ref[window, :HD]) + bias_ref[...]
        top = jnp.max(scores, axis=1, keepdims=True)
        weights = jnp.exp(scores - top)
        total = jnp.sum(weights, axis=1, keepdims=True)
        probs_ref[h] = (weights * (1.0 / total)).astype(LOW)
        out_ref[:, cols] = matmul(probs_ref[h], win_ref[window, HD:]).astype(LOW)


def attend(queries, window, place, hops):
    rows, width = queries.shape
    heads = width // HD
    block = min(256, rows)
    span = W + block
    return pl.pallas_call(
        functools.partial(attend_kernel, heads=heads, hops=hops, rows=rows, block=block),
        grid=(rows // block,),
        in_specs=[
            pl.BlockSpec(memory_space=pltpu.SMEM),
            pl.BlockSpec((block, width), lambda i: (i, 0)),
            pl.BlockSpec(window.shape, lambda i: (0, 0)),
        ],
        out_specs=[
            pl.BlockSpec((block, width), lambda i: (i, 0)),
            pl.BlockSpec((heads, block, span), lambda i: (0, i, 0)),
        ],
        out_shape=[
            jax.ShapeDtypeStruct((rows, width), LOW),
            jax.ShapeDtypeStruct((heads, rows, span), LOW),
        ],
        scratch_shapes=[pltpu.VMEM((block, span), WIDE)],
        compiler_params=pltpu.CompilerParams(vmem_limit_bytes=VMEM),
        cost_estimate=pl.CostEstimate(
            flops=4 * rows * span * width, bytes_accessed=2 * heads * rows * span, transcendentals=heads * rows * span
        ),
        name="attend",
    )(place, queries, window)


def attend_back_kernel(q_ref, win_ref, out_ref, probs_ref, back_ref, dq_ref, dwin_ref, ds_ref, *, heads, block):
    span = W + block
    step = pl.program_id(0)

    @pl.when(step == 0)
    def _():
        dwin_ref[...] = jnp.zeros_like(dwin_ref)

    window = pl.ds(pl.multiple_of(step * block, block), span)
    for h in range(heads):
        cols = slice(h * HD, (h + 1) * HD)
        back = back_ref[:, cols]
        along = jnp.sum(back.astype(WIDE) * out_ref[:, cols].astype(WIDE), axis=1, keepdims=True)
        grad_probs = right_transposed(back, win_ref[window, HD:])
        ds_ref[h] = (probs_ref[h].astype(WIDE) * (grad_probs - along)).astype(LOW)
        dq = matmul(ds_ref[h], win_ref[window, :HD]).astype(LOW)
        dq_ref[:, cols] = (dq.astype(WIDE) * HD ** (-0.5)).astype(LOW)
    queries = jnp.concatenate([q_ref[:, h * HD : (h + 1) * HD] for h in range(heads)], axis=0)
    backs = jnp.concatenate([back_ref[:, h * HD : (h + 1) * HD] for h in range(heads)], axis=0)
    dwin_ref[window, :HD] += rows_product(ds_ref[...].reshape(heads * block, span), queries)
    dwin_ref[window, HD:] += rows_product(probs_ref[...].reshape(heads * block, span), backs)


def attend_back(queries, window, attended, probs, grad_attended):
    rows, width = queries.shape
    heads = width // HD
    block = min(256, rows)
    span = W + block
    by_rows = pl.BlockSpec((block, width), lambda i: (i, 0))
    return pl.pallas_call(
        functools.partial(attend_back_kernel, heads=heads, block=block),
        grid=(rows // block,),
        in_specs=[
            by_rows,
            pl.BlockSpec(window.shape, lambda i: (0, 0)),
            by_rows,
            pl.BlockSpec((heads, block, span), lambda i: (0, i, 0)),
            by_rows,
        ],
        out_specs=[by_rows, pl.BlockSpec(window.shape, lambda i: (0, 0))],
        out_shape=[
            jax.ShapeDtypeStruct((rows, width), LOW),
            jax.ShapeDtypeStruct(window.shape, WIDE),
        ],
        scratch_shapes=[pltpu.VMEM((heads, block, span), LOW)],
        compiler_params=pltpu.CompilerParams(vmem_limit_bytes=VMEM),
        cost_estimate=pl.CostEstimate(
            flops=8 * rows * span * width, bytes_accessed=2 * heads * rows * span, transcendentals=0
        ),
        name="attend_back",
    )(queries, window, attended, probs, grad_attended)


def swap(array, axis, flip):
    count = lax.axis_size(axis)
    return lax.ppermute(array, axis, [(i, i ^ flip) for i in range(count)])


def from_place(array, by):
    count = lax.axis_size("ctx")
    return lax.ppermute(array, "ctx", [(i, i + by) for i in range(count) if 0 <= i + by < count])


def tp_sum(partial):
    own = partial.astype(LOW)
    return own.astype(WIDE) + swap(own, "tp", 1).astype(WIDE)


def scattered_product(left, right):
    place = lax.axis_index("fsdp")
    span = left.shape[1] // lax.axis_size("fsdp")

    def part(flip):
        return lax.dynamic_slice_in_dim(left, (place ^ flip) * span, span, 1)

    away = rows_product(jnp.concatenate([part(3), part(1)], axis=1), right).astype(LOW)
    got = swap(away, "fsdp", 1)
    far = (rows_product(part(2), right) + got[:span].astype(WIDE)).astype(LOW)
    arrived = swap(far, "fsdp", 2)
    near = rows_product(part(0), right) + got[span:].astype(WIDE) + arrived.astype(WIDE)
    return lax.psum_scatter(near.astype(LOW), "ctx", scatter_dimension=0, tiled=True).astype(WIDE)


def gathered(shard):
    return lax.all_gather(shard, ("fsdp", "ctx"), axis=0, tiled=True)


def on_device(
    tokens,
    query_weight,
    keyval_weight,
    out_weight,
    gate_weight,
    up_weight,
    down_weight,
    first_gain,
    second_gain,
    cotangent,
):
    rows = tokens.shape[0]
    width = query_weight.shape[1]
    scale = HD ** (-0.5)
    hops = min(-(-W // rows), lax.axis_size("ctx") - 1)
    place = lax.axis_index("ctx")

    gains = jnp.pad(jnp.stack([first_gain, second_gain], axis=1), ((0, 0), (0, 126)))
    qkv_full = gathered(jnp.concatenate([query_weight, keyval_weight, gains], axis=1))
    out_full = gathered(out_weight)
    gate_full = gathered(gate_weight)
    up_full = gathered(up_weight)
    down_full = gathered(down_weight)
    query_full = qkv_full[:, :width]
    keyval_full = qkv_full[:, width : width + 2 * HD]
    both_gains = 1.0 + qkv_full[:, width + 2 * HD :][:, :2].astype(WIDE).T
    gain_one, gain_two = both_gains[:1], both_gains[1:]

    source = tokens.astype(WIDE)
    first_inverse = lax.rsqrt(jnp.mean(source * source, axis=-1, keepdims=True) + EPS)
    first_low = (source * first_inverse * gain_one).astype(LOW)
    keyval = matmul(first_low, keyval_full).astype(LOW)
    before = [from_place(keyval, by) for by in range(hops, 0, -1)]
    queries = (matmul(first_low, query_full) * scale).astype(LOW)
    window = jnp.concatenate(before + [keyval], axis=0)
    attended, probs = attend(queries, window, place.reshape(1), hops)
    middle = source + tp_sum(right_transposed(attended, out_full))
    second_inverse = lax.rsqrt(jnp.mean(middle * middle, axis=-1, keepdims=True) + EPS)
    second_low = (middle * second_inverse * gain_two).astype(LOW)
    gate = matmul(second_low, gate_full)
    upward = matmul(second_low, up_full)
    value, slope = gelu_parts(gate)
    hidden = (value * upward).astype(LOW)
    to_up = value.astype(LOW)
    to_gate = (slope * upward).astype(LOW)
    output = (middle + tp_sum(right_transposed(hidden, down_full))).astype(LOW)

    down_grad = scattered_product(cotangent, hidden)
    grad_hidden = matmul(cotangent, down_full)
    gate_back = (grad_hidden * to_gate.astype(WIDE)).astype(LOW)
    up_back = (grad_hidden * to_up.astype(WIDE)).astype(LOW)
    grad_second = tp_sum(right_transposed(gate_back, gate_full) + right_transposed(up_back, up_full))
    gate_grad = scattered_product(second_low, gate_back)
    up_grad = scattered_product(second_low, up_back)

    scaled = grad_second * gain_two
    along = jnp.mean(scaled * middle, axis=-1, keepdims=True)
    grad_middle = (
        cotangent.astype(WIDE)
        + second_inverse * scaled
        - middle * second_inverse * second_inverse * second_inverse * along
    )
    middle_low = grad_middle.astype(LOW)
    grad_attended = matmul(middle_low, out_full).astype(LOW)
    out_grad = scattered_product(middle_low, attended)
    query_back, window_back = attend_back(queries, window, attended, probs, grad_attended)
    own = window_back[hops * rows :]
    for by in range(1, hops + 1):
        sent = window_back[(hops - by) * rows : (hops - by + 1) * rows].astype(LOW)
        own = own + from_place(sent, -by).astype(WIDE)
    keyval_back = tp_sum(own).astype(LOW)
    query_share = tp_sum(right_transposed(query_back, query_full))
    qkv_grad = scattered_product(first_low, jnp.concatenate([query_back, keyval_back], axis=1))
    query_grad = qkv_grad[:, :width]
    keyval_grad = qkv_grad[:, width:]
    grad_first = query_share + right_transposed(keyval_back, keyval_full)
    scaled = grad_first * gain_one
    along = jnp.mean(scaled * source, axis=-1, keepdims=True)
    input_grad = (
        grad_middle
        + first_inverse * scaled
        - source * first_inverse * first_inverse * first_inverse * along
    ).astype(LOW)

    def row_sum(weight, grad):
        return jnp.sum(weight.astype(WIDE) * grad, axis=1)

    sums = jnp.stack(
        [
            row_sum(query_weight, query_grad),
            row_sum(gate_weight, gate_grad) + row_sum(up_weight, up_grad),
        ]
    )
    sums = sums + swap(sums, "tp", 1)
    first_grad = (sums[0] + row_sum(keyval_weight, keyval_grad)) / (1.0 + first_gain.astype(WIDE))
    second_grad = sums[1] / (1.0 + second_gain.astype(WIDE))
    return (
        output,
        input_grad,
        query_grad,
        keyval_grad,
        out_grad,
        gate_grad,
        up_grad,
        down_grad,
        first_grad,
        second_grad,
    )


def solution(mesh):
    rows = P(("fsdp", "ctx"), None)
    split = P(("fsdp", "ctx"), "tp")
    vector = P(("fsdp", "ctx"))
    return jax.shard_map(
        on_device,
        mesh=mesh,
        in_specs=(rows, split, rows, split, split, split, split, vector, vector, rows),
        out_specs=(rows, rows, split, rows, split, split, split, split, vector, vector),
        check_vma=False,
    )
```

time: 3170 us -> 1630 us (0.51)
  waiting for transfers between devices: 2250 us -> 1010 us
  matrix products: 516 us -> 373 us
  blocking collectives: 127 us -> 0 us
  local copies, waits for them, and re-layouts: 88 us -> 9.94 us
  Pallas kernels: 0 us -> 61.9 us
    reduce_scatter x5, waiting for transfers between devices: 874 us -> 54.9 us  [scattered_product(): lax.psum_scatter(near.astype(LOW), 'ctx', scatter_dimension=0, tiled=True)]
    ppermute x4 -> x20, waiting for transfers between devices: 114 us -> 757 us  [the longest x16 646 us: swap(): return lax.ppermute(array, axis, [(i, i ^ flip) for i in range(count)])]
    psum x3 -> x0, waiting for transfers between devices: 618 us -> none  [the longest x1 266 us: on_device(): lax.psum(right_transposed(hidden, down_full).astype(jnp.bfloat16), 'tp')]
    unnamed x16 -> x10, waiting for transfers between devices: 388 us -> 2.53 us
    dot_general x24 -> x27, matrix products: 516 us -> 373 us  [the longest x15 146 us: rows_product(): lax.dot_general(left, right, CONTRACT_ROWS, preferred_element_type=WIDE)]
    unnamed x2 -> x0, blocking collectives: 127 us -> none
    all_gather x6 -> x5, waiting for transfers between devices: 258 us -> 195 us  [gathered(): return lax.all_gather(shard, ('fsdp', 'ctx'), axis=0, tiled=True)]
    pallas_call x0 -> x2, Pallas kernels: none -> 61.9 us  [the longest x1 33.5 us: attend_back(): pl.pallas_call(functools.partial(attend_back_kernel, heads=heads, block=b...]
  transfers between devices with their start and end apart: 19 -> 30, of which waited for: 14 -> 18; matrix products, arithmetic and copies ran while one was open for 13% -> 25% of each run, Pallas kernels for 0% -> 4%
where the time goes in v1:
time: 1630 us
  waiting for transfers between devices  1010 us (62%)
  matrix products  373 us (23%)
  other arithmetic  131 us (8%)
  Pallas kernels  61.9 us (4%)
  starting transfers between devices  26.4 us (2%)
    ppermute x16, waiting for transfers between devices, swap(): return lax.ppermute(array, axis, [(i, i ^ flip) for i in range(count)])  646 us
    all_gather x5, waiting for transfers between devices, gathered(): return lax.all_gather(shard, ('fsdp', 'ctx'), axis=0, tiled=True)  195 us
    dot_general x15, matrix products, rows_product(): lax.dot_general(left, right, CONTRACT_ROWS, preferred_element_type=WIDE)  146 us
    dot_general x6, matrix products, matmul(): return jnp.dot(left, right, preferred_element_type=WIDE)  121 us
    ppermute x4, waiting for transfers between devices, from_place(): lax.ppermute(array, 'ctx', [(i, i + by) for i in range(count) if 0 <= i +...  111 us
    dot_general x6, matrix products, right_transposed(): lax.dot_general(left, right, CONTRACT_LAST, preferred_element_type=WIDE)  106 us
    reduce_scatter x5, waiting for transfers between devices, scattered_product(): lax.psum_scatter(near.astype(LOW), 'ctx', scatter_dimension=0, tiled=True)  54.9 us
    convert_element_type x5, other arithmetic, scattered_product(): near.astype(LOW)  38 us
  transfers between devices with their start and end apart: 30, of which 18 were waited for; matrix products, arithmetic and copies ran while one was open for 25% of the time, Pallas kernels for 4%

profile of v1, /device:TPU:0, one launch (start us, length us, event | category | flops | bytes accessed | tf_op | source)
XLA Modules:
  0.0 1627.4 jit_solution(6173611276630582639)
XLA Ops:
  17.0 80.5 %all-gather.6.cloned.1.call-done = bf16[2560,1920]{1,0:T(8,128)(2,1)} async-done(((bf16[160,1920]{1,0:T(8,128)(2,1)}), bf16[2560,1920]{1,0:T(8,128)(2,1)}) %all-gather.6.cloned.1.call-update) | async-done | bytes 9830416 | tf_op jit(solution)/shard_map/all_gather | solution.py:175
  122.4 26.5 %collective-permute-done.1 = bf16[1024,512]{1,0:T(8,128)(2,1)S(1)} collective-permute-done((bf16[1024,512]{1,0:T(8,128)(2,1)S(1)}, bf16[1024,512]{1,0:T(8,128)(2,1)S(1)}, u32[]{:S(2)}, u32[]{:S(2)}) %collective-permute-start.1) | collective-permute-done | bytes 1048608 | tf_op jit(solution)/shard_map/ppermute | solution.py:151
  148.9 42.3 %collective-permute-done = bf16[1024,512]{1,0:T(8,128)(2,1)S(1)} collective-permute-done((bf16[1024,512]{1,0:T(8,128)(2,1)S(1)}, bf16[1024,512]{1,0:T(8,128)(2,1)S(1)}, u32[]{:S(2)}, u32[]{:S(2)}) %collective-permute-start) | collective-permute-done | bytes 1048608 | tf_op jit(solution)/shard_map/ppermute | solution.py:151
  193.0 28.4 %attend.1 = (bf16[1024,1280]{1,0:T(8,128)(2,1)}, bf16[5,1024,2304]{2,1,0:T(8,128)(2,1)}) custom-call(s32[1]{0:T(128)} %bitcast.place_ref, bf16[1024,1280]{1,0:T(8,128)(2,1)} %multiply_convert_fusion.4.q_ref, bf16[3072,512]{1,0:T(8,128)(2,1)} %pad_maximum_fusion.1.win_ref), custom_call_target="tpu_custom_call" | custom-call | flops 12079595520 | bytes 23592960 | tf_op jit(solution)/shard_map/attend/pallas_call | solution.py:66
  234.2 113.2 %collective-permute-done.2 = bf16[1024,2560]{1,0:T(8,128)(2,1)S(1)} collective-permute-done((bf16[1024,2560]{1,0:T(8,128)(2,1)S(1)}, bf16[1024,2560]{1,0:T(8,128)(2,1)S(1)}, u32[]{:S(2)}, u32[]{:S(2)}) %collective-permute-start.2) | collective-permute-done | bytes 5242912 | tf_op jit(solution)/shard_map/ppermute | solution.py:146
  366.1 26.8 %fusion.95 = f32[1024,3840]{1,0:T(8,128)} fusion(bf16[1024,2560]{1,0:T(8,128)(2,1)} %param.19, bf16[2560,3840]{1,0:T(8,128)(2,1)} %all-gather.14.cloned.1.call-done), kind=kOutput, calls=%fused_computation.145 | convolution fusion | flops 20132659200 | bytes 40632320 | tf_op jit(solution)/shard_map/dot_general | solution.py:22
  392.9 32.1 %all-gather.12.cloned.1.call-done = bf16[2560,3840]{1,0:T(8,128)(2,1)} async-done(((bf16[160,3840]{1,0:T(8,128)(2,1)}), bf16[2560,3840]{1,0:T(8,128)(2,1)}) %all-gather.12.cloned.1.call-update) | async-done | bytes 19660816 | tf_op jit(solution)/shard_map/all_gather | solution.py:175
  425.0 26.7 %fusion.94 = f32[1024,3840]{1,0:T(8,128)} fusion(bf16[1024,2560]{1,0:T(8,128)(2,1)} %multiply_convert_fusion.3, bf16[2560,3840]{1,0:T(8,128)(2,1)} %all-gather.12.cloned.1.call-done), kind=kOutput, calls=%fused_computation.144 | convolution fusion | flops 20132659200 | bytes 40632320 | tf_op jit(solution)/shard_map/dot_general | solution.py:22
  451.7 82.8 %all-gather.10.cloned.1.call-done = bf16[2560,3840]{1,0:T(8,128)(2,1)} async-done(((bf16[160,3840]{1,0:T(8,128)(2,1)}), bf16[2560,3840]{1,0:T(8,128)(2,1)}) %all-gather.10.cloned.1.call-update) | async-done | bytes 19660816 | tf_op jit(solution)/shard_map/all_gather | solution.py:175
  534.6 44.1 %multiply_convert_fusion = (bf16[1024,3840]{1,0:T(8,128)(2,1)}, bf16[1024,3840]{1,0:T(8,128)(2,1)}, bf16[1024,3840]{1,0:T(8,128)(2,1)}) fusion(f32[1024,3840]{1,0:T(8,128)} %fusion.95, f32[1024,3840]{1,0:T(8,128)} %fusion.94, bf16[1024,2560]{1,0:T(8,128)(2,1)} %multiply_convert_fusion.3, bf16[2560,3840]{1,0:T(8,128)(2,1)} %all-gather.10.cloned.1.call-done), kind=kOutput, calls=%fused_computation.13 | convolution fusion | flops 20246691840 | bytes 79953920 | tf_op jit(solution)/shard_map/dot_general | solution.py:22
  578.7 27.2 %fusion.96 = f32[1024,2560]{1,0:T(8,128)} fusion(bf16[1024,3840]{1,0:T(8,128)(2,1)} %get-tuple-element.31, bf16[2560,3840]{1,0:T(8,128)(2,1)} %all-gather.10.cloned.1.call-done), kind=kOutput, calls=%fused_computation.146 | convolution fusion | flops 20132659200 | bytes 38010880 | tf_op jit(solution)/shard_map/dot_general | solution.py:30
  606.0 25.4 %add_convert_fusion = bf16[1024,2560]{1,0:T(8,128)(2,1)} fusion(f32[1024,2560]{1,0:T(8,128)} %fusion.96, bf16[1024,3840]{1,0:T(8,128)(2,1)S(1)} %copy-done.2, bf16[2560,3840]{1,0:T(8,128)(2,1)} %all-gather.12.cloned.1.call-done), kind=kOutput, calls=%fused_computation.33 | convolution fusion | flops 20137902080 | bytes 43253760 | tf_op jit(solution)/shard_map/dot_general | solution.py:30
  632.8 24.7 %convolution_convert_fusion.5 = bf16[1024,2560]{1,0:T(8,128)(2,1)} fusion(bf16[1024,3840]{1,0:T(8,128)(2,1)S(1)} %bitcast.50, bf16[2560,3840]{1,0:T(8,128)(2,1)} %all-gather.14.cloned.1.call-done), kind=kOutput, calls=%fused_computation.50 | convolution fusion | flops 20135280640 | bytes 32768000 | tf_op jit(solution)/shard_map/dot_general | solution.py:30
  660.3 18.0 %convolution_convert_fusion.2 = bf16[1280,3840]{1,0:T(8,128)(2,1)} fusion(bf16[1024,3840]{1,0:T(8,128)(2,1)} %get-tuple-element.31, bf16[1024,640]{1,0:T(8,128)(2,1)S(1)} %get-tuple-element.37, bf16[1024,640]{1,0:T(8,128)(2,1)S(1)} %get-tuple-element.36), kind=kOutput, calls=%fused_computation.18 | convolution fusion | flops 10076487680 | bytes 20316160 | tf_op jit(solution)/shard_map/dot_general | solution.py:26
  678.3 69.2 %collective-permute-done.4 = bf16[1024,2560]{1,0:T(8,128)(2,1)} collective-permute-done((bf16[1024,2560]{1,0:T(8,128)(2,1)}, bf16[1024,2560]{1,0:T(8,128)(2,1)}, u32[]{:S(2)}, u32[]{:S(2)}) %collective-permute-start.4) | collective-permute-done | bytes 5242912 | tf_op jit(solution)/shard_map/ppermute | solution.py:146
  754.4 104.8 %collective-permute-done.3 = bf16[1024,2560]{1,0:T(8,128)(2,1)} collective-permute-done((bf16[1024,2560]{1,0:T(8,128)(2,1)}, bf16[1024,2560]{1,0:T(8,128)(2,1)}, u32[]{:S(2)}, u32[]{:S(2)}) %collective-permute-start.3) | collective-permute-done | bytes 5242912 | tf_op jit(solution)/shard_map/ppermute | solution.py:146
  859.2 21.9 %fusion.91 = (bf16[1024,2560]{1,0:T(8,128)(2,1)}, f32[1024,2560]{1,0:T(8,128)}, bf16[1024,2560]{1,0:T(8,128)(2,1)}) fusion(f32[1024]{0:T(1024)S(1)} %broadcast_multiply_fusion.1, bf16[1024,2560]{1,0:T(8,128)(2,1)} %copy-done.1, bf16[1024,2560]{1,0:T(8,128)(2,1)S(1)} %bitcast.44, bf16[1024,2560]{1,0:T(8,128)(2,1)S(1)} %bitcast.40, f32[2560]{0:T(1024)S(1)} %copy-done.16, ...), kind=kLoop, calls=%fused_computation.141 | loop fusion | flops 60293120 | bytes 62932992 | tf_op jit(solution)/shard_map/convert_element_type | solution.py:241
  892.9 33.5 %attend_back.1 = (bf16[1024,1280]{1,0:T(8,128)(2,1)}, f32[3072,512]{1,0:T(8,128)}) custom-call(bf16[1024,1280]{1,0:T(8,128)(2,1)} %multiply_convert_fusion.4.q_ref, bf16[3072,512]{1,0:T(8,128)(2,1)} %pad_maximum_fusion.1.win_ref, bf16[1024,1280]{1,0:T(8,128)(2,1)} %get-tuple-element.14.out_ref, bf16[5,1024,2304]{2,1,0:T(8,128)(2,1)} %get-tuple-element.15.probs_ref, ...), custom_call_target="tpu_custom_call" | custom-call | flops 24159191040 | bytes 23592960 | tf_op jit(solution)/shard_map/attend_back/pallas_call | solution.py:120
  938.3 40.6 %collective-permute-done.7 = bf16[1024,512]{1,0:T(8,128)(2,1)S(1)} collective-permute-done((bf16[1024,512]{1,0:T(8,128)(2,1)S(1)}, bf16[1024,512]{1,0:T(8,128)(2,1)S(1)}, u32[]{:S(2)}, u32[]{:S(2)}) %collective-permute-start.7) | collective-permute-done | bytes 1048608 | tf_op jit(solution)/shard_map/ppermute | solution.py:151
  984.0 22.3 %collective-permute-done.8 = bf16[1024,512]{1,0:T(8,128)(2,1)S(1)} collective-permute-done((bf16[1024,512]{1,0:T(8,128)(2,1)S(1)}, bf16[1024,512]{1,0:T(8,128)(2,1)S(1)}, u32[]{:S(2)}, u32[]{:S(2)}) %collective-permute-start.8) | collective-permute-done | bytes 1048608 | tf_op jit(solution)/shard_map/ppermute | solution.py:146
  1018.9 16.5 %convolution_convert_fusion.1 = bf16[1280,3840]{1,0:T(8,128)(2,1)} fusion(bf16[1024,3840]{1,0:T(8,128)(2,1)} %get-tuple-element.30, bf16[1024,640]{1,0:T(8,128)(2,1)S(1)} %copy-done.11, bf16[1024,640]{1,0:T(8,128)(2,1)S(1)} %copy-done.9), kind=kOutput, calls=%fused_computation.17 | convolution fusion | flops 10076487680 | bytes 20316160 | tf_op jit(solution)/shard_map/dot_general | solution.py:26
  1038.9 16.7 %collective-permute-done.12 = bf16[640,1280]{1,0:T(8,128)(2,1)S(1)} collective-permute-done((bf16[640,1280]{1,0:T(8,128)(2,1)S(1)}, bf16[640,1280]{1,0:T(8,128)(2,1)S(1)}, u32[]{:S(2)}, u32[]{:S(2)}) %collective-permute-start.12) | collective-permute-done | bytes 1638432 | tf_op jit(solution)/shard_map/ppermute | solution.py:146
  1066.2 12.7 add_convert_fusion.7
  1083.6 33.9 %collective-permute-done.10 = bf16[640,1792]{1,0:T(8,128)(2,1)S(1)} collective-permute-done((bf16[640,1792]{1,0:T(8,128)(2,1)S(1)}, bf16[640,1792]{1,0:T(8,128)(2,1)S(1)}, u32[]{:S(2)}, u32[]{:S(2)}) %collective-permute-start.10) | collective-permute-done | bytes 2293792 | tf_op jit(solution)/shard_map/ppermute | solution.py:146
  1137.7 83.9 %collective-permute-done.14 = bf16[640,3840]{1,0:T(8,128)(2,1)} collective-permute-done((bf16[640,3840]{1,0:T(8,128)(2,1)}, bf16[640,3840]{1,0:T(8,128)(2,1)}, u32[]{:S(2)}, u32[]{:S(2)}) %collective-permute-start.14) | collective-permute-done | bytes 4915232 | tf_op jit(solution)/shard_map/ppermute | solution.py:146
  1232.2 16.4 %convolution_convert_fusion = bf16[1280,3840]{1,0:T(8,128)(2,1)} fusion(bf16[1024,3840]{1,0:T(8,128)(2,1)} %get-tuple-element.32, bf16[1024,640]{1,0:T(8,128)(2,1)} %get-tuple-element.35, bf16[1024,640]{1,0:T(8,128)(2,1)S(1)} %get-tuple-element.34), kind=kOutput, calls=%fused_computation.16 | convolution fusion | flops 10076487680 | bytes 20316160 | tf_op jit(solution)/shard_map/dot_general | solution.py:26
  1268.6 99.5 %collective-permute-done.16 = bf16[640,3840]{1,0:T(8,128)(2,1)} collective-permute-done((bf16[640,3840]{1,0:T(8,128)(2,1)S(1)}, bf16[640,3840]{1,0:T(8,128)(2,1)}, u32[]{:S(2)}, u32[]{:S(2)}) %collective-permute-start.16) | collective-permute-done | bytes 4915232 | tf_op jit(solution)/shard_map/ppermute | solution.py:146
  1390.7 12.8 fusion.45
  1414.3 82.6 %collective-permute-done.18 = bf16[640,3840]{1,0:T(8,128)(2,1)} collective-permute-done((bf16[640,3840]{1,0:T(8,128)(2,1)S(1)}, bf16[640,3840]{1,0:T(8,128)(2,1)}, u32[]{:S(2)}, u32[]{:S(2)}) %collective-permute-start.18) | collective-permute-done | bytes 4915232 | tf_op jit(solution)/shard_map/ppermute | solution.py:146
  1507.1 20.1 %collective-permute-done.5 = bf16[1024,2560]{1,0:T(8,128)(2,1)} collective-permute-done((bf16[1024,2560]{1,0:T(8,128)(2,1)}, bf16[1024,2560]{1,0:T(8,128)(2,1)}, u32[]{:S(2)}, u32[]{:S(2)}) %collective-permute-start.5) | collective-permute-done | bytes 5242912 | tf_op jit(solution)/shard_map/ppermute | solution.py:146
  1535.9 12.9 fusion.13
  1561.7 54.9 %reduce-scatter.14.cloned.1.call-done = bf16[160,3840]{1,0:T(8,128)(2,1)} async-done(((bf16[640,3840]{1,0:T(8,128)(2,1)}), bf16[160,3840]{1,0:T(8,128)(2,1)}) %reduce-scatter.14.cloned.1.call-update) | async-done | bytes 1228816 | tf_op jit(solution)/shard_map/reduce_scatter | solution.py:171
  (220 shorter events, 258.1 us)
Async XLA Ops:
  7.2 90.3 %all-gather.6.cloned.1.call-start = ((), (), s32[]{:S(2)}) async-start(), calls=%async_computation.5 | async-start | bytes 10444800 | tf_op jit(solution)/shard_map/all_gather | solution.py:175
  10.7 210.8 %all-gather.8.cloned.1.call-start = ((), (), s32[]{:S(2)}) async-start(), calls=%async_computation.6 | async-start | bytes 6963200 | tf_op jit(solution)/shard_map/all_gather | solution.py:175
  11.4 354.6 %all-gather.14.cloned.1.call-start = ((), (), s32[]{:S(2)}) async-start(), calls=%async_computation.9 | async-start | bytes 20889600 | tf_op jit(solution)/shard_map/all_gather | solution.py:175
  12.2 412.8 %all-gather.12.cloned.1.call-start = ((), (), s32[]{:S(2)}) async-start(), calls=%async_computation.8 | async-start | bytes 20889600 | tf_op jit(solution)/shard_map/all_gather | solution.py:175
  12.8 521.8 %all-gather.10.cloned.1.call-start = ((), (), s32[]{:S(2)}) async-start(), calls=%async_computation.7 | async-start | bytes 20889600 | tf_op jit(solution)/shard_map/all_gather | solution.py:175
  13.3 1535.4 %reduce-scatter.8.cloned.1.call-start = ((), (), s32[]{:S(2)}) async-start(), calls=%async_computation.11 | async-start | bytes 2048000 | tf_op jit(solution)/shard_map/reduce_scatter | solution.py:171
  99.8 254.6 %copy-start.15 = (f32[2560]{0:T(1024)}, f32[2560]{0:T(1024)S(1)}, u32[]{:S(2)}) copy-start(f32[2560]{0:T(1024)S(1)} %get-tuple-element.19) | copy-start | bytes 30724
  108.0 40.9 %collective-permute-start.1 = (bf16[1024,512]{1,0:T(8,128)(2,1)S(1)}, bf16[1024,512]{1,0:T(8,128)(2,1)S(1)}, u32[]{:S(2)}, u32[]{:S(2)}) collective-permute-start(bf16[1024,512]{1,0:T(8,128)(2,1)S(1)} %fusion.38), channel_id=1, source_target_pairs={{0,2},{2,4},{4,6},{1,3},{3,5},{5,7},{8,10},{10,12},{12,14},{9,11},... | collective-permute-start | bytes 3145736 | tf_op jit(solution)/shard_map/ppermute | solution.py:151
  110.6 80.6 %collective-permute-start = (bf16[1024,512]{1,0:T(8,128)(2,1)S(1)}, bf16[1024,512]{1,0:T(8,128)(2,1)S(1)}, u32[]{:S(2)}, u32[]{:S(2)}) collective-permute-start(bf16[1024,512]{1,0:T(8,128)(2,1)S(1)} %fusion.38), channel_id=1, source_target_pairs={{0,4},{2,6},{1,5},{3,7},{8,12},{10,14},{9,13},{11,15},{16,20},{18,... | collective-permute-start | bytes 3145736 | tf_op jit(solution)/shard_map/ppermute | solution.py:151
  232.5 115.0 %collective-permute-start.2 = (bf16[1024,2560]{1,0:T(8,128)(2,1)S(1)}, bf16[1024,2560]{1,0:T(8,128)(2,1)S(1)}, u32[]{:S(2)}, u32[]{:S(2)}) collective-permute-start(bf16[1024,2560]{1,0:T(8,128)(2,1)S(1)} %convolution_convert_fusion.6), channel_id=1, source_target_pairs={{0,1},{1,0},{2,3},{3,2},{4,5},{5,4},{6,7},{7,6},{8,9},{9,8},{10,11... | collective-permute-start | bytes 15728648 | tf_op jit(solution)/shard_map/ppermute | solution.py:146
  631.3 116.2 %collective-permute-start.4 = (bf16[1024,2560]{1,0:T(8,128)(2,1)}, bf16[1024,2560]{1,0:T(8,128)(2,1)}, u32[]{:S(2)}, u32[]{:S(2)}) collective-permute-start(bf16[1024,2560]{1,0:T(8,128)(2,1)} %add_convert_fusion), channel_id=1, source_target_pairs={{0,1},{1,0},{2,3},{3,2},{4,5},{5,4},{6,7},{7,6},{8,9},{9,8},{10,11... | collective-permute-start | bytes 15728648 | tf_op jit(solution)/shard_map/ppermute | solution.py:146
  657.5 201.7 %collective-permute-start.3 = (bf16[1024,2560]{1,0:T(8,128)(2,1)}, bf16[1024,2560]{1,0:T(8,128)(2,1)}, u32[]{:S(2)}, u32[]{:S(2)}) collective-permute-start(bf16[1024,2560]{1,0:T(8,128)(2,1)} %convolution_convert_fusion.5), channel_id=1, source_target_pairs={{0,1},{1,0},{2,3},{3,2},{4,5},{5,4},{6,7},{7,6},{8,9},{9,8},{10,11... | collective-permute-start | bytes 15728648 | tf_op jit(solution)/shard_map/ppermute | solution.py:146
  678.2 181.0 %copy-start.23 = (f32[1024]{0:T(1024)S(1)}, f32[1024]{0:T(1024)}, u32[]{:S(2)}) copy-start(f32[1024]{0:T(1024)} %copy-done.22) | copy-start | bytes 12292
  678.2 388.0 %collective-permute-start.13 = (bf16[1280,3840]{1,0:T(8,128)(2,1)}, bf16[1280,3840]{1,0:T(8,128)(2,1)}, u32[]{:S(2)}, u32[]{:S(2)}) collective-permute-start(bf16[1280,3840]{1,0:T(8,128)(2,1)} %convolution_convert_fusion.2), channel_id=1, source_target_pairs={{0,8},{8,0},{16,24},{24,16},{1,9},{9,1},{17,25},{25,17},{2,10},{10... | collective-permute-start | bytes 29491208 | tf_op jit(solution)/shard_map/ppermute | solution.py:146
  930.0 48.9 %collective-permute-start.7 = (bf16[1024,512]{1,0:T(8,128)(2,1)S(1)}, bf16[1024,512]{1,0:T(8,128)(2,1)S(1)}, u32[]{:S(2)}, u32[]{:S(2)}) collective-permute-start(bf16[1024,512]{1,0:T(8,128)(2,1)S(1)} %get-tuple-element.43), channel_id=1, source_target_pairs={{4,0},{6,2},{5,1},{7,3},{12,8},{14,10},{13,9},{15,11},{20,16},{22,... | collective-permute-start | bytes 3145736 | tf_op jit(solution)/shard_map/ppermute | solution.py:151
  931.4 48.8 %collective-permute-start.6 = (bf16[1024,512]{1,0:T(8,128)(2,1)S(1)}, bf16[1024,512]{1,0:T(8,128)(2,1)S(1)}, u32[]{:S(2)}, u32[]{:S(2)}) collective-permute-start(bf16[1024,512]{1,0:T(8,128)(2,1)S(1)} %get-tuple-element.42), channel_id=1, source_target_pairs={{2,0},{4,2},{6,4},{3,1},{5,3},{7,5},{10,8},{12,10},{14,12},{11,9},... | collective-permute-start | bytes 3145736 | tf_op jit(solution)/shard_map/ppermute | solution.py:151
  938.3 75.1 %collective-permute-start.11 = (bf16[1280,1280]{1,0:T(8,128)(2,1)}, bf16[1280,1280]{1,0:T(8,128)(2,1)}, u32[]{:S(2)}, u32[]{:S(2)}) collective-permute-start(bf16[1280,1280]{1,0:T(8,128)(2,1)} %convolution_convert_fusion.4), channel_id=1, source_target_pairs={{0,8},{8,0},{16,24},{24,16},{1,9},{9,1},{17,25},{25,17},{2,10},{10... | collective-permute-start | bytes 9830408 | tf_op jit(solution)/shard_map/ppermute | solution.py:146
  982.3 24.0 %collective-permute-start.8 = (bf16[1024,512]{1,0:T(8,128)(2,1)S(1)}, bf16[1024,512]{1,0:T(8,128)(2,1)S(1)}, u32[]{:S(2)}, u32[]{:S(2)}) collective-permute-start(bf16[1024,512]{1,0:T(8,128)(2,1)S(1)} %add_convert_fusion.13), channel_id=1, source_target_pairs={{0,1},{1,0},{2,3},{3,2},{4,5},{5,4},{6,7},{7,6},{8,9},{9,8},{10,11... | collective-permute-start | bytes 3145736 | tf_op jit(solution)/shard_map/ppermute | solution.py:146
  1013.4 45.8 %collective-permute-start.9 = (bf16[1280,1792]{1,0:T(8,128)(2,1)}, bf16[1280,1792]{1,0:T(8,128)(2,1)}, u32[]{:S(2)}, u32[]{:S(2)}) collective-permute-start(bf16[1280,1792]{1,0:T(8,128)(2,1)} %convolution_convert_fusion.3), channel_id=1, source_target_pairs={{0,8},{8,0},{16,24},{24,16},{1,9},{9,1},{17,25},{25,17},{2,10},{10... | collective-permute-start | bytes 13762568 | tf_op jit(solution)/shard_map/ppermute | solution.py:146
  1017.3 38.3 %collective-permute-start.12 = (bf16[640,1280]{1,0:T(8,128)(2,1)S(1)}, bf16[640,1280]{1,0:T(8,128)(2,1)S(1)}, u32[]{:S(2)}, u32[]{:S(2)}) collective-permute-start(bf16[640,1280]{1,0:T(8,128)(2,1)S(1)} %add_convert_fusion.11), channel_id=1, source_target_pairs={{0,16},{8,24},{16,0},{24,8},{1,17},{9,25},{17,1},{25,9},{2,18},{10... | collective-permute-start | bytes 4915208 | tf_op jit(solution)/shard_map/ppermute | solution.py:146
  1035.4 213.3 %collective-permute-start.15 = (bf16[1280,3840]{1,0:T(8,128)(2,1)}, bf16[1280,3840]{1,0:T(8,128)(2,1)}, u32[]{:S(2)}, u32[]{:S(2)}) collective-permute-start(bf16[1280,3840]{1,0:T(8,128)(2,1)} %convolution_convert_fusion.1), channel_id=1, source_target_pairs={{0,8},{8,0},{16,24},{24,16},{1,9},{9,1},{17,25},{25,17},{2,10},{10... | collective-permute-start | bytes 29491208 | tf_op jit(solution)/shard_map/ppermute | solution.py:146
  1058.8 492.0 %reduce-scatter.6.cloned.1.call-start = ((), (), s32[]{:S(2)}) async-start(), calls=%async_computation.10 | async-start | bytes 2867200 | tf_op jit(solution)/shard_map/reduce_scatter | solution.py:171
  1064.6 52.8 %collective-permute-start.10 = (bf16[640,1792]{1,0:T(8,128)(2,1)S(1)}, bf16[640,1792]{1,0:T(8,128)(2,1)S(1)}, u32[]{:S(2)}, u32[]{:S(2)}) collective-permute-start(bf16[640,1792]{1,0:T(8,128)(2,1)S(1)} %add_convert_fusion.9), channel_id=1, source_target_pairs={{0,16},{8,24},{16,0},{24,8},{1,17},{9,25},{17,1},{25,9},{2,18},{10... | collective-permute-start | bytes 6881288 | tf_op jit(solution)/shard_map/ppermute | solution.py:146
  1078.9 142.6 %collective-permute-start.14 = (bf16[640,3840]{1,0:T(8,128)(2,1)}, bf16[640,3840]{1,0:T(8,128)(2,1)}, u32[]{:S(2)}, u32[]{:S(2)}) collective-permute-start(bf16[640,3840]{1,0:T(8,128)(2,1)} %add_convert_fusion.7), channel_id=1, source_target_pairs={{0,16},{8,24},{16,0},{24,8},{1,17},{9,25},{17,1},{25,9},{2,18},{10... | collective-permute-start | bytes 14745608 | tf_op jit(solution)/shard_map/ppermute | solution.py:146
  1121.5 431.5 %reduce-scatter.10.cloned.1.call-start = ((), (), s32[]{:S(2)}) async-start(), calls=%async_computation.12 | async-start | bytes 6144000 | tf_op jit(solution)/shard_map/reduce_scatter | solution.py:171
  1232.0 324.1 %reduce-scatter.12.cloned.1.call-start = ((), (), s32[]{:S(2)}) async-start(), calls=%async_computation.13 | async-start | bytes 6144000 | tf_op jit(solution)/shard_map/reduce_scatter | solution.py:171
  1248.7 129.9 %collective-permute-start.17 = (bf16[1280,3840]{1,0:T(8,128)(2,1)}, bf16[1280,3840]{1,0:T(8,128)(2,1)}, u32[]{:S(2)}, u32[]{:S(2)}) collective-permute-start(bf16[1280,3840]{1,0:T(8,128)(2,1)} %convolution_convert_fusion), channel_id=1, source_target_pairs={{0,8},{8,0},{16,24},{24,16},{1,9},{9,1},{17,25},{25,17},{2,10},{10... | collective-permute-start | bytes 29491208 | tf_op jit(solution)/shard_map/ppermute | solution.py:146
  1259.5 108.6 %collective-permute-start.16 = (bf16[640,3840]{1,0:T(8,128)(2,1)S(1)}, bf16[640,3840]{1,0:T(8,128)(2,1)}, u32[]{:S(2)}, u32[]{:S(2)}) collective-permute-start(bf16[640,3840]{1,0:T(8,128)(2,1)S(1)} %add_convert_fusion.5), channel_id=1, source_target_pairs={{0,16},{8,24},{16,0},{24,8},{1,17},{9,25},{17,1},{25,9},{2,18},{10... | collective-permute-start | bytes 14745608 | tf_op jit(solution)/shard_map/ppermute | solution.py:146
  1378.3 238.3 %reduce-scatter.14.cloned.1.call-start = ((), (), s32[]{:S(2)}) async-start(), calls=%async_computation.14 | async-start | bytes 6144000 | tf_op jit(solution)/shard_map/reduce_scatter | solution.py:171
  1389.1 107.8 %collective-permute-start.18 = (bf16[640,3840]{1,0:T(8,128)(2,1)S(1)}, bf16[640,3840]{1,0:T(8,128)(2,1)}, u32[]{:S(2)}, u32[]{:S(2)}) collective-permute-start(bf16[640,3840]{1,0:T(8,128)(2,1)S(1)} %add_convert_fusion.3), channel_id=1, source_target_pairs={{0,16},{8,24},{16,0},{24,8},{1,17},{9,25},{17,1},{25,9},{2,18},{10... | collective-permute-start | bytes 14745608 | tf_op jit(solution)/shard_map/ppermute | solution.py:146
  1412.5 114.7 %collective-permute-start.5 = (bf16[1024,2560]{1,0:T(8,128)(2,1)}, bf16[1024,2560]{1,0:T(8,128)(2,1)}, u32[]{:S(2)}, u32[]{:S(2)}) collective-permute-start(bf16[1024,2560]{1,0:T(8,128)(2,1)} %fusion.20), channel_id=1, source_target_pairs={{0,1},{1,0},{2,3},{3,2},{4,5},{5,4},{6,7},{7,6},{8,9},{9,8},{10,11... | collective-permute-start | bytes 15728648 | tf_op jit(solution)/shard_map/ppermute | solution.py:146
  1559.2 60.3 %collective-permute-start.19 = (f32[2,160]{1,0:T(2,128)S(1)}, f32[2,160]{1,0:T(2,128)S(1)}, u32[]{:S(2)}, u32[]{:S(2)}) collective-permute-start(f32[2,160]{1,0:T(2,128)S(1)} %pad_maximum_fusion.8), channel_id=1, source_target_pairs={{0,1},{1,0},{2,3},{3,2},{4,5},{5,4},{6,7},{7,6},{8,9},{9,8},{10,11... | collective-permute-start | bytes 3848 | tf_op jit(solution)/shard_map/ppermute | solution.py:146
  (48 other events, 1750.2 us)
Sparse Core Ops, SparseCore 0:
  10.9 86.5 all-gather.5
  99.8 89.2 all-gather.7
  190.7 121.2 all-gather.13
  313.4 111.5 all-gather.11
  426.4 108.1 all-gather.9
  1059.0 57.2 reduce-scatter.7
  1121.6 67.9 reduce-scatter.5
  1232.1 109.3 reduce-scatter.9
  1378.4 109.3 reduce-scatter.11
  1507.2 109.3 reduce-scatter.13

commit v2 on v1

v2 whole, which is shorter than its diff:
```python
import functools

import jax
import jax.numpy as jnp
from jax import lax
from jax.experimental import pallas as pl
from jax.experimental.pallas import tpu as pltpu
from jax.sharding import PartitionSpec as P

HD = 256
W = 2048
EPS = 1e-06
FAR = -1e30
LOW = jnp.bfloat16
WIDE = jnp.float32
CONTRACT_ROWS = (((0,), (0,)), ((), ()))
CONTRACT_LAST = (((1,), (1,)), ((), ()))
VMEM = 60 * 1024 * 1024


def matmul(left, right):
    return jnp.dot(left, right, preferred_element_type=WIDE)


def rows_product(left, right):
    return lax.dot_general(left, right, CONTRACT_ROWS, preferred_element_type=WIDE)


def right_transposed(left, right):
    return lax.dot_general(left, right, CONTRACT_LAST, preferred_element_type=WIDE)


def gelu_parts(gate):
    c = 0.7978845608028654
    inner = c * (gate + 0.044715 * gate * gate * gate)
    t = jnp.tanh(inner)
    value = 0.5 * gate * (1.0 + t)
    slope = 0.5 * (1.0 + t) + 0.5 * gate * (1.0 - t * t) * c * (1.0 + 3 * 0.044715 * gate * gate)
    return value, slope


def attend_kernel(place_ref, q_ref, win_ref, out_ref, probs_ref, bias_ref, *, heads, hops, rows, block):
    span = W + block
    start = pl.program_id(0) * block
    first = (hops - place_ref[0]) * rows - start
    row = lax.broadcasted_iota(jnp.int32, (block, span), 0)
    col = lax.broadcasted_iota(jnp.int32, (block, span), 1)
    live = (col > row) & (col <= row + W) & (col >= first)
    bias_ref[...] = jnp.where(live, 0.0, FAR)
    window = pl.ds(pl.multiple_of(start, block), span)
    for h in range(heads):
        cols = slice(h * HD, (h + 1) * HD)
        scores = right_transposed(q_ref[:, cols], win_ref[window, :HD]) + bias_ref[...]
        top = jnp.max(scores, axis=1, keepdims=True)
        weights = jnp.exp(scores - top)
        total = jnp.sum(weights, axis=1, keepdims=True)
        probs_ref[h] = (weights * (1.0 / total)).astype(LOW)
        out_ref[:, cols] = matmul(probs_ref[h], win_ref[window, HD:]).astype(LOW)


def attend(queries, window, place, hops):
    rows, width = queries.shape
    heads = width // HD
    block = min(256, rows)
    span = W + block
    return pl.pallas_call(
        functools.partial(attend_kernel, heads=heads, hops=hops, rows=rows, block=block),
        grid=(rows // block,),
        in_specs=[
            pl.BlockSpec(memory_space=pltpu.SMEM),
            pl.BlockSpec((block, width), lambda i: (i, 0)),
            pl.BlockSpec(window.shape, lambda i: (0, 0)),
        ],
        out_specs=[
            pl.BlockSpec((block, width), lambda i: (i, 0)),
            pl.BlockSpec((heads, block, span), lambda i: (0, i, 0)),
        ],
        out_shape=[
            jax.ShapeDtypeStruct((rows, width), LOW),
            jax.ShapeDtypeStruct((heads, rows, span), LOW),
        ],
        scratch_shapes=[pltpu.VMEM((block, span), WIDE)],
        compiler_params=pltpu.CompilerParams(vmem_limit_bytes=VMEM),
        name="attend",
    )(place, queries, window)


CONTRACT = {"nn": (((1,), (0,)), ((), ())), "nt": CONTRACT_LAST, "tn": CONTRACT_ROWS}


def products_body(kind, n_pairs, n_extras, finish, sub, keep):
    def body(*refs):
        pairs = [(refs[2 * p], refs[2 * p + 1]) for p in range(n_pairs)]
        extras = refs[2 * n_pairs : 2 * n_pairs + n_extras]
        outs = refs[2 * n_pairs + n_extras :]
        bn = pairs[0][1].shape[0 if kind == "nt" else 1]
        step = sub or bn
        for start in range(0, bn, step):
            cols = slice(start, start + step)
            total = None
            for left, right in pairs:
                part = right[cols, :] if kind == "nt" else right[:, cols]
                term = lax.dot_general(left[...], part, CONTRACT[kind], preferred_element_type=WIDE)
                total = term if total is None else total + term
            given = [e[:, cols].astype(WIDE) for e in extras]
            keep(outs, cols, finish(total, *given) if finish else [sum(given, total)])

    return body


def keep_blocks(outs, cols, results):
    for out, result in zip(outs, results, strict=True):
        out[:, cols] = result.astype(out.dtype)


def products_specs(kind, depths, bm, bn, left_block, right_col):
    specs = []
    for depth in depths:
        if kind == "tn":
            specs.append(pl.BlockSpec((depth, bm), lambda i, j: (0, left_block(i))))
        else:
            specs.append(pl.BlockSpec((bm, depth), lambda i, j: (left_block(i), 0)))
        if kind == "nt":
            specs.append(pl.BlockSpec((bn, depth), lambda i, j: (j, right_col)))
        else:
            specs.append(pl.BlockSpec((depth, bn), lambda i, j: (0, right_col + j)))
    return specs


def product(kind, left, right, *, bm, bn, width, col=0, extras=(), finish=None, outs=(LOW,), sub=0):
    depth = left.shape[1]
    by_block = pl.BlockSpec((bm, bn), lambda i, j: (i, j))
    return pl.pallas_call(
        products_body(kind, 1, len(extras), finish, sub, keep_blocks),
        grid=(left.shape[0] // bm, width // bn),
        in_specs=products_specs(kind, [depth], bm, bn, lambda i: i, col) + [by_block] * len(extras),
        out_specs=[by_block] * len(outs),
        out_shape=[jax.ShapeDtypeStruct((left.shape[0], width), each) for each in outs],
        compiler_params=pltpu.CompilerParams(vmem_limit_bytes=VMEM),
        name="product",
    )(left, right, *extras)


def by_rows(body, sliced, whole, outs, block):
    rows = sliced[0].shape[0]
    n_in = len(sliced) + len(whole)
    specs = [pl.BlockSpec((block, a.shape[1]), lambda i: (i, 0)) for a in sliced]
    specs += [pl.BlockSpec(a.shape, lambda i: (0, 0)) for a in whole]
    return pl.pallas_call(
        lambda *refs: body(refs[:n_in], refs[n_in:]),
        grid=(rows // block,),
        in_specs=specs,
        out_specs=[pl.BlockSpec((block, cols), lambda i: (i, 0)) for cols, _ in outs],
        out_shape=[jax.ShapeDtypeStruct((rows, cols), kind) for cols, kind in outs],
        compiler_params=pltpu.CompilerParams(vmem_limit_bytes=VMEM),
        name="by_rows",
    )(*sliced, *whole)


def add_norm(ins, outs):
    tokens, own, other, gain = ins
    middle = tokens[...].astype(WIDE) + (own[...].astype(WIDE) + other[...].astype(WIDE))
    inverse = lax.rsqrt(jnp.mean(middle * middle, axis=1, keepdims=True) + EPS)
    outs[0][...] = middle.astype(LOW)
    outs[1][...] = (middle * inverse * gain[...]).astype(LOW)
    outs[2][...] = jnp.broadcast_to(inverse, outs[2].shape)


def norm_back(values, grad, gain, inverse):
    scaled = grad * gain
    along = jnp.sum(scaled * values, axis=1, keepdims=True) * (1.0 / values.shape[1])
    return inverse * scaled - values * (inverse * inverse * inverse * along)


def middle_back(ins, outs):
    cotangent, middle, inverse, own, other, gain, out_full = ins
    grad = own[...].astype(WIDE) + other[...].astype(WIDE)
    back = norm_back(middle[...].astype(WIDE), grad, gain[...], inverse[:, :1])
    low = (cotangent[...].astype(WIDE) + back).astype(LOW)
    outs[0][...] = low
    outs[1][...] = matmul(low, out_full[...]).astype(LOW)


def source_back(ins, outs):
    tokens, middle_low, own, other, keyval_back, gain, keyval_full = ins
    grad = own[...].astype(WIDE) + other[...].astype(WIDE)
    grad = grad + right_transposed(keyval_back[...], keyval_full[...])
    values = tokens[...].astype(WIDE)
    inverse = lax.rsqrt(jnp.mean(values * values, axis=1, keepdims=True) + EPS)
    back = middle_low[...].astype(WIDE) + norm_back(values, grad, gain[...], inverse)
    outs[0][...] = back.astype(LOW)


def finish_up(upward, gate):
    value, slope = gelu_parts(gate)
    return value * upward, value, slope * upward


def finish_hidden(grad_hidden, to_gate, to_up):
    return grad_hidden * to_gate, grad_hidden * to_up


MESH = pl.DeviceIdType.MESH


class Links:
    def __init__(self, send_sems, recv_sems):
        self.send_sems, self.recv_sems = send_sems, recv_sems
        self.count = 0
        self.open = []
        self.fsdp = lax.axis_index("fsdp")
        self.place = lax.axis_index("ctx")
        self.core = {"fsdp": self.fsdp + 1 - 2 * lax.rem(self.fsdp, 2)}
        self.chip = {"fsdp": lax.rem(self.fsdp + 2, 4)}
        self.tp = {"tp": 1 - lax.axis_index("tp")}

    def block(self, flip):
        return (self.fsdp, self.core["fsdp"], self.chip["fsdp"], 3 - self.fsdp)[flip]

    def along(self, bit):
        return {"ctx": self.place + bit - 2 * bit * lax.rem(lax.div(self.place, bit), 2)}

    def meet(self, partners):
        barrier = pltpu.get_barrier_semaphore()
        for partner in partners:
            pl.semaphore_signal(barrier, inc=1, device_id=partner, device_id_type=MESH)
        pl.semaphore_wait(barrier, len(partners))

    def copy(self, source, target, partner):
        made = pltpu.make_async_remote_copy(
            src_ref=source,
            dst_ref=target,
            send_sem=self.send_sems.at[self.count],
            recv_sem=self.recv_sems.at[self.count],
            device_id=partner,
            device_id_type=MESH,
        )
        self.count += 1
        return made

    def send(self, source, target, partner):
        made = self.copy(source, target, partner)
        made.start()
        self.open.append(made)
        return made

    def close(self):
        for made in self.open:
            made.wait_send()


def job(kind, pairs, outs, *, bm, bn, steps=1, left_block=None, right_col=0, extras=(), finish=None, sub=0):
    depths = [left.shape[0 if kind == "tn" else 1] for left, _ in pairs]
    width = outs[0].shape[1]
    specs = products_specs(kind, depths, bm, bn, left_block or (lambda i: i), right_col)
    specs += [pl.BlockSpec((bm, bn), lambda i, j, at=at: (i + at, j)) for _, at in extras]
    pltpu.emit_pipeline(
        products_body(kind, len(pairs), len(extras), finish, sub, keep_blocks),
        grid=(steps, width // bn),
        in_specs=specs,
        out_specs=[pl.BlockSpec((bm, bn), lambda i, j: (i, j))] * len(outs),
    )(*[ref for pair in pairs for ref in pair], *[ref for ref, _ in extras], *outs)


def rows_job(body, sliced, whole, outs, block):
    n_in = len(sliced) + len(whole)
    specs = [pl.BlockSpec((block, a.shape[1]), lambda i: (i, 0)) for a in sliced]
    specs += [pl.BlockSpec(a.shape, lambda i: (0, 0)) for a in whole]
    pltpu.emit_pipeline(
        lambda *refs: body(refs[:n_in], refs[n_in:]),
        grid=(sliced[0].shape[0] // block,),
        in_specs=specs,
        out_specs=[pl.BlockSpec((block, a.shape[1]), lambda i: (i, 0)) for a in outs],
    )(*sliced, *whole, *outs)


def bits_of(count):
    bits = []
    while 1 << len(bits) < count:
        bits.append(1 << len(bits))
    return bits


def piece_order(count):
    order = [0]
    for bit in reversed(bits_of(count)):
        order = order + [r + bit for r in order]
    return order


class Scatter:
    @staticmethod
    def shapes(prefix, features, width, count):
        part = features // 4
        size = part // count
        out = {"away": (2 * part, width), "got": (2 * part, width), "far": (part, width), "arrived": (part, width)}
        left = count
        out["near"] = (left, size, width)
        for k in range(len(bits_of(count))):
            left //= 2
            out[f"recv{k}"] = (left, size, width)
            if left > 1:
                out[f"mid{k}"] = (left, size, width)
        return {prefix + key: jax.ShapeDtypeStruct(shape, LOW) for key, shape in out.items()}

    def __init__(self, prefix, refs, links, left, right, bn, count, total=None):
        self.refs, self.prefix, self.links, self.bn, self.total = refs, prefix, links, bn, total
        self.pairs = [(refs[left], refs[right])]
        self.part = refs[left].shape[1] // 4
        self.bits = bits_of(count)
        self.moving = {}

    def ref(self, key):
        return self.refs[self.prefix + key]

    def wait(self, key):
        if key in self.moving:
            self.moving.pop(key).wait_recv()

    def away(self):
        core, both = self.links.block(1), self.links.block(3)
        job(
            "tn",
            self.pairs,
            [self.ref("away")],
            bm=self.part,
            bn=self.bn,
            steps=2,
            left_block=lambda i: both + i * (core - both),
        )
        self.moving["got"] = self.links.send(self.ref("away"), self.ref("got"), self.links.core)

    def far(self):
        self.wait("got")
        chip = self.links.block(2)
        job(
            "tn",
            self.pairs,
            [self.ref("far")],
            bm=self.part,
            bn=self.bn,
            left_block=lambda i: chip,
            extras=[(self.ref("got"), 0)],
        )

    def cross(self):
        self.moving["arrived"] = self.links.send(self.ref("far"), self.ref("arrived"), self.links.chip)

    def near(self):
        self.wait("arrived")
        own, place = self.links.block(0), self.links.place
        near, total = self.ref("near"), self.total
        count, size = near.shape[0], near.shape[1]
        order = piece_order(count)

        def keep(outs, cols, results):
            total[:, cols] = results[0]
            for k in range(count):
                at = 0
                for bit in self.bits:
                    mine = lax.rem(lax.div(place, bit), 2)
                    at = at + bit * (1 - mine if order[k] & bit else mine)
                rows = pl.ds(pl.multiple_of(at * size, size), size)
                outs[0][k, :, cols] = total[rows, cols].astype(LOW)

        bm, bn = self.part, self.bn
        left, right = self.pairs[0]
        pltpu.emit_pipeline(
            products_body("tn", 1, 2, None, 0, keep),
            grid=(1, right.shape[1] // bn),
            in_specs=products_specs("tn", [left.shape[0]], bm, bn, lambda i: own, 0)
            + [pl.BlockSpec((bm, bn), lambda i, j: (1, j)), pl.BlockSpec((bm, bn), lambda i, j: (0, j))],
            out_specs=[pl.BlockSpec((count, size, bn), lambda i, j: (0, 0, j))],
        )(left, right, self.ref("got"), self.ref("arrived"), near)

    def kept(self, k):
        return self.ref(f"mid{k - 1}" if k else "near")

    def halve(self, k):
        now = self.kept(k)
        half = now.shape[0] // 2
        self.moving[f"recv{k}"] = self.links.send(
            now.at[pl.ds(half, half)], self.ref(f"recv{k}"), self.links.along(self.bits[k])
        )

    def add(self, k):
        self.wait(f"recv{k}")
        if k + 1 == len(self.bits):
            return
        now, mid = self.kept(k), self.ref(f"mid{k}")
        half, size, bn = mid.shape[0], mid.shape[1], self.bn

        def body(own, other, out):
            out[...] = (own[...].astype(WIDE) + other[...].astype(WIDE)).astype(LOW)

        block = pl.BlockSpec((half, size, bn), lambda j: (0, 0, j))
        pltpu.emit_pipeline(body, grid=(mid.shape[2] // bn,), in_specs=[block, block], out_specs=[block])(
            now, self.ref(f"recv{k}"), mid
        )

    def rest(self, k):
        self.add(k)
        for later in range(k + 1, len(self.bits)):
            self.halve(later)
            self.add(later)


def scatter_result(prefix, arrays):
    last = len(bits_of(arrays[prefix + "near"].shape[0])) - 1
    now = arrays[prefix + (f"mid{last - 1}" if last else "near")]
    return now[0].astype(WIDE) + arrays[prefix + f"recv{last}"][0].astype(WIDE)


def remote_call(kernel, inputs, outputs, scratch, collective_id, name):
    anywhere = pl.BlockSpec(memory_space=pl.ANY)
    sems = pltpu.SemaphoreType.DMA((32,))
    return pl.pallas_call(
        kernel,
        in_specs=[anywhere] * len(inputs),
        out_specs=[anywhere] * len(outputs),
        out_shape=outputs,
        scratch_shapes=scratch + [sems, sems],
        compiler_params=pltpu.CompilerParams(
            collective_id=collective_id, has_side_effects=True, vmem_limit_bytes=VMEM
        ),
        name=name,
    )


def by_name(body, reads, writes, n_scratch):
    names = reads + writes

    def kernel(*refs):
        rest = refs[len(names) :]
        body(dict(zip(names, refs)), Links(rest[-2], rest[-1]), *rest[:n_scratch])

    return kernel


def down_start(r, links, *, count):
    links.meet([links.core])
    down = Scatter("d_", r, links, "cotangent", "hidden", r["hidden"].shape[1] // 3, count)
    down.away()
    down.far()
    links.close()


def attend_back(refs, rows, heads, block):
    span = W + block
    steps = rows // block
    queries, backs, outs, probs = (refs[k] for k in ("queries", "grad_attended", "attended", "probs"))

    def scoped(win, dwin, q, back, out, dq, p, ds, sems):
        loads = [
            pltpu.make_async_copy(a, b, sems.at[k])
            for k, (a, b) in enumerate([(refs["window"], win), (queries, q), (backs, back), (outs, out)])
        ]

        def fetch(i):
            slot = lax.rem(i, 2)
            at = pl.ds(pl.multiple_of(i * block, block), block)
            return pltpu.make_async_copy(probs.at[:, at, :], p.at[slot], sems.at[4 + slot])

        fetch(0).start()
        for load in loads:
            load.start()
        dwin[...] = jnp.zeros_like(dwin)
        for load in loads:
            load.wait()

        def step(i, carry):
            @pl.when(i + 1 < steps)
            def _():
                fetch(i + 1).start()

            fetch(i).wait()
            slot = lax.rem(i, 2)
            at = pl.ds(pl.multiple_of(i * block, block), block)
            window = pl.ds(pl.multiple_of(i * block, block), span)
            for h in range(heads):
                cols = slice(h * HD, (h + 1) * HD)
                g = back[at, cols]
                along = jnp.sum(g.astype(WIDE) * out[at, cols].astype(WIDE), axis=1, keepdims=True)
                grad_probs = right_transposed(g, win[window, HD:])
                ds[h] = (p[slot, h].astype(WIDE) * (grad_probs - along)).astype(LOW)
                part = matmul(ds[h], win[window, :HD]).astype(LOW)
                dq[at, cols] = (part.astype(WIDE) * HD ** (-0.5)).astype(LOW)
            q_all = jnp.concatenate([q[at, h * HD : (h + 1) * HD] for h in range(heads)], axis=0)
            g_all = jnp.concatenate([back[at, h * HD : (h + 1) * HD] for h in range(heads)], axis=0)
            dwin[window, :HD] += rows_product(ds[...].reshape(heads * block, span), q_all)
            dwin[window, HD:] += rows_product(p[slot].reshape(heads * block, span), g_all)
            return carry

        lax.fori_loop(0, steps, step, 0)
        win[...] = dwin[...].astype(LOW)
        stores = [
            pltpu.make_async_copy(win, refs["window_back"], sems.at[0]),
            pltpu.make_async_copy(dq, refs["query_back"], sems.at[1]),
        ]
        for store in stores:
            store.start()
        for store in stores:
            store.wait()

    width = heads * HD
    length = refs["window"].shape[0]
    pl.run_scoped(
        scoped,
        pltpu.VMEM((length, 2 * HD), LOW),
        pltpu.VMEM((length, 2 * HD), WIDE),
        pltpu.VMEM((rows, width), LOW),
        pltpu.VMEM((rows, width), LOW),
        pltpu.VMEM((rows, width), LOW),
        pltpu.VMEM((rows, width), LOW),
        pltpu.VMEM((2, heads, block, span), LOW),
        pltpu.VMEM((heads, block, span), LOW),
        pltpu.SemaphoreType.DMA((6,)),
    )


def window_sum(place, count, hops):
    def body(ins, outs):
        total = ins[0][...].astype(WIDE)
        for by in range(1, hops + 1):
            total = total + jnp.where(place + by < count, ins[by][...].astype(WIDE), 0.0)
        outs[0][...] = total.astype(LOW)

    return body


def pair_sum(ins, outs):
    outs[0][...] = (ins[0][...].astype(WIDE) + ins[1][...].astype(WIDE)).astype(LOW)


def feed_back(r, links, total, *, rows, heads, count):
    half, block = rows // 2, min(256, rows)
    features = r["cotangent"].shape[1]
    width = heads * HD
    third = r["hidden"].shape[1] // 3
    bits = bits_of(count)
    links.meet([links.core, links.chip, links.tp] + [links.along(bit) for bit in bits])
    down = Scatter("d_", r, links, "cotangent", "hidden", third, count, total)
    gate = Scatter("g_", r, links, "second_low", "gate_back", third, count, total)
    up = Scatter("u_", r, links, "second_low", "up_back", third, count, total)
    out = Scatter("o_", r, links, "middle_low", "attended", width, count, total)
    top, bottom = pl.ds(0, half), pl.ds(half, half)

    down.cross()
    job(
        "nn",
        [(r["cotangent"], r["down_full"])],
        [r["gate_back"], r["up_back"]],
        bm=rows,
        bn=third * 3 // 5,
        sub=third // 5,
        extras=[(r["to_gate"], 0), (r["to_up"], 0)],
        finish=finish_hidden,
    )

    def second(part):
        job(
            "nt",
            [(r["gate_back"].at[part], r["gate_full"]), (r["up_back"].at[part], r["up_full"])],
            [r["second"].at[part]],
            bm=half,
            bn=256,
        )
        return links.send(r["second"].at[part], r["second_other"].at[part], links.tp)

    first = second(top)
    last = second(bottom)
    gate.away()
    down.near()
    down.halve(0)
    gate.far()
    gate.cross()
    up.away()
    job("nt", [(r["hidden"].at[top], r["down_full"])], [r["feed0"]], bm=half, bn=512)
    job("nt", [(r["hidden"].at[bottom], r["down_full"])], [r["feed1"]], bm=half, bn=512)
    up.far()
    first.wait_recv()
    last.wait_recv()
    feed = links.send(r["feed0"], r["feed_other0"], links.tp)
    rows_job(
        middle_back,
        [r["cotangent"], r["middle"], r["second_inverse"], r["second"], r["second_other"]],
        [r["gain_two"], r["small_full"].at[:, pl.ds(width, width)]],
        [r["middle_low"], r["grad_attended"]],
        block,
    )
    out.away()
    down.add(0)
    out.far()
    gate.wait("arrived")
    feed.wait_recv()
    links.close()


def scores_back(r, links, total, *, rows, heads, hops, count):
    half, block = rows // 2, min(256, rows)
    width = heads * HD
    third = r["up_back"].shape[1] // 3
    links.meet([links.core, links.chip, links.tp] + [{"ctx": lax.rem(links.place + k, count)} for k in range(1, count)])
    down = Scatter("d_", r, links, "cotangent", "hidden", third, count, total)
    gate = Scatter("g_", r, links, "second_low", "gate_back", third, count, total)
    up = Scatter("u_", r, links, "second_low", "up_back", third, count, total)
    query = Scatter("q_", r, links, "first_low", "query_back", width, count, total)
    keyval = Scatter("k_", r, links, "first_low", "keyval_back", 2 * HD, count, total)

    up.cross()
    feed = links.send(r["feed1"], r["feed_other1"], links.tp)
    down.halve(1)
    attend_back(r, rows, heads, block)
    windows = []
    for by in range(1, hops + 1):
        move = links.copy(
            r["window_back"].at[pl.ds((hops - by) * rows, rows)],
            r["window_other"].at[by - 1],
            {"ctx": lax.rem(links.place + count - by, count)},
        )

        @pl.when(links.place >= by)
        def _(move=move):
            move.start()

        windows.append(move)
    gate.near()
    gate.halve(0)
    job("nt", [(r["query_back"], r["small_full"].at[:, pl.ds(0, width)])], [r["share"]], bm=rows, bn=512)
    feed.wait_recv()
    share = links.send(r["share"].at[pl.ds(0, half)], r["share_other0"], links.tp)
    query.away()
    for by in range(1, hops + 1):

        @pl.when(links.place + by < count)
        def _(move=windows[by - 1]):
            move.wait_recv()

    rows_job(
        window_sum(links.place, count, hops),
        [r["window_back"].at[pl.ds(hops * rows, rows)]] + [r["window_other"].at[by] for by in range(hops)],
        [],
        [r["keyval_own"]],
        block,
    )
    swap = links.send(r["keyval_own"], r["keyval_other"], links.tp)
    query.far()
    gate.add(0)
    swap.wait_recv()
    rows_job(pair_sum, [r["keyval_own"], r["keyval_other"]], [], [r["keyval_back"]], block)
    keyval.away()
    down.rest(1)
    keyval.far()
    up.wait("arrived")
    share.wait_recv()
    for by in range(1, hops + 1):

        @pl.when(links.place >= by)
        def _(move=windows[by - 1]):
            move.wait_send()

    links.close()


def last_sums(r, links, total, *, rows, heads, count):
    half = rows // 2
    width = heads * HD
    third = r["up_back"].shape[1] // 3
    bits = bits_of(count)
    links.meet([links.chip, links.tp] + [links.along(bit) for bit in bits])
    gate = Scatter("g_", r, links, "second_low", "gate_back", third, count, total)
    up = Scatter("u_", r, links, "second_low", "up_back", third, count, total)
    out = Scatter("o_", r, links, "middle_low", "attended", width, count, total)
    query = Scatter("q_", r, links, "first_low", "query_back", width, count, total)
    keyval = Scatter("k_", r, links, "first_low", "keyval_back", 2 * HD, count, total)
    share = links.send(r["share"].at[pl.ds(half, half)], r["share_other1"], links.tp)
    out.cross()
    gate.halve(1)
    up.near()
    up.halve(0)
    out.near()
    out.halve(0)
    query.cross()
    keyval.cross()
    up.add(0)
    up.halve(1)
    query.near()
    query.halve(0)
    out.add(0)
    out.halve(1)
    keyval.near()
    keyval.halve(0)
    query.add(0)
    query.halve(1)
    keyval.add(0)
    keyval.halve(1)
    for each in (gate, up, out, query, keyval):
        each.rest(1)
    share.wait_recv()
    links.close()


def from_place(array, by):
    count = lax.axis_size("ctx")
    return lax.ppermute(array, "ctx", [(i, i + by) for i in range(count) if i + by < count])


def swap_tp(array):
    return lax.ppermute(array, "tp", [(0, 1), (1, 0)])


def gathered(shard):
    return lax.all_gather(shard, ("fsdp", "ctx"), axis=0, tiled=True)


def on_device(
    tokens,
    query_weight,
    keyval_weight,
    out_weight,
    gate_weight,
    up_weight,
    down_weight,
    first_gain,
    second_gain,
    cotangent,
):
    rows, features = tokens.shape
    width = query_weight.shape[1]
    units = gate_weight.shape[1]
    heads = width // HD
    scale = HD ** (-0.5)
    count = lax.axis_size("ctx")
    hops = min(-(-W // rows), count - 1)
    place = lax.axis_index("ctx")
    block = min(256, rows)

    gains = jnp.pad(jnp.stack([first_gain, second_gain], axis=1), ((0, 0), (0, 126)))
    small_full = gathered(jnp.concatenate([query_weight, out_weight, keyval_weight, gains], axis=1))
    gate_full = gathered(gate_weight)
    up_full = gathered(up_weight)
    down_full = gathered(down_weight)
    query_full = small_full[:, :width]
    keyval_full = small_full[:, 2 * width : 2 * width + 2 * HD]
    both_gains = 1.0 + small_full[:, 2 * width + 2 * HD :][:, :2].astype(WIDE).T
    gain_one, gain_two = both_gains[:1], both_gains[1:]

    source = tokens.astype(WIDE)
    first_inverse = lax.rsqrt(jnp.mean(source * source, axis=-1, keepdims=True) + EPS)
    first_low = (source * first_inverse * gain_one).astype(LOW)
    keyval = matmul(first_low, keyval_full).astype(LOW)
    before = [from_place(keyval, by) for by in range(hops, 0, -1)]
    queries = (matmul(first_low, query_full) * scale).astype(LOW)
    window = jnp.concatenate(before + [keyval], axis=0)
    attended, probs = attend(queries, window, place.reshape(1), hops)
    (branch,) = product("nt", attended, small_full, bm=rows, bn=512, width=features, col=1)
    middle, second_low, second_inverse = by_rows(
        add_norm,
        [tokens, branch, swap_tp(branch)],
        [gain_two],
        [(features, LOW), (features, LOW), (128, WIDE)],
        block,
    )
    (gate,) = product("nn", second_low, gate_full, bm=rows, bn=768, width=units, outs=(WIDE,))
    hidden, to_up, to_gate = product(
        "nn",
        second_low,
        up_full,
        bm=rows,
        bn=768,
        width=units,
        sub=256,
        extras=[gate],
        finish=finish_up,
        outs=(LOW, LOW, LOW),
    )

    plain = {
        "gate_back": (rows, units),
        "up_back": (rows, units),
        "second": (rows, features),
        "second_other": (rows, features),
        "feed0": (rows // 2, features),
        "feed1": (rows // 2, features),
        "feed_other0": (rows // 2, features),
        "feed_other1": (rows // 2, features),
        "middle_low": (rows, features),
        "grad_attended": (rows, width),
        "query_back": (rows, width),
        "window_back": window.shape,
        "window_other": (hops, rows, 2 * HD),
        "keyval_own": (rows, 2 * HD),
        "keyval_other": (rows, 2 * HD),
        "keyval_back": (rows, 2 * HD),
        "share": (rows, features),
        "share_other0": (rows // 2, features),
        "share_other1": (rows // 2, features),
    }
    shapes = {key: jax.ShapeDtypeStruct(shape, LOW) for key, shape in plain.items()}
    for prefix, each in (("d_", units), ("g_", units), ("u_", units), ("o_", width), ("q_", width), ("k_", 2 * HD)):
        shapes |= Scatter.shapes(prefix, features, each, count)
    done = dict(
        cotangent=cotangent,
        down_full=down_full,
        gate_full=gate_full,
        up_full=up_full,
        small_full=small_full,
        to_gate=to_gate,
        to_up=to_up,
        hidden=hidden,
        first_low=first_low,
        second_low=second_low,
        middle=middle,
        second_inverse=second_inverse,
        gain_two=gain_two,
        queries=queries,
        window=window,
        attended=attended,
        probs=probs,
    )
    total = pltpu.VMEM((features // 4, max(width, units // 3)), WIDE)
    sizes = dict(rows=rows, heads=heads, count=count)
    late = len(bits_of(count)) - 1

    def stage(prefix, *keys):
        return [prefix + key for key in keys]

    def halving(prefix, first, end):
        keys = []
        for k in range(first, end):
            keys += [f"{prefix}recv{k}"] + ([f"{prefix}mid{k}"] if k < late else [])
        return keys

    reads, writes = ["cotangent", "hidden"], stage("d_", "away", "got", "far")
    call = remote_call(
        by_name(functools.partial(down_start, count=count), reads, writes, 0),
        reads,
        [shapes[key] for key in writes],
        [],
        0,
        "down_start",
    )
    done |= zip(writes, call(*[done[key] for key in reads]))

    reads = stage("d_", "got", "far") + ["cotangent", "hidden", "down_full", "gate_full", "up_full", "small_full"]
    reads += ["to_gate", "to_up", "second_low", "middle", "second_inverse", "gain_two", "attended"]
    writes = ["gate_back", "up_back", "second", "second_other", "feed0", "feed1", "feed_other0", "middle_low"]
    writes += ["grad_attended"] + stage("d_", "arrived", "near") + halving("d_", 0, 1)
    writes += stage("g_", "away", "got", "far", "arrived") + stage("u_", "away", "got", "far")
    writes += stage("o_", "away", "got", "far")
    call = remote_call(
        by_name(functools.partial(feed_back, **sizes), reads, writes, 1),
        reads,
        [shapes[key] for key in writes],
        [total],
        1,
        "feed_back",
    )
    done |= zip(writes, call(*[done[key] for key in reads]))

    reads = ["cotangent", "hidden", "gate_back", "up_back", "second_low", "first_low", "small_full", "feed1"]
    reads += ["queries", "window", "attended", "probs", "grad_attended", "u_far", "g_got", "g_arrived"]
    reads += ["d_near"] + halving("d_", 0, 1)
    writes = ["feed_other1", "u_arrived", "query_back", "window_back", "window_other", "keyval_own", "keyval_other"]
    writes += ["keyval_back", "share", "share_other0", "g_near"] + halving("g_", 0, 1) + halving("d_", 1, late + 1)
    writes += stage("q_", "away", "got", "far") + stage("k_", "away", "got", "far")
    call = remote_call(
        by_name(functools.partial(scores_back, hops=hops, **sizes), reads, writes, 1),
        reads,
        [shapes[key] for key in writes],
        [total],
        2,
        "scores_back",
    )
    done |= zip(writes, call(*[done[key] for key in reads]))

    reads = ["gate_back", "up_back", "second_low", "first_low", "middle_low", "attended", "query_back", "keyval_back"]
    reads += ["share", "u_got", "u_arrived", "g_near"] + halving("g_", 0, 1)
    reads += [prefix + key for prefix in ("o_", "q_", "k_") for key in ("got", "far")]
    writes = ["share_other1", "u_near"] + [prefix + key for prefix in ("o_", "q_", "k_") for key in ("arrived", "near")]
    writes += halving("g_", 1, late + 1)
    for prefix in ("u_", "o_", "q_", "k_"):
        writes += halving(prefix, 0, late + 1)
    call = remote_call(
        by_name(functools.partial(last_sums, **sizes), reads, writes, 1),
        reads,
        [shapes[key] for key in writes],
        [total],
        3,
        "last_sums",
    )
    done |= zip(writes, call(*[done[key] for key in reads]))
    share_other = jnp.concatenate([done["share_other0"], done["share_other1"]])
    feed = jnp.concatenate([done["feed0"], done["feed1"]]).astype(WIDE)
    feed_other = jnp.concatenate([done["feed_other0"], done["feed_other1"]]).astype(WIDE)
    (input_grad,) = by_rows(
        source_back,
        [tokens, done["middle_low"], done["share"], share_other, done["keyval_back"]],
        [gain_one, keyval_full],
        [(features, LOW)],
        block,
    )
    output = (middle.astype(WIDE) + (feed + feed_other)).astype(LOW)
    down_grad, gate_grad, up_grad, out_grad, query_grad, keyval_grad = (
        scatter_result(prefix, done) for prefix in ("d_", "g_", "u_", "o_", "q_", "k_")
    )

    def row_sum(weight, grad):
        return jnp.sum(weight.astype(WIDE) * grad, axis=1)

    sums = jnp.stack(
        [
            row_sum(query_weight, query_grad),
            row_sum(gate_weight, gate_grad) + row_sum(up_weight, up_grad),
        ]
    )
    sums = sums + swap_tp(sums)
    first_grad = (sums[0] + row_sum(keyval_weight, keyval_grad)) / (1.0 + first_gain.astype(WIDE))
    second_grad = sums[1] / (1.0 + second_gain.astype(WIDE))
    return (
        output,
        input_grad,
        query_grad,
        keyval_grad,
        out_grad,
        gate_grad,
        up_grad,
        down_grad,
        first_grad,
        second_grad,
    )


def solution(mesh):
    rows = P(("fsdp", "ctx"), None)
    split = P(("fsdp", "ctx"), "tp")
    vector = P(("fsdp", "ctx"))
    return jax.shard_map(
        on_device,
        mesh=mesh,
        in_specs=(rows, split, rows, split, split, split, split, vector, vector, rows),
        out_specs=(rows, rows, split, rows, split, split, split, split, vector, vector),
        check_vma=False,
    )
```

time: 1630 us -> 1240 us (0.76)
  Pallas kernels: 61.9 us -> 819 us
  waiting for transfers between devices: 1010 us -> 327 us
  matrix products: 373 us -> 11 us
  other arithmetic: 131 us -> 38 us
  starting transfers between devices: 26.4 us -> 9.49 us
    pallas_call x1 -> x9, Pallas kernels: 33.5 us -> 791 us  [the longest x4 690 us: on_device(): done |= zip(writes, call(*[done[key] for key in reads]))]
    ppermute x20 -> x4, waiting for transfers between devices: 757 us -> 164 us  [the longest x2 106 us: swap_tp(): return lax.ppermute(array, 'tp', [(0, 1), (1, 0)])]
    dot_general x21 -> x0, matrix products: 252 us -> none  [the longest x15 146 us: rows_product(): lax.dot_general(left, right, CONTRACT_ROWS, preferred_element_type=WIDE)]
    dot_general x6 -> x2, matrix products: 121 us -> 11 us  [matmul(): return jnp.dot(left, right, preferred_element_type=WIDE)]
    convert_element_type x12 -> x1, other arithmetic: 91.8 us -> 8.25 us  [on_device(): output = (middle.astype(WIDE) + (feed + feed_other)).astype(LOW)]
    reduce_scatter x5 -> x0, waiting for transfers between devices: 54.9 us -> none  [scattered_product(): lax.psum_scatter(near.astype(LOW), 'ctx', scatter_dimension=0, tiled=True)]
    all_gather x5 -> x4, waiting for transfers between devices: 195 us -> 161 us  [gathered(): return lax.all_gather(shard, ('fsdp', 'ctx'), axis=0, tiled=True)]
  transfers between devices with their start and end apart: 30 -> 8, of which waited for: 18 -> 6; matrix products, arithmetic and copies ran while one was open for 25% -> 4% of each run, Pallas kernels for 4% -> 14%
where the time goes in v2:
time: 1240 us; the launch traced here: 1230 us
  Pallas kernels  819 us (66%)
  waiting for transfers between devices  327 us (26%)
  other arithmetic  38 us (3%)
  between operations  14.2 us (1%)
  local copies, waits for them, and re-layouts  12.8 us (1%)
    pallas_call x4, Pallas kernels, on_device(): done |= zip(writes, call(*[done[key] for key in reads]))  690 us
    all_gather x4, waiting for transfers between devices, gathered(): return lax.all_gather(shard, ('fsdp', 'ctx'), axis=0, tiled=True)  161 us
    ppermute x2, waiting for transfers between devices, swap_tp(): return lax.ppermute(array, 'tp', [(0, 1), (1, 0)])  106 us
    pallas_call x3, Pallas kernels, product(): pl.pallas_call(products_body(kind, 1, len(extras), finish, sub, keep_bloc...  74.8 us
    ppermute x2, waiting for transfers between devices, from_place(): lax.ppermute(array, 'ctx', [(i, i + by) for i in range(count) if i + by <...  57.5 us
    pallas_call x1, Pallas kernels, attend(): pl.pallas_call(functools.partial(attend_kernel, heads=heads, hops=hops, r...  28.6 us
    pallas_call x2, Pallas kernels, by_rows(): pl.pallas_call(lambda *refs: body(refs[:n_in], refs[n_in:]), grid=(rows /...  25.6 us
  transfers between devices with their start and end apart: 8, of which 6 were waited for; matrix products, arithmetic and copies ran while one was open for 4% of the time, Pallas kernels for 14%

profile of v2, /device:TPU:0, one launch (start us, length us, event | category | flops | bytes accessed | tf_op | source)
XLA Modules:
  0.0 1231.9 jit_solution(9887183622173902614)
XLA Ops:
  8.7 2.3 fusion.8
  13.0 3.6 fusion
  16.6 121.5 %all-gather.5.cloned.1.call-done.refs_1_.refs_7_.refs_6_ = bf16[2560,3200]{1,0:T(8,128)(2,1)} async-done(((bf16[160,3200]{1,0:T(8,128)(2,1)}), bf16[2560,3200]{1,0:T(8,128)(2,1)}) %all-gather.5.cloned.1.call-update) | async-done | bytes 16384016 | tf_op jit(solution)/shard_map/all_gather | solution.py:713
  139.5 1.7 fusion.11
  141.2 4.5 fusion.2.refs_5_.refs_3_
  146.5 2.9 convolution_convert_fusion
  149.3 3.3 collective-permute-start
  152.6 2.4 collective-permute-start.1
  155.0 8.2 multiply_convert_fusion.q_ref.refs_8_
  163.2 24.1 %collective-permute-done = bf16[1024,512]{1,0:T(8,128)(2,1)S(1)} collective-permute-done((bf16[1024,512]{1,0:T(8,128)(2,1)S(1)}, bf16[1024,512]{1,0:T(8,128)(2,1)S(1)}, u32[]{:S(2)}, u32[]{:S(2)}) %collective-permute-start) | collective-permute-done | bytes 1048608 | tf_op jit(solution)/shard_map/ppermute | solution.py:705
  187.3 33.4 %collective-permute-done.1 = bf16[1024,512]{1,0:T(8,128)(2,1)S(1)} collective-permute-done((bf16[1024,512]{1,0:T(8,128)(2,1)S(1)}, bf16[1024,512]{1,0:T(8,128)(2,1)S(1)}, u32[]{:S(2)}, u32[]{:S(2)}) %collective-permute-start.1) | collective-permute-done | bytes 1048608 | tf_op jit(solution)/shard_map/ppermute | solution.py:705
  220.7 1.7 pad_maximum_fusion.1.win_ref.refs_9_
  222.4 28.6 %attend.1 = (bf16[1024,1280]{1,0:T(8,128)(2,1)}, bf16[5,1024,2304]{2,1,0:T(8,128)(2,1)}) custom-call(s32[1]{0:T(128)} %bitcast.place_ref, bf16[1024,1280]{1,0:T(8,128)(2,1)} %multiply_convert_fusion.q_ref.refs_8_, bf16[3072,512]{1,0:T(8,128)(2,1)} %pad_maximum_fusion.1.win_ref.refs_9_), custom_call_target="tpu_custom_call" | custom-call | tf_op jit(solution)/shard_map/attend/pallas_call | solution.py:66
  251.0 11.2 product.3.refs_1_
  263.7 2.4 copy.29.refs_3_.refs_13_
  267.1 3.4 slice.57.refs_6_
  270.5 106.4 %collective-permute-done.2.refs_2_ = bf16[1024,2560]{1,0:T(8,128)(2,1)} collective-permute-done((bf16[1024,2560]{1,0:T(8,128)(2,1)}, bf16[1024,2560]{1,0:T(8,128)(2,1)}, u32[]{:S(2)}, u32[]{:S(2)}) %collective-permute-start.2) | collective-permute-done | bytes 5242912 | tf_op jit(solution)/shard_map/ppermute | solution.py:709
  377.0 11.9 by_rows.2
  388.9 27.0 %product.4.refs_2_ = f32[1024,3840]{1,0:T(8,128)} custom-call(bf16[1024,2560]{1,0:T(8,128)(2,1)} %get-tuple-element.62.refs_0_.refs_10_.refs_4_.refs_2_, bf16[2560,3840]{1,0:T(8,128)(2,1)} %all-gather.9.cloned.1.call-done.refs_1_.refs_5_), custom_call_target="tpu_custom_call" | custom-call | tf_op jit(solution)/shard_map/product/pallas_call | solution.py:133
  415.9 6.3 all-gather.7.cloned.1.call-done.refs_1_.refs_6_
  422.3 36.5 %product.5 = (bf16[1024,3840]{1,0:T(8,128)(2,1)}, bf16[1024,3840]{1,0:T(8,128)(2,1)}, bf16[1024,3840]{1,0:T(8,128)(2,1)}) custom-call(bf16[1024,2560]{1,0:T(8,128)(2,1)} %get-tuple-element.62.refs_0_.refs_10_.refs_4_.refs_2_, bf16[2560,3840]{1,0:T(8,128)(2,1)} %all-gather.7.cloned.1.call-done.refs_1_.refs_6_, f32[1024,3840]{1,0:T(8,128)} %product.4.refs_2_), custom_call_target="tpu_custom_call" | custom-call | tf_op jit(solution)/shard_map/product/pallas_call | solution.py:133
  458.8 44.1 %down_start.1 = (bf16[1280,3840]{1,0:T(8,128)(2,1)}, bf16[1280,3840]{1,0:T(8,128)(2,1)}, bf16[640,3840]{1,0:T(8,128)(2,1)}) custom-call(bf16[1024,2560]{1,0:T(8,128)(2,1)} %refs_0_.6, bf16[1024,3840]{1,0:T(8,128)(2,1)} %get-tuple-element.63.refs_1_.refs_3_), custom_call_target="tpu_custom_call" | custom-call | tf_op jit(solution)/shard_map/down_start/pallas_call | solution.py:843
  503.0 33.6 %all-gather.11.cloned.1.call-done.refs_4_ = bf16[2560,3840]{1,0:T(8,128)(2,1)} async-done(((bf16[160,3840]{1,0:T(8,128)(2,1)}), bf16[2560,3840]{1,0:T(8,128)(2,1)}) %all-gather.11.cloned.1.call-update) | async-done | bytes 19660816 | tf_op jit(solution)/shard_map/all_gather | solution.py:713
  536.5 254.5 %feed_back.1 = (bf16[1024,3840]{1,0:T(8,128)(2,1)}, bf16[1024,3840]{1,0:T(8,128)(2,1)}, bf16[1024,2560]{1,0:T(8,128)(2,1)}, bf16[1024,2560]{1,0:T(8,128)(2,1)}, ...) custom-call(bf16[1280,3840]{1,0:T(8,128)(2,1)} %get-tuple-element.64, ...), custom_call_target="tpu_custom_call" | custom-call | tf_op jit(solution)/shard_map/feed_back/pallas_call | solution.py:859
  791.0 176.3 %scores_back.1 = (bf16[512,2560]{1,0:T(8,128)(2,1)}, bf16[640,3840]{1,0:T(8,128)(2,1)}, bf16[1024,1280]{1,0:T(8,128)(2,1)}, bf16[3072,512]{1,0:T(8,128)(2,1)}, b...) custom-call(bf16[1024,2560]{1,0:T(8,128)(2,1)} %refs_0_.6, ...), custom_call_target="tpu_custom_call" | custom-call | tf_op jit(solution)/shard_map/scores_back/pallas_call | solution.py:875
  967.4 215.2 %last_sums.1 = (bf16[512,2560]{1,0:T(8,128)(2,1)}, bf16[4,160,3840]{2,1,0:T(8,128)(2,1)}, bf16[640,1280]{1,0:T(8,128)(2,1)}, bf16[4,160,1280]{2,1,0:T(8,128)(2,1...) custom-call(bf16[1024,3840]{1,0:T(8,128)(2,1)} %get-tuple-element.72, ...), custom_call_target="tpu_custom_call" | custom-call | tf_op jit(solution)/shard_map/last_sums/pallas_call | solution.py:892
  1182.7 5.7 multiply_reduce_fusion
  1189.5 2.2 collective-permute-start.3
  1191.7 1.7 add_bitcast_fusion
  1194.4 4.9 pad_maximum_fusion.refs_3_
  1201.3 8.3 add_convert_fusion
  1210.4 13.7 %by_rows.3 = bf16[1024,2560]{1,0:T(8,128)(2,1)} custom-call(bf16[1024,2560]{1,0:T(8,128)(2,1)} %refs_0_.7, bf16[1024,2560]{1,0:T(8,128)(2,1)} %get-tuple-element.83.refs_4_.refs_1_, bf16[1024,2560]{1,0:T(8,128)(2,1)} %get-tuple-element.84.refs_8_.refs_2_, bf16[1024,2560]{1,0:T(8,128)(2,1)} %pad_maximum_fusion.refs_3_, ...), custom_call_target="tpu_custom_call" | custom-call | tf_op jit(solution)/shard_map/by_rows/pallas_call | solution.py:149
  (74 shorter events, 14.2 us)
Async XLA Ops:
  7.2 131.0 %all-gather.5.cloned.1.call-start = ((), (), s32[]{:S(2)}) async-start(), calls=%async_computation | async-start | bytes 17408000 | tf_op jit(solution)/shard_map/all_gather | solution.py:713
  11.0 377.9 %all-gather.9.cloned.1.call-start = ((), (), s32[]{:S(2)}) async-start(), calls=%async_computation.2 | async-start | bytes 20889600 | tf_op jit(solution)/shard_map/all_gather | solution.py:713
  11.7 410.5 %all-gather.7.cloned.1.call-start = ((), (), s32[]{:S(2)}) async-start(), calls=%async_computation.1 | async-start | bytes 20889600 | tf_op jit(solution)/shard_map/all_gather | solution.py:713
  12.5 524.1 %all-gather.11.cloned.1.call-start = ((), (), s32[]{:S(2)}) async-start(), calls=%async_computation.3 | async-start | bytes 20889600 | tf_op jit(solution)/shard_map/all_gather | solution.py:713
  138.2 8.3 copy-start
  146.5 8.5 copy-start.1
  149.3 38.0 %collective-permute-start = (bf16[1024,512]{1,0:T(8,128)(2,1)S(1)}, bf16[1024,512]{1,0:T(8,128)(2,1)S(1)}, u32[]{:S(2)}, u32[]{:S(2)}) collective-permute-start(bf16[1024,512]{1,0:T(8,128)(2,1)S(1)} %convolution_convert_fusion), channel_id=1, source_target_pairs={{0,4},{2,6},{1,5},{3,7},{8,12},{10,14},{9,13},{11,15},{16,20},{18,... | collective-permute-start | bytes 3145736 | tf_op jit(solution)/shard_map/ppermute | solution.py:705
  152.6 68.1 %collective-permute-start.1 = (bf16[1024,512]{1,0:T(8,128)(2,1)S(1)}, bf16[1024,512]{1,0:T(8,128)(2,1)S(1)}, u32[]{:S(2)}, u32[]{:S(2)}) collective-permute-start(bf16[1024,512]{1,0:T(8,128)(2,1)S(1)} %convolution_convert_fusion), channel_id=1, source_target_pairs={{0,2},{2,4},{4,6},{1,3},{3,5},{5,7},{8,10},{10,12},{12,14},{9,11},... | collective-permute-start | bytes 3145736 | tf_op jit(solution)/shard_map/ppermute | solution.py:705
  262.2 114.7 %collective-permute-start.2 = (bf16[1024,2560]{1,0:T(8,128)(2,1)}, bf16[1024,2560]{1,0:T(8,128)(2,1)}, u32[]{:S(2)}, u32[]{:S(2)}) collective-permute-start(bf16[1024,2560]{1,0:T(8,128)(2,1)} %product.3.refs_1_), channel_id=1, source_target_pairs={{0,1},{1,0},{2,3},{3,2},{4,5},{5,4},{6,7},{7,6},{8,9},{9,8},{10,11... | collective-permute-start | bytes 15728648 | tf_op jit(solution)/shard_map/ppermute | solution.py:709
  967.4 215.2 %copy-start.4 = (bf16[2,160,3840]{2,1,0:T(8,128)(2,1)S(1)}, bf16[2,160,3840]{2,1,0:T(8,128)(2,1)}, u32[]{:S(2)}) copy-start(bf16[2,160,3840]{2,1,0:T(8,128)(2,1)} %get-tuple-element.92.refs_13_) | copy-start | bytes 7372804
  967.4 215.2 %copy-start.5 = (bf16[160,3840]{1,0:T(8,128)(2,1)S(1)}, bf16[160,3840]{1,0:T(8,128)(2,1)}, u32[]{:S(2)}) copy-start(bf16[160,3840]{1,0:T(8,128)(2,1)} %param.14) | copy-start | bytes 3686404
  1182.6 5.8 copy-start.10
  1182.6 5.8 copy-start.13
  1182.6 5.8 copy-start.15
  1182.6 9.1 copy-start.3
  1182.6 9.1 copy-start.11
  1182.7 10.7 copy-start.16
  1188.4 5.0 copy-start.14
  1188.4 5.9 copy-start.9
  1189.5 34.5 %collective-permute-start.3 = (f32[2,160]{1,0:T(2,128)S(1)}, f32[2,160]{1,0:T(2,128)S(1)}, u32[]{:S(2)}, u32[]{:S(2)}) collective-permute-start(f32[2,160]{1,0:T(2,128)S(1)} %pad_maximum_fusion.2), channel_id=1, source_target_pairs={{0,1},{1,0},{2,3},{3,2},{4,5},{5,4},{6,7},{7,6},{8,9},{9,8},{10,11... | collective-permute-start | bytes 3848 | tf_op jit(solution)/shard_map/ppermute | solution.py:709
  1191.7 7.6 copy-start.7
  1191.7 7.6 copy-start.8
  1194.4 4.9 slice-start
  1194.4 4.9 slice-start.1
  1194.4 6.2 copy-start.2
  1194.4 6.9 copy-start.6
  1201.3 8.3 copy-start.12
  1201.3 8.3 copy-start.17
  1201.3 8.3 copy-start.18
  1210.4 13.7 %copy-start.19 = (bf16[160]{0:T(256)(128)(2,1)S(1)}, bf16[160]{0:T(256)(128)(2,1)}, u32[]{:S(2)}) copy-start(bf16[160]{0:T(256)(128)(2,1)} %param.18) | copy-start | bytes 964
  1210.4 14.3 %copy-start.20 = (bf16[160]{0:T(256)(128)(2,1)S(1)}, bf16[160]{0:T(256)(128)(2,1)}, u32[]{:S(2)}) copy-start(bf16[160]{0:T(256)(128)(2,1)} %param.17) | copy-start | bytes 964
Sparse Core Ops, SparseCore 0:
  11.1 127.0 all-gather.4
  139.7 162.2 all-gather.8
  303.6 118.6 all-gather.6
  423.7 112.7 all-gather.10

commit v3 on v2

--- a/solution.py
+++ b/solution.py
@@ -182,13 +182,16 @@
 
 
 def source_back(ins, outs):
-    tokens, middle_low, own, other, keyval_back, gain, keyval_full = ins
+    tokens, middle_low, inverse, own, other, keyval_back, gain, keyval_full = ins
     grad = own[...].astype(WIDE) + other[...].astype(WIDE)
     grad = grad + right_transposed(keyval_back[...], keyval_full[...])
-    values = tokens[...].astype(WIDE)
-    inverse = lax.rsqrt(jnp.mean(values * values, axis=1, keepdims=True) + EPS)
-    back = middle_low[...].astype(WIDE) + norm_back(values, grad, gain[...], inverse)
-    outs[0][...] = back.astype(LOW)
+    back = norm_back(tokens[...].astype(WIDE), grad, gain[...], inverse[:, :1])
+    outs[0][...] = (middle_low[...].astype(WIDE) + back).astype(LOW)
+
+
+def add_feed(ins, outs):
+    middle, own, other = ins
+    outs[0][...] = (middle[...].astype(WIDE) + (own[...].astype(WIDE) + other[...].astype(WIDE))).astype(LOW)
 
 
 def finish_up(upward, gate):
@@ -567,20 +570,22 @@
         )
         return links.send(r["second"].at[part], r["second_other"].at[part], links.tp)
 
+    gate.away()
     first = second(top)
+    gate.far()
+    gate.cross()
     last = second(bottom)
-    gate.away()
     down.near()
     down.halve(0)
-    gate.far()
-    gate.cross()
     up.away()
     job("nt", [(r["hidden"].at[top], r["down_full"])], [r["feed0"]], bm=half, bn=512)
-    job("nt", [(r["hidden"].at[bottom], r["down_full"])], [r["feed1"]], bm=half, bn=512)
     up.far()
     first.wait_recv()
     last.wait_recv()
     feed = links.send(r["feed0"], r["feed_other0"], links.tp)
+    down.add(0)
+    if len(bits) > 1:
+        down.halve(1)
     rows_job(
         middle_back,
         [r["cotangent"], r["middle"], r["second_inverse"], r["second"], r["second_other"]],
@@ -589,8 +594,9 @@
         block,
     )
     out.away()
-    down.add(0)
     out.far()
+    if len(bits) > 1:
+        down.rest(1)
     gate.wait("arrived")
     feed.wait_recv()
     links.close()
@@ -601,15 +607,14 @@
     width = heads * HD
     third = r["up_back"].shape[1] // 3
     links.meet([links.core, links.chip, links.tp] + [{"ctx": lax.rem(links.place + k, count)} for k in range(1, count)])
-    down = Scatter("d_", r, links, "cotangent", "hidden", third, count, total)
     gate = Scatter("g_", r, links, "second_low", "gate_back", third, count, total)
     up = Scatter("u_", r, links, "second_low", "up_back", third, count, total)
     query = Scatter("q_", r, links, "first_low", "query_back", width, count, total)
-    keyval = Scatter("k_", r, links, "first_low", "keyval_back", 2 * HD, count, total)
+    top, bottom = pl.ds(0, half), pl.ds(half, half)
 
     up.cross()
+    job("nt", [(r["hidden"].at[bottom], r["down_full"])], [r["feed1"]], bm=half, bn=512)
     feed = links.send(r["feed1"], r["feed_other1"], links.tp)
-    down.halve(1)
     attend_back(r, rows, heads, block)
     windows = []
     for by in range(1, hops + 1):
@@ -624,12 +629,13 @@
             move.start()
 
         windows.append(move)
+    job("nt", [(r["query_back"], r["small_full"].at[:, pl.ds(0, width)])], [r["share"]], bm=rows, bn=512)
+    feed.wait_recv()
+    share = links.send(r["share"].at[top], r["share_other0"], links.tp)
+    query.away()
     gate.near()
     gate.halve(0)
-    job("nt", [(r["query_back"], r["small_full"].at[:, pl.ds(0, width)])], [r["share"]], bm=rows, bn=512)
-    feed.wait_recv()
-    share = links.send(r["share"].at[pl.ds(0, half)], r["share_other0"], links.tp)
-    query.away()
+    query.far()
     for by in range(1, hops + 1):
 
         @pl.when(links.place + by < count)
@@ -643,15 +649,8 @@
         [r["keyval_own"]],
         block,
     )
-    swap = links.send(r["keyval_own"], r["keyval_other"], links.tp)
-    query.far()
-    gate.add(0)
-    swap.wait_recv()
-    rows_job(pair_sum, [r["keyval_own"], r["keyval_other"]], [], [r["keyval_back"]], block)
-    keyval.away()
-    down.rest(1)
-    keyval.far()
     up.wait("arrived")
+    gate.wait("recv0")
     share.wait_recv()
     for by in range(1, hops + 1):
 
@@ -664,39 +663,67 @@
 
 def last_sums(r, links, total, *, rows, heads, count):
     half = rows // 2
+    block = min(256, half)
     width = heads * HD
     third = r["up_back"].shape[1] // 3
     bits = bits_of(count)
-    links.meet([links.chip, links.tp] + [links.along(bit) for bit in bits])
+    links.meet([links.core, links.chip, links.tp] + [links.along(bit) for bit in bits])
     gate = Scatter("g_", r, links, "second_low", "gate_back", third, count, total)
     up = Scatter("u_", r, links, "second_low", "up_back", third, count, total)
     out = Scatter("o_", r, links, "middle_low", "attended", width, count, total)
     query = Scatter("q_", r, links, "first_low", "query_back", width, count, total)
     keyval = Scatter("k_", r, links, "first_low", "keyval_back", 2 * HD, count, total)
-    share = links.send(r["share"].at[pl.ds(half, half)], r["share_other1"], links.tp)
+    parts = (pl.ds(0, half), pl.ds(half, half))
+
+    def finish_source(k):
+        part = parts[k]
+        rows_job(
+            source_back,
+            [r[key].at[part] for key in ("tokens", "middle_low", "first_inverse", "share")]
+            + [r[f"share_other{k}"], r["keyval_back"].at[part]],
+            [r["gain_one"], r["small_full"].at[:, pl.ds(2 * width, 2 * HD)]],
+            [r["input_grad"].at[part]],
+            block,
+        )
+
+    def finish_output(k):
+        part = parts[k]
+        rows_job(add_feed, [r["middle"].at[part], r[f"feed{k}"], r[f"feed_other{k}"]], [], [r["output"].at[part]], block)
+
+    swap = links.send(r["keyval_own"], r["keyval_other"], links.tp)
     out.cross()
+    gate.add(0)
     gate.halve(1)
+    share = links.send(r["share"].at[parts[1]], r["share_other1"], links.tp)
     up.near()
     up.halve(0)
+    query.cross()
+    swap.wait_recv()
+    rows_job(pair_sum, [r["keyval_own"], r["keyval_other"]], [], [r["keyval_back"]], block)
+    keyval.away()
     out.near()
     out.halve(0)
-    query.cross()
+    keyval.far()
     keyval.cross()
+    finish_source(0)
     up.add(0)
     up.halve(1)
     query.near()
     query.halve(0)
+    finish_output(0)
     out.add(0)
     out.halve(1)
     keyval.near()
     keyval.halve(0)
     query.add(0)
     query.halve(1)
+    share.wait_recv()
+    finish_source(1)
     keyval.add(0)
     keyval.halve(1)
+    finish_output(1)
     for each in (gate, up, out, query, keyval):
         each.rest(1)
-    share.wait_recv()
     links.close()
 
 
@@ -749,9 +776,14 @@
     first_inverse = lax.rsqrt(jnp.mean(source * source, axis=-1, keepdims=True) + EPS)
     first_low = (source * first_inverse * gain_one).astype(LOW)
     keyval = matmul(first_low, keyval_full).astype(LOW)
-    before = [from_place(keyval, by) for by in range(hops, 0, -1)]
+    first_tp = lax.axis_index("tp") == 0
+    mine = jnp.where(first_tp, keyval[:, :HD], keyval[:, HD:])
+    before = jnp.concatenate([from_place(mine, by) for by in range(hops, 0, -1)])
+    theirs = swap_tp(before)
     queries = (matmul(first_low, query_full) * scale).astype(LOW)
-    window = jnp.concatenate(before + [keyval], axis=0)
+    keys = jnp.where(first_tp, before, theirs)
+    values = jnp.where(first_tp, theirs, before)
+    window = jnp.concatenate([jnp.concatenate([keys, values], axis=1), keyval], axis=0)
     attended, probs = attend(queries, window, place.reshape(1), hops)
     (branch,) = product("nt", attended, small_full, bm=rows, bn=512, width=features, col=1)
     middle, second_low, second_inverse = by_rows(
@@ -795,6 +827,8 @@
         "share": (rows, features),
         "share_other0": (rows // 2, features),
         "share_other1": (rows // 2, features),
+        "input_grad": (rows, features),
+        "output": (rows, features),
     }
     shapes = {key: jax.ShapeDtypeStruct(shape, LOW) for key, shape in plain.items()}
     for prefix, each in (("d_", units), ("g_", units), ("u_", units), ("o_", width), ("q_", width), ("k_", 2 * HD)):
@@ -813,6 +847,9 @@
         middle=middle,
         second_inverse=second_inverse,
         gain_two=gain_two,
+        gain_one=gain_one,
+        tokens=tokens,
+        first_inverse=jnp.broadcast_to(first_inverse, (rows, 128)),
         queries=queries,
         window=window,
         attended=attended,
@@ -844,8 +881,8 @@
 
     reads = stage("d_", "got", "far") + ["cotangent", "hidden", "down_full", "gate_full", "up_full", "small_full"]
     reads += ["to_gate", "to_up", "second_low", "middle", "second_inverse", "gain_two", "attended"]
-    writes = ["gate_back", "up_back", "second", "second_other", "feed0", "feed1", "feed_other0", "middle_low"]
-    writes += ["grad_attended"] + stage("d_", "arrived", "near") + halving("d_", 0, 1)
+    writes = ["gate_back", "up_back", "second", "second_other", "feed0", "feed_other0", "middle_low"]
+    writes += ["grad_attended"] + stage("d_", "arrived", "near") + halving("d_", 0, late + 1)
     writes += stage("g_", "away", "got", "far", "arrived") + stage("u_", "away", "got", "far")
     writes += stage("o_", "away", "got", "far")
     call = remote_call(
@@ -858,12 +895,10 @@
     )
     done |= zip(writes, call(*[done[key] for key in reads]))
 
-    reads = ["cotangent", "hidden", "gate_back", "up_back", "second_low", "first_low", "small_full", "feed1"]
+    reads = ["down_full", "hidden", "gate_back", "up_back", "second_low", "first_low", "small_full"]
     reads += ["queries", "window", "attended", "probs", "grad_attended", "u_far", "g_got", "g_arrived"]
-    reads += ["d_near"] + halving("d_", 0, 1)
-    writes = ["feed_other1", "u_arrived", "query_back", "window_back", "window_other", "keyval_own", "keyval_other"]
-    writes += ["keyval_back", "share", "share_other0", "g_near"] + halving("g_", 0, 1) + halving("d_", 1, late + 1)
-    writes += stage("q_", "away", "got", "far") + stage("k_", "away", "got", "far")
+    writes = ["feed1", "feed_other1", "u_arrived", "query_back", "window_back", "window_other", "keyval_own"]
+    writes += ["share", "share_other0", "g_near", "g_recv0"] + stage("q_", "away", "got", "far")
     call = remote_call(
         by_name(functools.partial(scores_back, hops=hops, **sizes), reads, writes, 1),
         reads,
@@ -874,11 +909,14 @@
     )
     done |= zip(writes, call(*[done[key] for key in reads]))
 
-    reads = ["gate_back", "up_back", "second_low", "first_low", "middle_low", "attended", "query_back", "keyval_back"]
-    reads += ["share", "u_got", "u_arrived", "g_near"] + halving("g_", 0, 1)
-    reads += [prefix + key for prefix in ("o_", "q_", "k_") for key in ("got", "far")]
-    writes = ["share_other1", "u_near"] + [prefix + key for prefix in ("o_", "q_", "k_") for key in ("arrived", "near")]
-    writes += halving("g_", 1, late + 1)
+    reads = ["gate_back", "up_back", "second_low", "first_low", "middle_low", "attended", "query_back", "keyval_own"]
+    reads += ["share", "share_other0", "tokens", "first_inverse", "gain_one", "small_full", "middle"]
+    reads += ["feed0", "feed1", "feed_other0", "feed_other1", "u_got", "u_arrived", "g_near", "g_recv0"]
+    reads += [prefix + key for prefix in ("o_", "q_") for key in ("got", "far")]
+    writes = ["share_other1", "u_near", "keyval_other", "keyval_back", "input_grad", "output"]
+    writes += stage("k_", "away", "got", "far")
+    writes += [prefix + key for prefix in ("o_", "q_", "k_") for key in ("arrived", "near")]
+    writes += [key for key in halving("g_", 0, late + 1) if key != "g_recv0"]
     for prefix in ("u_", "o_", "q_", "k_"):
         writes += halving(prefix, 0, late + 1)
     call = remote_call(
@@ -890,17 +928,6 @@
         "last_sums",
     )
     done |= zip(writes, call(*[done[key] for key in reads]))
-    share_other = jnp.concatenate([done["share_other0"], done["share_other1"]])
-    feed = jnp.concatenate([done["feed0"], done["feed1"]]).astype(WIDE)
-    feed_other = jnp.concatenate([done["feed_other0"], done["feed_other1"]]).astype(WIDE)
-    (input_grad,) = by_rows(
-        source_back,
-        [tokens, done["middle_low"], done["share"], share_other, done["keyval_back"]],
-        [gain_one, keyval_full],
-        [(features, LOW)],
-        block,
-    )
-    output = (middle.astype(WIDE) + (feed + feed_other)).astype(LOW)
     down_grad, gate_grad, up_grad, out_grad, query_grad, keyval_grad = (
         scatter_result(prefix, done) for prefix in ("d_", "g_", "u_", "o_", "q_", "k_")
     )
@@ -918,8 +945,8 @@
     first_grad = (sums[0] + row_sum(keyval_weight, keyval_grad)) / (1.0 + first_gain.astype(WIDE))
     second_grad = sums[1] / (1.0 + second_gain.astype(WIDE))
     return (
-        output,
-        input_grad,
+        done["output"],
+        done["input_grad"],
         query_grad,
         keyval_grad,
         out_grad,

time: 1240 us -> 1180 us (0.952)
  waiting for transfers between devices: 327 us -> 288 us
  Pallas kernels: 819 us -> 800 us
    ppermute x2, waiting for transfers between devices: 57.5 us -> 29.2 us  [from_place(): lax.ppermute(array, 'ctx', [(i, i + by) for i in range(count) if i + by <...]
    all_gather x4, waiting for transfers between devices: 161 us -> 135 us  [gathered(): return lax.all_gather(shard, ('fsdp', 'ctx'), axis=0, tiled=True)]
    ppermute x2 -> x3, waiting for transfers between devices: 106 us -> 122 us  [swap_tp(): return lax.ppermute(array, 'tp', [(0, 1), (1, 0)])]
    pallas_call x2 -> x1, Pallas kernels: 25.6 us -> 12 us  [by_rows(): pl.pallas_call(lambda *refs: body(refs[:n_in], refs[n_in:]), grid=(rows /...]
  transfers between devices with their start and end apart: 8 -> 9, of which waited for: 6 -> 7; matrix products, arithmetic and copies ran while one was open for 4% -> 3% of each run, Pallas kernels for 14% -> 14%
where the time goes in v3:
time: 1180 us; the launch traced here: 1170 us
  Pallas kernels  800 us (68%)
  waiting for transfers between devices  288 us (24%)
  other arithmetic  25.6 us (2%)
  matrix products  18.4 us (2%)
  local copies, waits for them, and re-layouts  15.1 us (1%)
  between operations  14.3 us (1%)
    pallas_call x4, Pallas kernels, on_device(): done |= zip(writes, call(*[done[key] for key in reads]))  684 us
    all_gather x4, waiting for transfers between devices, gathered(): return lax.all_gather(shard, ('fsdp', 'ctx'), axis=0, tiled=True)  135 us
    ppermute x3, waiting for transfers between devices, swap_tp(): return lax.ppermute(array, 'tp', [(0, 1), (1, 0)])  122 us
    pallas_call x3, Pallas kernels, product(): pl.pallas_call(products_body(kind, 1, len(extras), finish, sub, keep_bloc...  75.1 us
    ppermute x2, waiting for transfers between devices, from_place(): lax.ppermute(array, 'ctx', [(i, i + by) for i in range(count) if i + by <...  29.2 us
    pallas_call x1, Pallas kernels, attend(): pl.pallas_call(functools.partial(attend_kernel, heads=heads, hops=hops, r...  28.6 us
  transfers between devices with their start and end apart: 9, of which 7 were waited for; matrix products, arithmetic and copies ran while one was open for 3% of the time, Pallas kernels for 14%

profile of v3, /device:TPU:0, one launch (start us, length us, event | category | flops | bytes accessed | tf_op | source)
XLA Modules:
  0.0 1171.8 jit_solution(15011565511034905609)
XLA Ops:
  8.7 2.3 fusion.13
  13.0 3.6 fusion
  16.6 121.5 %all-gather.5.cloned.1.call-done.refs_1_.refs_7_.refs_6_.refs_13_ = bf16[2560,3200]{1,0:T(8,128)(2,1)} async-done(((bf16[160,3200]{1,0:T(8,128)(2,1)}), bf16[2560,3200]{1,0:T(8,128)(2,1)}) %all-gather.5.cloned.1.call-update) | async-done | bytes 16384016 | tf_op jit(solution)/shard_map/all_gather | solution.py:740
  138.2 1.2 add_bitcast_fusion.3
  140.1 3.8 fusion.2.refs_5_.refs_3_
  143.9 6.5 fusion.10
  151.4 4.2 collective-permute-start
  155.6 3.3 collective-permute-start.1
  158.9 13.7 %collective-permute-done = bf16[1024,256]{1,0:T(8,128)(2,1)} collective-permute-done((bf16[1024,256]{1,0:T(8,128)(2,1)S(1)}, bf16[1024,256]{1,0:T(8,128)(2,1)}, u32[]{:S(2)}, u32[]{:S(2)}) %collective-permute-start) | collective-permute-done | bytes 524320 | tf_op jit(solution)/shard_map/ppermute | solution.py:732
  173.7 15.5 %collective-permute-done.1 = bf16[1024,256]{1,0:T(8,128)(2,1)} collective-permute-done((bf16[1024,256]{1,0:T(8,128)(2,1)S(1)}, bf16[1024,256]{1,0:T(8,128)(2,1)}, u32[]{:S(2)}, u32[]{:S(2)}) %collective-permute-start.1) | collective-permute-done | bytes 524320 | tf_op jit(solution)/shard_map/ppermute | solution.py:732
  190.3 1.6 collective-permute-start.2
  191.8 11.9 %multiply_convert_fusion.q_ref.refs_7_ = bf16[1024,1280]{1,0:T(8,128)(2,1)} fusion(bf16[1024,2560]{1,0:T(8,128)(2,1)} %copy-done, bf16[2560,3200]{1,0:T(8,128)(2,1)} %all-gather.5.cloned.1.call-done.refs_1_.refs_7_.refs_6_.refs_13_), kind=kOutput, calls=%fused_computation.7 | convolution fusion | flops 6713507840 | bytes 14417920 | tf_op jit(solution)/shard_map/dot_general | solution.py:22
  203.8 11.1 collective-permute-done.2
  215.0 1.8 pad_maximum_fusion.win_ref.refs_8_
  216.9 28.6 %attend.1 = (bf16[1024,1280]{1,0:T(8,128)(2,1)}, bf16[5,1024,2304]{2,1,0:T(8,128)(2,1)}) custom-call(s32[1]{0:T(128)} %bitcast.place_ref, bf16[1024,1280]{1,0:T(8,128)(2,1)} %multiply_convert_fusion.q_ref.refs_7_, bf16[3072,512]{1,0:T(8,128)(2,1)} %pad_maximum_fusion.win_ref.refs_8_), custom_call_target="tpu_custom_call" | custom-call | tf_op jit(solution)/shard_map/attend/pallas_call | solution.py:66
  245.5 11.4 product.3.refs_1_
  256.9 1.5 collective-permute-start.3
  260.3 110.4 %collective-permute-done.3.refs_2_ = bf16[1024,2560]{1,0:T(8,128)(2,1)} collective-permute-done((bf16[1024,2560]{1,0:T(8,128)(2,1)}, bf16[1024,2560]{1,0:T(8,128)(2,1)}, u32[]{:S(2)}, u32[]{:S(2)}) %collective-permute-start.3) | collective-permute-done | bytes 5242912 | tf_op jit(solution)/shard_map/ppermute | solution.py:736
  370.7 12.0 %by_rows.1 = (bf16[1024,2560]{1,0:T(8,128)(2,1)}, bf16[1024,2560]{1,0:T(8,128)(2,1)}, f32[1024,128]{1,0:T(8,128)}) custom-call(bf16[1024,2560]{1,0:T(8,128)(2,1)} %refs_10_.1, bf16[1024,2560]{1,0:T(8,128)(2,1)} %product.3.refs_1_, bf16[1024,2560]{1,0:T(8,128)(2,1)} %collective-permute-done.3.refs_2_, f32[1,2560]{1,0:T(1,128)} %copy.29.refs_3_.refs_13_), custom_call_target="tpu_custom_call" | custom-call | tf_op jit(solution)/shard_map/by_rows/pallas_call | solution.py:149
  382.7 26.9 %product.4.refs_2_ = f32[1024,3840]{1,0:T(8,128)} custom-call(bf16[1024,2560]{1,0:T(8,128)(2,1)} %get-tuple-element.58.refs_0_.refs_10_.refs_4_.refs_2_, bf16[2560,3840]{1,0:T(8,128)(2,1)} %all-gather.9.cloned.1.call-done.refs_1_.refs_5_), custom_call_target="tpu_custom_call" | custom-call | tf_op jit(solution)/shard_map/product/pallas_call | solution.py:133
  409.6 36.8 %product.5 = (bf16[1024,3840]{1,0:T(8,128)(2,1)}, bf16[1024,3840]{1,0:T(8,128)(2,1)}, bf16[1024,3840]{1,0:T(8,128)(2,1)}) custom-call(bf16[1024,2560]{1,0:T(8,128)(2,1)} %get-tuple-element.58.refs_0_.refs_10_.refs_4_.refs_2_, bf16[2560,3840]{1,0:T(8,128)(2,1)} %all-gather.7.cloned.1.call-done.refs_1_.refs_6_, f32[1024,3840]{1,0:T(8,128)} %product.4.refs_2_), custom_call_target="tpu_custom_call" | custom-call | tf_op jit(solution)/shard_map/product/pallas_call | solution.py:133
  446.4 44.1 %down_start.1 = (bf16[1280,3840]{1,0:T(8,128)(2,1)}, bf16[1280,3840]{1,0:T(8,128)(2,1)}, bf16[640,3840]{1,0:T(8,128)(2,1)}) custom-call(bf16[1024,2560]{1,0:T(8,128)(2,1)} %refs_2_.1, bf16[1024,3840]{1,0:T(8,128)(2,1)} %get-tuple-element.59.refs_1_.refs_3_), custom_call_target="tpu_custom_call" | custom-call | tf_op jit(solution)/shard_map/down_start/pallas_call | solution.py:880
  490.5 13.4 %all-gather.11.cloned.1.call-done.refs_4_.refs_0_ = bf16[2560,3840]{1,0:T(8,128)(2,1)} async-done(((bf16[160,3840]{1,0:T(8,128)(2,1)}), bf16[2560,3840]{1,0:T(8,128)(2,1)}) %all-gather.11.cloned.1.call-update) | async-done | bytes 19660816 | tf_op jit(solution)/shard_map/all_gather | solution.py:740
  503.9 250.0 %feed_back.1 = (bf16[1024,3840]{1,0:T(8,128)(2,1)}, bf16[1024,3840]{1,0:T(8,128)(2,1)}, bf16[1024,2560]{1,0:T(8,128)(2,1)}, bf16[1024,2560]{1,0:T(8,128)(2,1)}, ...) custom-call(bf16[1280,3840]{1,0:T(8,128)(2,1)} %get-tuple-element.60, ...), custom_call_target="tpu_custom_call" | custom-call | tf_op jit(solution)/shard_map/feed_back/pallas_call | solution.py:896
  753.9 175.1 %scores_back.1 = (bf16[512,2560]{1,0:T(8,128)(2,1)}, bf16[512,2560]{1,0:T(8,128)(2,1)}, bf16[640,3840]{1,0:T(8,128)(2,1)}, bf16[1024,1280]{1,0:T(8,128)(2,1)}, b...) custom-call(bf16[2560,3840]{1,0:T(8,128)(2,1)} %all-gather.11.cloned, ...), custom_call_target="tpu_custom_call" | custom-call | tf_op jit(solution)/shard_map/scores_back/pallas_call | solution.py:910
  930.0 215.2 %last_sums.1 = (bf16[512,2560]{1,0:T(8,128)(2,1)}, bf16[4,160,3840]{2,1,0:T(8,128)(2,1)}, bf16[1024,512]{1,0:T(8,128)(2,1)}, bf16[1024,512]{1,0:T(8,128)(2,1)}, ...) custom-call(bf16[1024,3840]{1,0:T(8,128)(2,1)} %get-tuple-element.66, ...), custom_call_target="tpu_custom_call" | custom-call | tf_op jit(solution)/shard_map/last_sums/pallas_call | solution.py:930
  1145.3 2.2 multiply_reduce_fusion.2
  1147.5 6.0 multiply_reduce_fusion
  1154.6 1.7 add_bitcast_fusion
  1158.4 2.7 copy.35
  1161.1 1.4 slice-done
  1162.7 2.4 copy.36
  (72 shorter events, 14.0 us)
Async XLA Ops:
  7.2 131.0 %all-gather.5.cloned.1.call-start = ((), (), s32[]{:S(2)}) async-start(), calls=%async_computation | async-start | bytes 17408000 | tf_op jit(solution)/shard_map/all_gather | solution.py:740
  11.0 371.7 %all-gather.9.cloned.1.call-start = ((), (), s32[]{:S(2)}) async-start(), calls=%async_computation.2 | async-start | bytes 20889600 | tf_op jit(solution)/shard_map/all_gather | solution.py:740
  11.7 397.9 %all-gather.7.cloned.1.call-start = ((), (), s32[]{:S(2)}) async-start(), calls=%async_computation.1 | async-start | bytes 20889600 | tf_op jit(solution)/shard_map/all_gather | solution.py:740
  12.5 491.4 %all-gather.11.cloned.1.call-start = ((), (), s32[]{:S(2)}) async-start(), calls=%async_computation.3 | async-start | bytes 20889600 | tf_op jit(solution)/shard_map/all_gather | solution.py:740
  143.9 6.5 copy-start
  150.4 1.0 copy-start.3
  151.4 21.3 %collective-permute-start = (bf16[1024,256]{1,0:T(8,128)(2,1)S(1)}, bf16[1024,256]{1,0:T(8,128)(2,1)}, u32[]{:S(2)}, u32[]{:S(2)}) collective-permute-start(bf16[1024,256]{1,0:T(8,128)(2,1)S(1)} %slice_select_fusion), channel_id=1, source_target_pairs={{0,4},{2,6},{1,5},{3,7},{8,12},{10,14},{9,13},{11,15},{16,20},{18,... | collective-permute-start | bytes 1572872 | tf_op jit(solution)/shard_map/ppermute | solution.py:732
  155.6 33.6 %collective-permute-start.1 = (bf16[1024,256]{1,0:T(8,128)(2,1)S(1)}, bf16[1024,256]{1,0:T(8,128)(2,1)}, u32[]{:S(2)}, u32[]{:S(2)}) collective-permute-start(bf16[1024,256]{1,0:T(8,128)(2,1)S(1)} %slice_select_fusion), channel_id=1, source_target_pairs={{0,2},{2,4},{4,6},{1,3},{3,5},{5,7},{8,10},{10,12},{12,14},{9,11},... | collective-permute-start | bytes 1572872 | tf_op jit(solution)/shard_map/ppermute | solution.py:732
  190.3 24.6 %collective-permute-start.2 = (bf16[2048,256]{1,0:T(8,128)(2,1)S(1)}, bf16[2048,256]{1,0:T(8,128)(2,1)S(1)}, u32[]{:S(2)}, u32[]{:S(2)}) collective-permute-start(bf16[2048,256]{1,0:T(8,128)(2,1)S(1)} %constant_dynamic-update-slice_fusion), channel_id=1, source_target_pairs={{0,1},{1,0},{2,3},{3,2},{4,5},{5,4},{6,7},{7,6},{8,9},{9,8},{10,11... | collective-permute-start | bytes 3145736 | tf_op jit(solution)/shard_map/ppermute | solution.py:736
  203.8 11.3 copy-start.4
  256.9 113.8 %collective-permute-start.3 = (bf16[1024,2560]{1,0:T(8,128)(2,1)}, bf16[1024,2560]{1,0:T(8,128)(2,1)}, u32[]{:S(2)}, u32[]{:S(2)}) collective-permute-start(bf16[1024,2560]{1,0:T(8,128)(2,1)} %product.3.refs_1_), channel_id=1, source_target_pairs={{0,1},{1,0},{2,3},{3,2},{4,5},{5,4},{6,7},{7,6},{8,9},{9,8},{10,11... | collective-permute-start | bytes 15728648 | tf_op jit(solution)/shard_map/ppermute | solution.py:736
  930.0 215.3 %copy-start.5 = (bf16[160,1280]{1,0:T(8,128)(2,1)S(1)}, bf16[160,1280]{1,0:T(8,128)(2,1)}, u32[]{:S(2)}) copy-start(bf16[160,1280]{1,0:T(8,128)(2,1)} %param.11) | copy-start | bytes 1228804
  930.0 217.5 %copy-start.1 = (bf16[160,3840]{1,0:T(8,128)(2,1)S(1)}, bf16[160,3840]{1,0:T(8,128)(2,1)}, u32[]{:S(2)}) copy-start(bf16[160,3840]{1,0:T(8,128)(2,1)} %param.14) | copy-start | bytes 3686404
  930.0 217.5 %copy-start.2 = (bf16[160,3840]{1,0:T(8,128)(2,1)S(1)}, bf16[160,3840]{1,0:T(8,128)(2,1)}, u32[]{:S(2)}) copy-start(bf16[160,3840]{1,0:T(8,128)(2,1)} %param.15) | copy-start | bytes 3686404
  1147.5 10.9 slice-start.2
  1147.5 6.1 copy-start.9
  1147.5 6.1 copy-start.10
  1147.5 7.2 copy-start.6
  1147.5 7.1 copy-start.8
  1147.5 10.9 slice-start.3
  1153.5 3.6 collective-permute-start.4
  1153.6 2.7 copy-start.7
  1153.6 2.7 copy-start.11
  1153.6 2.7 copy-start.12
  1154.6 2.6 copy-start.13
  1154.6 3.2 copy-start.14
  1158.4 4.1 slice-start
  1158.4 4.4 slice-start.1
Sparse Core Ops, SparseCore 0:
  11.1 127.0 all-gather.4
  139.7 128.6 all-gather.8
  269.9 118.5 all-gather.6
  390.0 113.8 all-gather.10

commit v4 on v2

--- a/solution.py
+++ b/solution.py
@@ -182,13 +182,16 @@
 
 
 def source_back(ins, outs):
-    tokens, middle_low, own, other, keyval_back, gain, keyval_full = ins
+    tokens, middle_low, inverse, own, other, keyval_back, gain, keyval_full = ins
     grad = own[...].astype(WIDE) + other[...].astype(WIDE)
     grad = grad + right_transposed(keyval_back[...], keyval_full[...])
-    values = tokens[...].astype(WIDE)
-    inverse = lax.rsqrt(jnp.mean(values * values, axis=1, keepdims=True) + EPS)
-    back = middle_low[...].astype(WIDE) + norm_back(values, grad, gain[...], inverse)
-    outs[0][...] = back.astype(LOW)
+    back = norm_back(tokens[...].astype(WIDE), grad, gain[...], inverse[:, :1])
+    outs[0][...] = (middle_low[...].astype(WIDE) + back).astype(LOW)
+
+
+def add_feed(ins, outs):
+    middle, own, other = ins
+    outs[0][...] = (middle[...].astype(WIDE) + (own[...].astype(WIDE) + other[...].astype(WIDE))).astype(LOW)
 
 
 def finish_up(upward, gate):
@@ -413,7 +416,7 @@
 
 def remote_call(kernel, inputs, outputs, scratch, collective_id, name):
     anywhere = pl.BlockSpec(memory_space=pl.ANY)
-    sems = pltpu.SemaphoreType.DMA((32,))
+    sems = pltpu.SemaphoreType.DMA((64,))
     return pl.pallas_call(
         kernel,
         in_specs=[anywhere] * len(inputs),
@@ -532,18 +535,60 @@
     outs[0][...] = (ins[0][...].astype(WIDE) + ins[1][...].astype(WIDE)).astype(LOW)
 
 
-def feed_back(r, links, total, *, rows, heads, count):
-    half, block = rows // 2, min(256, rows)
+def backward(r, links, total, *, rows, heads, hops, count):
+    half = rows // 2
+    block = min(256, half)
     features = r["cotangent"].shape[1]
     width = heads * HD
     third = r["hidden"].shape[1] // 3
     bits = bits_of(count)
-    links.meet([links.core, links.chip, links.tp] + [links.along(bit) for bit in bits])
+    links.meet([links.core, links.chip, links.tp] + [{"ctx": lax.rem(links.place + k, count)} for k in range(1, count)])
     down = Scatter("d_", r, links, "cotangent", "hidden", third, count, total)
     gate = Scatter("g_", r, links, "second_low", "gate_back", third, count, total)
     up = Scatter("u_", r, links, "second_low", "up_back", third, count, total)
     out = Scatter("o_", r, links, "middle_low", "attended", width, count, total)
-    top, bottom = pl.ds(0, half), pl.ds(half, half)
+    query = Scatter("q_", r, links, "first_low", "query_back", width, count, total)
+    keyval = Scatter("k_", r, links, "first_low", "keyval_back", 2 * HD, count, total)
+    parts = (pl.ds(0, half), pl.ds(half, half))
+
+    def second(part):
+        job(
+            "nt",
+            [(r["gate_back"].at[part], r["gate_full"]), (r["up_back"].at[part], r["up_full"])],
+            [r["second"].at[part]],
+            bm=half,
+            bn=256,
+        )
+        return links.send(r["second"].at[part], r["second_other"].at[part], links.tp)
+
+    def feed(k):
+        job("nt", [(r["hidden"].at[parts[k]], r["down_full"])], [r[f"feed{k}"]], bm=half, bn=512)
+        return links.send(r[f"feed{k}"], r[f"feed_other{k}"], links.tp)
+
+    def share(k):
+        return links.send(r["share"].at[parts[k]], r[f"share_other{k}"], links.tp)
+
+    def finish_source(k):
+        part = parts[k]
+        rows_job(
+            source_back,
+            [r[key].at[part] for key in ("tokens", "middle_low", "first_inverse", "share")]
+            + [r[f"share_other{k}"], r["keyval_back"].at[part]],
+            [r["gain_one"], r["small_full"].at[:, pl.ds(2 * width, 2 * HD)]],
+            [r["input_grad"].at[part]],
+            block,
+        )
+
+    def finish_output(k):
+        part = parts[k]
+        rows_job(add_feed, [r["middle"].at[part], r[f"feed{k}"], r[f"feed_other{k}"]], [], [r["output"].at[part]], block)
+
+    def windows_to(place, by):
+        return links.copy(
+            r["window_back"].at[pl.ds((hops - by) * rows, rows)],
+            r["window_other"].at[by - 1],
+            {"ctx": lax.rem(place + count - by, count)},
+        )
 
     down.cross()
     job(
@@ -556,31 +601,18 @@
         extras=[(r["to_gate"], 0), (r["to_up"], 0)],
         finish=finish_hidden,
     )
-
-    def second(part):
-        job(
-            "nt",
-            [(r["gate_back"].at[part], r["gate_full"]), (r["up_back"].at[part], r["up_full"])],
-            [r["second"].at[part]],
-            bm=half,
-            bn=256,
-        )
-        return links.send(r["second"].at[part], r["second_other"].at[part], links.tp)
-
-    first = second(top)
-    last = second(bottom)
     gate.away()
+    second0 = second(parts[0])
+    gate.far()
+    gate.cross()
+    second1 = second(parts[1])
+    up.away()
     down.near()
     down.halve(0)
-    gate.far()
-    gate.cross()
-    up.away()
-    job("nt", [(r["hidden"].at[top], r["down_full"])], [r["feed0"]], bm=half, bn=512)
-    job("nt", [(r["hidden"].at[bottom], r["down_full"])], [r["feed1"]], bm=half, bn=512)
     up.far()
-    first.wait_recv()
-    last.wait_recv()
-    feed = links.send(r["feed0"], r["feed_other0"], links.tp)
+    feed0 = feed(0)
+    second0.wait_recv()
+    second1.wait_recv()
     rows_job(
         middle_back,
         [r["cotangent"], r["middle"], r["second_inverse"], r["second"], r["second_other"]],
@@ -588,36 +620,16 @@
         [r["middle_low"], r["grad_attended"]],
         block,
     )
-    out.away()
+    feed1 = feed(1)
+    gate.wait("arrived")
+    up.cross()
     down.add(0)
-    out.far()
-    gate.wait("arrived")
-    feed.wait_recv()
-    links.close()
-
-
-def scores_back(r, links, total, *, rows, heads, hops, count):
-    half, block = rows // 2, min(256, rows)
-    width = heads * HD
-    third = r["up_back"].shape[1] // 3
-    links.meet([links.core, links.chip, links.tp] + [{"ctx": lax.rem(links.place + k, count)} for k in range(1, count)])
-    down = Scatter("d_", r, links, "cotangent", "hidden", third, count, total)
-    gate = Scatter("g_", r, links, "second_low", "gate_back", third, count, total)
-    up = Scatter("u_", r, links, "second_low", "up_back", third, count, total)
-    query = Scatter("q_", r, links, "first_low", "query_back", width, count, total)
-    keyval = Scatter("k_", r, links, "first_low", "keyval_back", 2 * HD, count, total)
-
-    up.cross()
-    feed = links.send(r["feed1"], r["feed_other1"], links.tp)
-    down.halve(1)
-    attend_back(r, rows, heads, block)
+    if len(bits) > 1:
+        down.halve(1)
+    attend_back(r, rows, heads, min(256, rows))
     windows = []
     for by in range(1, hops + 1):
-        move = links.copy(
-            r["window_back"].at[pl.ds((hops - by) * rows, rows)],
-            r["window_other"].at[by - 1],
-            {"ctx": lax.rem(links.place + count - by, count)},
-        )
+        move = windows_to(links.place, by)
 
         @pl.when(links.place >= by)
         def _(move=move):
@@ -626,10 +638,21 @@
         windows.append(move)
     gate.near()
     gate.halve(0)
+    out.away()
     job("nt", [(r["query_back"], r["small_full"].at[:, pl.ds(0, width)])], [r["share"]], bm=rows, bn=512)
-    feed.wait_recv()
-    share = links.send(r["share"].at[pl.ds(0, half)], r["share_other0"], links.tp)
+    share0 = share(0)
+    out.far()
     query.away()
+    feed0.wait_recv()
+    finish_output(0)
+    query.far()
+    up.wait("arrived")
+    out.cross()
+    up.near()
+    gate.add(0)
+    if len(bits) > 1:
+        gate.halve(1)
+    up.halve(0)
     for by in range(1, hops + 1):
 
         @pl.when(links.place + by < count)
@@ -644,59 +667,45 @@
         block,
     )
     swap = links.send(r["keyval_own"], r["keyval_other"], links.tp)
-    query.far()
-    gate.add(0)
+    share1 = share(1)
+    out.near()
+    out.halve(0)
+    query.cross()
+    feed1.wait_recv()
+    finish_output(1)
     swap.wait_recv()
     rows_job(pair_sum, [r["keyval_own"], r["keyval_other"]], [], [r["keyval_back"]], block)
     keyval.away()
-    down.rest(1)
+    up.add(0)
+    if len(bits) > 1:
+        up.halve(1)
     keyval.far()
-    up.wait("arrived")
-    share.wait_recv()
+    keyval.cross()
+    query.near()
+    query.halve(0)
+    out.add(0)
+    if len(bits) > 1:
+        out.halve(1)
+    share0.wait_recv()
+    finish_source(0)
+    keyval.near()
+    keyval.halve(0)
+    query.add(0)
+    if len(bits) > 1:
+        query.halve(1)
+    share1.wait_recv()
+    finish_source(1)
+    keyval.add(0)
+    if len(bits) > 1:
+        keyval.halve(1)
+        for each in (down, gate, up, out, query, keyval):
+            each.rest(1)
     for by in range(1, hops + 1):
 
         @pl.when(links.place >= by)
         def _(move=windows[by - 1]):
             move.wait_send()
 
-    links.close()
-
-
-def last_sums(r, links, total, *, rows, heads, count):
-    half = rows // 2
-    width = heads * HD
-    third = r["up_back"].shape[1] // 3
-    bits = bits_of(count)
-    links.meet([links.chip, links.tp] + [links.along(bit) for bit in bits])
-    gate = Scatter("g_", r, links, "second_low", "gate_back", third, count, total)
-    up = Scatter("u_", r, links, "second_low", "up_back", third, count, total)
-    out = Scatter("o_", r, links, "middle_low", "attended", width, count, total)
-    query = Scatter("q_", r, links, "first_low", "query_back", width, count, total)
-    keyval = Scatter("k_", r, links, "first_low", "keyval_back", 2 * HD, count, total)
-    share = links.send(r["share"].at[pl.ds(half, half)], r["share_other1"], links.tp)
-    out.cross()
-    gate.halve(1)
-    up.near()
-    up.halve(0)
-    out.near()
-    out.halve(0)
-    query.cross()
-    keyval.cross()
-    up.add(0)
-    up.halve(1)
-    query.near()
-    query.halve(0)
-    out.add(0)
-    out.halve(1)
-    keyval.near()
-    keyval.halve(0)
-    query.add(0)
-    query.halve(1)
-    keyval.add(0)
-    keyval.halve(1)
-    for each in (gate, up, out, query, keyval):
-        each.rest(1)
-    share.wait_recv()
     links.close()
 
 
@@ -749,9 +758,14 @@
     first_inverse = lax.rsqrt(jnp.mean(source * source, axis=-1, keepdims=True) + EPS)
     first_low = (source * first_inverse * gain_one).astype(LOW)
     keyval = matmul(first_low, keyval_full).astype(LOW)
-    before = [from_place(keyval, by) for by in range(hops, 0, -1)]
+    first_tp = lax.axis_index("tp") == 0
+    mine = jnp.where(first_tp, keyval[:, :HD], keyval[:, HD:])
+    before = jnp.concatenate([from_place(mine, by) for by in range(hops, 0, -1)])
+    theirs = swap_tp(before)
     queries = (matmul(first_low, query_full) * scale).astype(LOW)
-    window = jnp.concatenate(before + [keyval], axis=0)
+    keys = jnp.where(first_tp, before, theirs)
+    values = jnp.where(first_tp, theirs, before)
+    window = jnp.concatenate([jnp.concatenate([keys, values], axis=1), keyval], axis=0)
     attended, probs = attend(queries, window, place.reshape(1), hops)
     (branch,) = product("nt", attended, small_full, bm=rows, bn=512, width=features, col=1)
     middle, second_low, second_inverse = by_rows(
@@ -795,6 +809,8 @@
         "share": (rows, features),
         "share_other0": (rows // 2, features),
         "share_other1": (rows // 2, features),
+        "input_grad": (rows, features),
+        "output": (rows, features),
     }
     shapes = {key: jax.ShapeDtypeStruct(shape, LOW) for key, shape in plain.items()}
     for prefix, each in (("d_", units), ("g_", units), ("u_", units), ("o_", width), ("q_", width), ("k_", 2 * HD)):
@@ -813,6 +829,9 @@
         middle=middle,
         second_inverse=second_inverse,
         gain_two=gain_two,
+        gain_one=gain_one,
+        tokens=tokens,
+        first_inverse=jnp.broadcast_to(first_inverse, (rows, 128)),
         queries=queries,
         window=window,
         attended=attended,
@@ -843,64 +862,20 @@
     done |= zip(writes, call(*[done[key] for key in reads]))
 
     reads = stage("d_", "got", "far") + ["cotangent", "hidden", "down_full", "gate_full", "up_full", "small_full"]
-    reads += ["to_gate", "to_up", "second_low", "middle", "second_inverse", "gain_two", "attended"]
-    writes = ["gate_back", "up_back", "second", "second_other", "feed0", "feed1", "feed_other0", "middle_low"]
-    writes += ["grad_attended"] + stage("d_", "arrived", "near") + halving("d_", 0, 1)
-    writes += stage("g_", "away", "got", "far", "arrived") + stage("u_", "away", "got", "far")
-    writes += stage("o_", "away", "got", "far")
+    reads += ["to_gate", "to_up", "first_low", "second_low", "middle", "tokens", "first_inverse", "second_inverse"]
+    reads += ["gain_one", "gain_two", "attended", "queries", "window", "probs"]
+    writes = list(plain) + stage("d_", "arrived", "near") + halving("d_", 0, late + 1)
+    for prefix in ("g_", "u_", "o_", "q_", "k_"):
+        writes += stage(prefix, "away", "got", "far", "arrived", "near") + halving(prefix, 0, late + 1)
     call = remote_call(
-        by_name(functools.partial(feed_back, **sizes), reads, writes, 1),
+        by_name(functools.partial(backward, hops=hops, **sizes), reads, writes, 1),
         reads,
         [shapes[key] for key in writes],
         [total],
         1,
-        "feed_back",
+        "backward",
     )
     done |= zip(writes, call(*[done[key] for key in reads]))
-
-    reads = ["cotangent", "hidden", "gate_back", "up_back", "second_low", "first_low", "small_full", "feed1"]
-    reads += ["queries", "window", "attended", "probs", "grad_attended", "u_far", "g_got", "g_arrived"]
-    reads += ["d_near"] + halving("d_", 0, 1)
-    writes = ["feed_other1", "u_arrived", "query_back", "window_back", "window_other", "keyval_own", "keyval_other"]
-    writes += ["keyval_back", "share", "share_other0", "g_near"] + halving("g_", 0, 1) + halving("d_", 1, late + 1)
-    writes += stage("q_", "away", "got", "far") + stage("k_", "away", "got", "far")
-    call = remote_call(
-        by_name(functools.partial(scores_back, hops=hops, **sizes), reads, writes, 1),
-        reads,
-        [shapes[key] for key in writes],
-        [total],
-        2,
-        "scores_back",
-    )
-    done |= zip(writes, call(*[done[key] for key in reads]))
-
-    reads = ["gate_back", "up_back", "second_low", "first_low", "middle_low", "attended", "query_back", "keyval_back"]
-    reads += ["share", "u_got", "u_arrived", "g_near"] + halving("g_", 0, 1)
-    reads += [prefix + key for prefix in ("o_", "q_", "k_") for key in ("got", "far")]
-    writes = ["share_other1", "u_near"] + [prefix + key for prefix in ("o_", "q_", "k_") for key in ("arrived", "near")]
-    writes += halving("g_", 1, late + 1)
-    for prefix in ("u_", "o_", "q_", "k_"):
-        writes += halving(prefix, 0, late + 1)
-    call = remote_call(
-        by_name(functools.partial(last_sums, **sizes), reads, writes, 1),
-        reads,
-        [shapes[key] for key in writes],
-        [total],
-        3,
-        "last_sums",
-    )
-    done |= zip(writes, call(*[done[key] for key in reads]))
-    share_other = jnp.concatenate([done["share_other0"], done["share_other1"]])
-    feed = jnp.concatenate([done["feed0"], done["feed1"]]).astype(WIDE)
-    feed_other = jnp.concatenate([done["feed_other0"], done["feed_other1"]]).astype(WIDE)
-    (input_grad,) = by_rows(
-        source_back,
-        [tokens, done["middle_low"], done["share"], share_other, done["keyval_back"]],
-        [gain_one, keyval_full],
-        [(features, LOW)],
-        block,
-    )
-    output = (middle.astype(WIDE) + (feed + feed_other)).astype(LOW)
     down_grad, gate_grad, up_grad, out_grad, query_grad, keyval_grad = (
         scatter_result(prefix, done) for prefix in ("d_", "g_", "u_", "o_", "q_", "k_")
     )
@@ -918,8 +893,8 @@
     first_grad = (sums[0] + row_sum(keyval_weight, keyval_grad)) / (1.0 + first_gain.astype(WIDE))
     second_grad = sums[1] / (1.0 + second_gain.astype(WIDE))
     return (
-        output,
-        input_grad,
+        done["output"],
+        done["input_grad"],
         query_grad,
         keyval_grad,
         out_grad,

time: 1240 us -> 1110 us (0.90)
  Pallas kernels: 819 us -> 726 us
  waiting for transfers between devices: 327 us -> 293 us
    pallas_call x4 -> x2, Pallas kernels: 690 us -> 611 us  [on_device(): done |= zip(writes, call(*[done[key] for key in reads]))]
    ppermute x2, waiting for transfers between devices: 57.5 us -> 31.7 us  [from_place(): lax.ppermute(array, 'ctx', [(i, i + by) for i in range(count) if i + by <...]
    all_gather x4, waiting for transfers between devices: 161 us -> 136 us  [gathered(): return lax.all_gather(shard, ('fsdp', 'ctx'), axis=0, tiled=True)]
    ppermute x2 -> x3, waiting for transfers between devices: 106 us -> 124 us  [swap_tp(): return lax.ppermute(array, 'tp', [(0, 1), (1, 0)])]
    pallas_call x2 -> x1, Pallas kernels: 25.6 us -> 12 us  [by_rows(): pl.pallas_call(lambda *refs: body(refs[:n_in], refs[n_in:]), grid=(rows /...]
  transfers between devices with their start and end apart: 8 -> 9, of which waited for: 6 -> 6; matrix products, arithmetic and copies ran while one was open for 4% -> 3% of each run, Pallas kernels for 14% -> 15%
where the time goes in v4:
time: 1110 us; the launch traced here: 1100 us
  Pallas kernels  726 us (65%)
  waiting for transfers between devices  293 us (26%)
  other arithmetic  25.7 us (2%)
  matrix products  18.4 us (2%)
  between operations  14.2 us (1%)
    pallas_call x2, Pallas kernels, on_device(): done |= zip(writes, call(*[done[key] for key in reads]))  611 us
    all_gather x4, waiting for transfers between devices, gathered(): return lax.all_gather(shard, ('fsdp', 'ctx'), axis=0, tiled=True)  136 us
    ppermute x3, waiting for transfers between devices, swap_tp(): return lax.ppermute(array, 'tp', [(0, 1), (1, 0)])  124 us
    pallas_call x3, Pallas kernels, product(): pl.pallas_call(products_body(kind, 1, len(extras), finish, sub, keep_bloc...  74.9 us
    ppermute x2, waiting for transfers between devices, from_place(): lax.ppermute(array, 'ctx', [(i, i + by) for i in range(count) if i + by <...  31.7 us
    pallas_call x1, Pallas kernels, attend(): pl.pallas_call(functools.partial(attend_kernel, heads=heads, hops=hops, r...  28.6 us
  transfers between devices with their start and end apart: 9, of which 6 were waited for; matrix products, arithmetic and copies ran while one was open for 3% of the time, Pallas kernels for 15%

profile of v4, /device:TPU:0, one launch (start us, length us, event | category | flops | bytes accessed | tf_op | source)
XLA Modules:
  0.0 1098.5 jit_solution(15820153103810560221)
XLA Ops:
  8.7 2.3 fusion.13
  13.0 3.6 fusion
  16.6 121.5 %all-gather.5.cloned.1.call-done.refs_1_.refs_7_ = bf16[2560,3200]{1,0:T(8,128)(2,1)} async-done(((bf16[160,3200]{1,0:T(8,128)(2,1)}), bf16[2560,3200]{1,0:T(8,128)(2,1)}) %all-gather.5.cloned.1.call-update) | async-done | bytes 16384016 | tf_op jit(solution)/shard_map/all_gather | solution.py:722
  138.2 1.2 convert_add_fusion
  140.4 3.7 fusion.2.refs_10_
  144.1 6.5 fusion.10
  150.7 3.5 collective-permute-start
  154.2 2.6 collective-permute-start.1
  156.8 15.2 %collective-permute-done = bf16[1024,256]{1,0:T(8,128)(2,1)S(1)} collective-permute-done((bf16[1024,256]{1,0:T(8,128)(2,1)S(1)}, bf16[1024,256]{1,0:T(8,128)(2,1)S(1)}, u32[]{:S(2)}, u32[]{:S(2)}) %collective-permute-start) | collective-permute-done | bytes 524320 | tf_op jit(solution)/shard_map/ppermute | solution.py:714
  172.0 16.5 %collective-permute-done.1 = bf16[1024,256]{1,0:T(8,128)(2,1)S(1)} collective-permute-done((bf16[1024,256]{1,0:T(8,128)(2,1)S(1)}, bf16[1024,256]{1,0:T(8,128)(2,1)S(1)}, u32[]{:S(2)}, u32[]{:S(2)}) %collective-permute-start.1) | collective-permute-done | bytes 524320 | tf_op jit(solution)/shard_map/ppermute | solution.py:714
  188.6 1.5 collective-permute-start.2
  190.1 11.9 %multiply_convert_fusion.q_ref.refs_19_ = bf16[1024,1280]{1,0:T(8,128)(2,1)} fusion(bf16[1024,2560]{1,0:T(8,128)(2,1)} %copy-done, bf16[2560,3200]{1,0:T(8,128)(2,1)} %all-gather.5.cloned.1.call-done.refs_1_.refs_7_), kind=kOutput, calls=%fused_computation.7 | convolution fusion | flops 6713507840 | bytes 14417920 | tf_op jit(solution)/shard_map/dot_general | solution.py:22
  202.0 11.2 %collective-permute-done.2 = bf16[2048,256]{1,0:T(8,128)(2,1)S(1)} collective-permute-done((bf16[2048,256]{1,0:T(8,128)(2,1)S(1)}, bf16[2048,256]{1,0:T(8,128)(2,1)S(1)}, u32[]{:S(2)}, u32[]{:S(2)}) %collective-permute-start.2) | collective-permute-done | bytes 1048608 | tf_op jit(solution)/shard_map/ppermute | solution.py:718
  213.3 1.9 pad_maximum_fusion.win_ref.refs_20_
  215.2 28.6 %attend.1 = (bf16[1024,1280]{1,0:T(8,128)(2,1)}, bf16[5,1024,2304]{2,1,0:T(8,128)(2,1)}) custom-call(s32[1]{0:T(128)} %bitcast.place_ref, bf16[1024,1280]{1,0:T(8,128)(2,1)} %multiply_convert_fusion.q_ref.refs_19_, bf16[3072,512]{1,0:T(8,128)(2,1)} %pad_maximum_fusion.win_ref.refs_20_), custom_call_target="tpu_custom_call" | custom-call | tf_op jit(solution)/shard_map/attend/pallas_call | solution.py:66
  243.8 11.4 %product.3.refs_1_ = bf16[1024,2560]{1,0:T(8,128)(2,1)} custom-call(bf16[1024,1280]{1,0:T(8,128)(2,1)} %get-tuple-element.34.refs_0_.refs_18_, bf16[2560,3200]{1,0:T(8,128)(2,1)} %all-gather.5.cloned.1.call-done.refs_1_.refs_7_), custom_call_target="tpu_custom_call" | custom-call | tf_op jit(solution)/shard_map/product/pallas_call | solution.py:133
  255.2 1.5 collective-permute-start.3
  256.7 112.4 %collective-permute-done.3.refs_2_ = bf16[1024,2560]{1,0:T(8,128)(2,1)} collective-permute-done((bf16[1024,2560]{1,0:T(8,128)(2,1)}, bf16[1024,2560]{1,0:T(8,128)(2,1)}, u32[]{:S(2)}, u32[]{:S(2)}) %collective-permute-start.3) | collective-permute-done | bytes 5242912 | tf_op jit(solution)/shard_map/ppermute | solution.py:718
  369.1 12.0 %by_rows.1 = (bf16[1024,2560]{1,0:T(8,128)(2,1)}, bf16[1024,2560]{1,0:T(8,128)(2,1)}, f32[1024,128]{1,0:T(8,128)}) custom-call(bf16[1024,2560]{1,0:T(8,128)(2,1)} %refs_13_.1, bf16[1024,2560]{1,0:T(8,128)(2,1)} %product.3.refs_1_, bf16[1024,2560]{1,0:T(8,128)(2,1)} %collective-permute-done.3.refs_2_, f32[1,2560]{1,0:T(1,128)} %get-tuple-element.70.refs_3_.refs_17_), custom_call_target="tpu_custom_call" | custom-call | tf_op jit(solution)/shard_map/by_rows/pallas_call | solution.py:149
  381.0 26.9 %product.4.refs_2_ = f32[1024,3840]{1,0:T(8,128)} custom-call(bf16[1024,2560]{1,0:T(8,128)(2,1)} %get-tuple-element.35.refs_0_.refs_11_, bf16[2560,3840]{1,0:T(8,128)(2,1)} %all-gather.9.cloned.1.call-done.refs_1_.refs_5_), custom_call_target="tpu_custom_call" | custom-call | tf_op jit(solution)/shard_map/product/pallas_call | solution.py:133
  407.9 36.6 %product.5 = (bf16[1024,3840]{1,0:T(8,128)(2,1)}, bf16[1024,3840]{1,0:T(8,128)(2,1)}, bf16[1024,3840]{1,0:T(8,128)(2,1)}) custom-call(bf16[1024,2560]{1,0:T(8,128)(2,1)} %get-tuple-element.35.refs_0_.refs_11_, bf16[2560,3840]{1,0:T(8,128)(2,1)} %all-gather.7.cloned.1.call-done.refs_1_.refs_6_, f32[1024,3840]{1,0:T(8,128)} %product.4.refs_2_), custom_call_target="tpu_custom_call" | custom-call | tf_op jit(solution)/shard_map/product/pallas_call | solution.py:133
  444.5 45.0 %down_start.1 = (bf16[1280,3840]{1,0:T(8,128)(2,1)}, bf16[1280,3840]{1,0:T(8,128)(2,1)}, bf16[640,3840]{1,0:T(8,128)(2,1)}) custom-call(bf16[1024,2560]{1,0:T(8,128)(2,1)} %refs_2_.1, bf16[1024,3840]{1,0:T(8,128)(2,1)} %get-tuple-element.36.refs_1_.refs_3_), custom_call_target="tpu_custom_call" | custom-call | tf_op jit(solution)/shard_map/down_start/pallas_call | solution.py:862
  489.5 14.3 %all-gather.11.cloned.1.call-done.refs_4_ = bf16[2560,3840]{1,0:T(8,128)(2,1)} async-done(((bf16[160,3840]{1,0:T(8,128)(2,1)}), bf16[2560,3840]{1,0:T(8,128)(2,1)}) %all-gather.11.cloned.1.call-update) | async-done | bytes 19660816 | tf_op jit(solution)/shard_map/all_gather | solution.py:722
  503.8 1.0 broadcast_in_dim.2.refs_14_
  504.8 565.5 %backward.1 = (bf16[1024,3840]{1,0:T(8,128)(2,1)}, bf16[1024,3840]{1,0:T(8,128)(2,1)}, bf16[1024,2560]{1,0:T(8,128)(2,1)}, bf16[1024,2560]{1,0:T(8,128)(2,1)}, b...) custom-call(bf16[1280,3840]{1,0:T(8,128)(2,1)} %get-tuple-element.37, ...), custom_call_target="tpu_custom_call" | custom-call | tf_op jit(solution)/shard_map/backward/pallas_call | solution.py:878
  1070.4 2.2 multiply_reduce_fusion.2
  1072.6 6.0 multiply_reduce_fusion
  1078.6 1.8 collective-permute-start.4
  1081.4 1.7 add_bitcast_fusion
  1085.1 2.7 copy.34
  1087.8 1.4 slice-done
  1089.5 2.4 copy.35
  (65 shorter events, 8.1 us)
Async XLA Ops:
  7.2 131.0 %all-gather.5.cloned.1.call-start = ((), (), s32[]{:S(2)}) async-start(), calls=%async_computation | async-start | bytes 17408000 | tf_op jit(solution)/shard_map/all_gather | solution.py:722
  11.0 370.0 %all-gather.9.cloned.1.call-start = ((), (), s32[]{:S(2)}) async-start(), calls=%async_computation.2 | async-start | bytes 20889600 | tf_op jit(solution)/shard_map/all_gather | solution.py:722
  11.7 396.2 %all-gather.7.cloned.1.call-start = ((), (), s32[]{:S(2)}) async-start(), calls=%async_computation.1 | async-start | bytes 20889600 | tf_op jit(solution)/shard_map/all_gather | solution.py:722
  12.5 491.4 %all-gather.11.cloned.1.call-start = ((), (), s32[]{:S(2)}) async-start(), calls=%async_computation.3 | async-start | bytes 20889600 | tf_op jit(solution)/shard_map/all_gather | solution.py:722
  144.1 6.5 copy-start
  150.7 21.3 %collective-permute-start = (bf16[1024,256]{1,0:T(8,128)(2,1)S(1)}, bf16[1024,256]{1,0:T(8,128)(2,1)S(1)}, u32[]{:S(2)}, u32[]{:S(2)}) collective-permute-start(bf16[1024,256]{1,0:T(8,128)(2,1)S(1)} %slice_select_fusion), channel_id=1, source_target_pairs={{0,4},{2,6},{1,5},{3,7},{8,12},{10,14},{9,13},{11,15},{16,20},{18,... | collective-permute-start | bytes 1572872 | tf_op jit(solution)/shard_map/ppermute | solution.py:714
  154.2 34.3 %collective-permute-start.1 = (bf16[1024,256]{1,0:T(8,128)(2,1)S(1)}, bf16[1024,256]{1,0:T(8,128)(2,1)S(1)}, u32[]{:S(2)}, u32[]{:S(2)}) collective-permute-start(bf16[1024,256]{1,0:T(8,128)(2,1)S(1)} %slice_select_fusion), channel_id=1, source_target_pairs={{0,2},{2,4},{4,6},{1,3},{3,5},{5,7},{8,10},{10,12},{12,14},{9,11},... | collective-permute-start | bytes 1572872 | tf_op jit(solution)/shard_map/ppermute | solution.py:714
  188.6 24.6 %collective-permute-start.2 = (bf16[2048,256]{1,0:T(8,128)(2,1)S(1)}, bf16[2048,256]{1,0:T(8,128)(2,1)S(1)}, u32[]{:S(2)}, u32[]{:S(2)}) collective-permute-start(bf16[2048,256]{1,0:T(8,128)(2,1)S(1)} %constant_dynamic-update-slice_fusion), channel_id=1, source_target_pairs={{0,1},{1,0},{2,3},{3,2},{4,5},{5,4},{6,7},{7,6},{8,9},{9,8},{10,11... | collective-permute-start | bytes 3145736 | tf_op jit(solution)/shard_map/ppermute | solution.py:718
  255.2 113.8 %collective-permute-start.3 = (bf16[1024,2560]{1,0:T(8,128)(2,1)}, bf16[1024,2560]{1,0:T(8,128)(2,1)}, u32[]{:S(2)}, u32[]{:S(2)}) collective-permute-start(bf16[1024,2560]{1,0:T(8,128)(2,1)} %product.3.refs_1_), channel_id=1, source_target_pairs={{0,1},{1,0},{2,3},{3,2},{4,5},{5,4},{6,7},{7,6},{8,9},{9,8},{10,11... | collective-permute-start | bytes 15728648 | tf_op jit(solution)/shard_map/ppermute | solution.py:718
  504.8 565.6 %copy-start.3 = (bf16[160,1280]{1,0:T(8,128)(2,1)S(1)}, bf16[160,1280]{1,0:T(8,128)(2,1)}, u32[]{:S(2)}) copy-start(bf16[160,1280]{1,0:T(8,128)(2,1)} %param.11) | copy-start | bytes 1228804
  504.8 567.7 %copy-start.1 = (bf16[160,3840]{1,0:T(8,128)(2,1)S(1)}, bf16[160,3840]{1,0:T(8,128)(2,1)}, u32[]{:S(2)}) copy-start(bf16[160,3840]{1,0:T(8,128)(2,1)} %param.14) | copy-start | bytes 3686404
  504.8 567.7 %copy-start.2 = (bf16[160,3840]{1,0:T(8,128)(2,1)S(1)}, bf16[160,3840]{1,0:T(8,128)(2,1)}, u32[]{:S(2)}) copy-start(bf16[160,3840]{1,0:T(8,128)(2,1)} %param.15) | copy-start | bytes 3686404
  1072.6 12.5 %slice-start.2 = ((s8[5242880]{0:T(1024)(128)(4,1)}), s8[4194304]{0:T(1024)(128)(4,1)S(1)}, s32[]{:S(2)}) async-start(s8[5242880]{0:T(1024)(128)(4,1)} %bitcast.26), calls=%async_computation.6 | async-start | bytes 8388608
  1072.6 7.8 copy-start.7
  1072.6 7.8 copy-start.8
  1072.6 8.8 copy-start.4
  1072.6 8.8 copy-start.6
  1072.6 12.5 %slice-start.3 = ((s8[5242880]{0:T(1024)(128)(4,1)}), s8[1048576]{0:T(1024)(128)(4,1)S(1)}, s32[]{:S(2)}) async-start(s8[5242880]{0:T(1024)(128)(4,1)} %bitcast.26), calls=%async_computation.7 | async-start | bytes 2097152
  1078.6 5.3 collective-permute-start.4
  1080.4 2.7 copy-start.5
  1080.4 2.7 copy-start.9
  1080.4 2.7 copy-start.10
  1081.4 2.5 copy-start.11
  1081.4 3.1 copy-start.12
  1085.1 4.1 slice-start
  1085.1 4.4 slice-start.1
Sparse Core Ops, SparseCore 0:
  11.1 127.0 all-gather.4
  139.7 128.5 all-gather.8
  269.9 118.6 all-gather.6
  390.0 113.8 all-gather.10

commit v5 on v4

--- a/solution.py
+++ b/solution.py
@@ -292,6 +292,8 @@
 
 
 class Scatter:
+    add_last = False
+
     @staticmethod
     def shapes(prefix, features, width, count):
         part = features // 4
@@ -351,9 +353,15 @@
 
     def near(self):
         self.wait("arrived")
-        own, place = self.links.block(0), self.links.place
+        own = self.links.block(0)
+        extras = [pl.BlockSpec((self.part, self.bn), lambda i, j: (1, j)), pl.BlockSpec((self.part, self.bn), lambda i, j: (0, j))]
+        self.make_near(1, lambda i: own, [self.ref("got"), self.ref("arrived")], extras)
+
+    def make_near(self, steps, left_block, given, extras):
+        place = self.links.place
         near, total = self.ref("near"), self.total
-        count, size = near.shape[0], near.shape[1]
+        count = near.shape[0]
+        size = self.part // count
         order = piece_order(count)
 
         def keep(outs, cols, results):
@@ -369,12 +377,11 @@
         bm, bn = self.part, self.bn
         left, right = self.pairs[0]
         pltpu.emit_pipeline(
-            products_body("tn", 1, 2, None, 0, keep),
-            grid=(1, right.shape[1] // bn),
-            in_specs=products_specs("tn", [left.shape[0]], bm, bn, lambda i: own, 0)
-            + [pl.BlockSpec((bm, bn), lambda i, j: (1, j)), pl.BlockSpec((bm, bn), lambda i, j: (0, j))],
-            out_specs=[pl.BlockSpec((count, size, bn), lambda i, j: (0, 0, j))],
-        )(left, right, self.ref("got"), self.ref("arrived"), near)
+            products_body("tn", 1, len(given), None, 0, keep),
+            grid=(steps, right.shape[1] // bn),
+            in_specs=products_specs("tn", [left.shape[0]], bm, bn, left_block, 0) + extras,
+            out_specs=[pl.BlockSpec((count, size, bn), lambda i, j: (0, i, j))],
+        )(left, right, *given, near)
 
     def kept(self, k):
         return self.ref(f"mid{k - 1}" if k else "near")
@@ -388,7 +395,7 @@
 
     def add(self, k):
         self.wait(f"recv{k}")
-        if k + 1 == len(self.bits):
+        if k + 1 == len(self.bits) and not self.add_last:
             return
         now, mid = self.kept(k), self.ref(f"mid{k}")
         half, size, bn = mid.shape[0], mid.shape[1], self.bn
@@ -408,10 +415,45 @@
             self.add(later)
 
 
+class ScatterFirst(Scatter):
+    add_last = True
+
+    @staticmethod
+    def shapes(prefix, features, width, count):
+        part = features // 4
+        size = part // count
+        out = {"away": (2 * part, width), "got": (2 * part, width), "near": (count, 2 * size, width)}
+        left = count
+        for k in range(len(bits_of(count))):
+            left //= 2
+            out[f"recv{k}"] = out[f"mid{k}"] = (left, 2 * size, width)
+        out["arrived"] = (size, width)
+        return {prefix + key: jax.ShapeDtypeStruct(shape, LOW) for key, shape in out.items()}
+
+    def near(self):
+        self.wait("got")
+        chip, own = self.links.block(2), self.links.block(0)
+        extras = [pl.BlockSpec((self.part, self.bn), lambda i, j: (i, j))]
+        self.make_near(2, lambda i: chip + i * (own - chip), [self.ref("got")], extras)
+
+    def cross(self):
+        last = self.kept(len(self.bits))
+        size = last.shape[1] // 2
+        self.moving["arrived"] = self.links.send(
+            last.at[0, pl.ds(0, size)], self.ref("arrived"), self.links.chip
+        )
+
+
 def scatter_result(prefix, arrays):
     last = len(bits_of(arrays[prefix + "near"].shape[0])) - 1
     now = arrays[prefix + (f"mid{last - 1}" if last else "near")]
     return now[0].astype(WIDE) + arrays[prefix + f"recv{last}"][0].astype(WIDE)
+
+
+def scatter_first_result(prefix, arrays):
+    size = arrays[prefix + "arrived"].shape[0]
+    last = len(bits_of(arrays[prefix + "near"].shape[0])) - 1
+    return arrays[prefix + f"mid{last}"][0, size:].astype(WIDE) + arrays[prefix + "arrived"].astype(WIDE)
 
 
 def remote_call(kernel, inputs, outputs, scratch, collective_id, name):
@@ -440,11 +482,11 @@
     return kernel
 
 
-def down_start(r, links, *, count):
+def down_start(r, links, total, *, count):
     links.meet([links.core])
-    down = Scatter("d_", r, links, "cotangent", "hidden", r["hidden"].shape[1] // 3, count)
+    down = ScatterFirst("d_", r, links, "cotangent", "hidden", r["hidden"].shape[1] // 3, count, total)
     down.away()
-    down.far()
+    down.near()
     links.close()
 
 
@@ -543,7 +585,7 @@
     third = r["hidden"].shape[1] // 3
     bits = bits_of(count)
     links.meet([links.core, links.chip, links.tp] + [{"ctx": lax.rem(links.place + k, count)} for k in range(1, count)])
-    down = Scatter("d_", r, links, "cotangent", "hidden", third, count, total)
+    down = ScatterFirst("d_", r, links, "cotangent", "hidden", third, count, total)
     gate = Scatter("g_", r, links, "second_low", "gate_back", third, count, total)
     up = Scatter("u_", r, links, "second_low", "up_back", third, count, total)
     out = Scatter("o_", r, links, "middle_low", "attended", width, count, total)
@@ -590,7 +632,7 @@
             {"ctx": lax.rem(place + count - by, count)},
         )
 
-    down.cross()
+    down.halve(0)
     job(
         "nn",
         [(r["cotangent"], r["down_full"])],
@@ -607,10 +649,15 @@
     gate.cross()
     second1 = second(parts[1])
     up.away()
-    down.near()
-    down.halve(0)
+    down.add(0)
+    if len(bits) > 1:
+        down.halve(1)
     up.far()
+    feed1 = feed(1)
     feed0 = feed(0)
+    up.cross()
+    gate.near()
+    gate.halve(0)
     second0.wait_recv()
     second1.wait_recv()
     rows_job(
@@ -620,12 +667,6 @@
         [r["middle_low"], r["grad_attended"]],
         block,
     )
-    feed1 = feed(1)
-    gate.wait("arrived")
-    up.cross()
-    down.add(0)
-    if len(bits) > 1:
-        down.halve(1)
     attend_back(r, rows, heads, min(256, rows))
     windows = []
     for by in range(1, hops + 1):
@@ -636,23 +677,22 @@
             move.start()
 
         windows.append(move)
-    gate.near()
-    gate.halve(0)
     out.away()
-    job("nt", [(r["query_back"], r["small_full"].at[:, pl.ds(0, width)])], [r["share"]], bm=rows, bn=512)
-    share0 = share(0)
     out.far()
-    query.away()
-    feed0.wait_recv()
-    finish_output(0)
-    query.far()
-    up.wait("arrived")
-    out.cross()
-    up.near()
     gate.add(0)
     if len(bits) > 1:
         gate.halve(1)
+    job("nt", [(r["query_back"], r["small_full"].at[:, pl.ds(0, width)])], [r["share"]], bm=rows, bn=512)
+    share0 = share(0)
+    up.near()
     up.halve(0)
+    out.cross()
+    query.away()
+    query.far()
+    query.cross()
+    if len(bits) > 1:
+        down.rest(1)
+    down.cross()
     for by in range(1, hops + 1):
 
         @pl.when(links.place + by < count)
@@ -667,39 +707,42 @@
         block,
     )
     swap = links.send(r["keyval_own"], r["keyval_other"], links.tp)
-    share1 = share(1)
     out.near()
     out.halve(0)
-    query.cross()
-    feed1.wait_recv()
-    finish_output(1)
-    swap.wait_recv()
-    rows_job(pair_sum, [r["keyval_own"], r["keyval_other"]], [], [r["keyval_back"]], block)
-    keyval.away()
     up.add(0)
     if len(bits) > 1:
         up.halve(1)
-    keyval.far()
-    keyval.cross()
+    swap.wait_recv()
+    rows_job(pair_sum, [r["keyval_own"], r["keyval_other"]], [], [r["keyval_back"]], block)
+    share0.wait_recv()
+    finish_source(0)
+    share1 = share(1)
+    feed0.wait_recv()
+    finish_output(0)
     query.near()
     query.halve(0)
+    keyval.away()
+    feed1.wait_recv()
+    finish_output(1)
+    keyval.far()
     out.add(0)
     if len(bits) > 1:
         out.halve(1)
-    share0.wait_recv()
-    finish_source(0)
-    keyval.near()
-    keyval.halve(0)
+    keyval.cross()
     query.add(0)
     if len(bits) > 1:
         query.halve(1)
-    share1.wait_recv()
-    finish_source(1)
+    keyval.near()
+    keyval.halve(0)
     keyval.add(0)
     if len(bits) > 1:
         keyval.halve(1)
-        for each in (down, gate, up, out, query, keyval):
+    share1.wait_recv()
+    finish_source(1)
+    if len(bits) > 1:
+        for each in (gate, up, out, query, keyval):
             each.rest(1)
+    down.wait("arrived")
     for by in range(1, hops + 1):
 
         @pl.when(links.place >= by)
@@ -813,7 +856,8 @@
         "output": (rows, features),
     }
     shapes = {key: jax.ShapeDtypeStruct(shape, LOW) for key, shape in plain.items()}
-    for prefix, each in (("d_", units), ("g_", units), ("u_", units), ("o_", width), ("q_", width), ("k_", 2 * HD)):
+    shapes |= ScatterFirst.shapes("d_", features, units, count)
+    for prefix, each in (("g_", units), ("u_", units), ("o_", width), ("q_", width), ("k_", 2 * HD)):
         shapes |= Scatter.shapes(prefix, features, each, count)
     done = dict(
         cotangent=cotangent,
@@ -850,21 +894,21 @@
             keys += [f"{prefix}recv{k}"] + ([f"{prefix}mid{k}"] if k < late else [])
         return keys
 
-    reads, writes = ["cotangent", "hidden"], stage("d_", "away", "got", "far")
+    reads, writes = ["cotangent", "hidden"], stage("d_", "away", "got", "near")
     call = remote_call(
-        by_name(functools.partial(down_start, count=count), reads, writes, 0),
+        by_name(functools.partial(down_start, count=count), reads, writes, 1),
         reads,
         [shapes[key] for key in writes],
-        [],
+        [total],
         0,
         "down_start",
     )
     done |= zip(writes, call(*[done[key] for key in reads]))
 
-    reads = stage("d_", "got", "far") + ["cotangent", "hidden", "down_full", "gate_full", "up_full", "small_full"]
+    reads = ["d_near", "cotangent", "hidden", "down_full", "gate_full", "up_full", "small_full"]
     reads += ["to_gate", "to_up", "first_low", "second_low", "middle", "tokens", "first_inverse", "second_inverse"]
     reads += ["gain_one", "gain_two", "attended", "queries", "window", "probs"]
-    writes = list(plain) + stage("d_", "arrived", "near") + halving("d_", 0, late + 1)
+    writes = list(plain) + ["d_arrived"] + halving("d_", 0, late + 1) + [f"d_mid{late}"]
     for prefix in ("g_", "u_", "o_", "q_", "k_"):
         writes += stage(prefix, "away", "got", "far", "arrived", "near") + halving(prefix, 0, late + 1)
     call = remote_call(
@@ -876,8 +920,9 @@
         "backward",
     )
     done |= zip(writes, call(*[done[key] for key in reads]))
-    down_grad, gate_grad, up_grad, out_grad, query_grad, keyval_grad = (
-        scatter_result(prefix, done) for prefix in ("d_", "g_", "u_", "o_", "q_", "k_")
+    down_grad = scatter_first_result("d_", done)
+    gate_grad, up_grad, out_grad, query_grad, keyval_grad = (
+        scatter_result(prefix, done) for prefix in ("g_", "u_", "o_", "q_", "k_")
     )
 
     def row_sum(weight, grad):

time: 1110 us -> 1080 us (0.973)
  Pallas kernels: 726 us -> 707 us
    pallas_call x2, Pallas kernels: 611 us -> 591 us  [on_device(): done |= zip(writes, call(*[done[key] for key in reads]))]
  transfers between devices with their start and end apart: 9 -> 9, of which waited for: 6 -> 7; matrix products, arithmetic and copies ran while one was open for 3% -> 3% of each run, Pallas kernels for 15% -> 16%
where the time goes in v5:
time: 1080 us; the launch traced here: 1070 us
  Pallas kernels  707 us (65%)
  waiting for transfers between devices  284 us (26%)
  other arithmetic  25.9 us (2%)
  matrix products  18.4 us (2%)
  between operations  14.2 us (1%)
    pallas_call x2, Pallas kernels, on_device(): done |= zip(writes, call(*[done[key] for key in reads]))  591 us
    all_gather x4, waiting for transfers between devices, gathered(): return lax.all_gather(shard, ('fsdp', 'ctx'), axis=0, tiled=True)  126 us
    ppermute x3, waiting for transfers between devices, swap_tp(): return lax.ppermute(array, 'tp', [(0, 1), (1, 0)])  124 us
    pallas_call x3, Pallas kernels, product(): pl.pallas_call(products_body(kind, 1, len(extras), finish, sub, keep_bloc...  74.9 us
    ppermute x2, waiting for transfers between devices, from_place(): lax.ppermute(array, 'ctx', [(i, i + by) for i in range(count) if i + by <...  31.7 us
    pallas_call x1, Pallas kernels, attend(): pl.pallas_call(functools.partial(attend_kernel, heads=heads, hops=hops, r...  28.6 us
  transfers between devices with their start and end apart: 9, of which 7 were waited for; matrix products, arithmetic and copies ran while one was open for 3% of the time, Pallas kernels for 16%

profile of v5, /device:TPU:0, one launch (start us, length us, event | category | flops | bytes accessed | tf_op | source)
XLA Modules:
  0.0 1070.1 jit_solution(5797617178008231316)
XLA Ops:
  8.7 2.3 fusion.13
  13.0 3.6 fusion
  16.6 121.5 %all-gather.5.cloned.1.call-done.refs_1_.refs_6_ = bf16[2560,3200]{1,0:T(8,128)(2,1)} async-done(((bf16[160,3200]{1,0:T(8,128)(2,1)}), bf16[2560,3200]{1,0:T(8,128)(2,1)}) %all-gather.5.cloned.1.call-update) | async-done | bytes 16384016 | tf_op jit(solution)/shard_map/all_gather | solution.py:765
  138.2 1.2 convert_add_fusion.1
  140.4 3.7 fusion.2.refs_9_
  144.1 6.5 fusion.10
  150.7 3.5 collective-permute-start
  154.2 2.6 collective-permute-start.1
  156.8 15.2 %collective-permute-done = bf16[1024,256]{1,0:T(8,128)(2,1)S(1)} collective-permute-done((bf16[1024,256]{1,0:T(8,128)(2,1)S(1)}, bf16[1024,256]{1,0:T(8,128)(2,1)S(1)}, u32[]{:S(2)}, u32[]{:S(2)}) %collective-permute-start) | collective-permute-done | bytes 524320 | tf_op jit(solution)/shard_map/ppermute | solution.py:757
  172.0 16.5 %collective-permute-done.1 = bf16[1024,256]{1,0:T(8,128)(2,1)S(1)} collective-permute-done((bf16[1024,256]{1,0:T(8,128)(2,1)S(1)}, bf16[1024,256]{1,0:T(8,128)(2,1)S(1)}, u32[]{:S(2)}, u32[]{:S(2)}) %collective-permute-start.1) | collective-permute-done | bytes 524320 | tf_op jit(solution)/shard_map/ppermute | solution.py:757
  188.6 1.5 collective-permute-start.2
  190.1 11.9 %multiply_convert_fusion.q_ref.refs_18_ = bf16[1024,1280]{1,0:T(8,128)(2,1)} fusion(bf16[1024,2560]{1,0:T(8,128)(2,1)} %copy-done, bf16[2560,3200]{1,0:T(8,128)(2,1)} %all-gather.5.cloned.1.call-done.refs_1_.refs_6_), kind=kOutput, calls=%fused_computation.7 | convolution fusion | flops 6713507840 | bytes 14417920 | tf_op jit(solution)/shard_map/dot_general | solution.py:22
  202.0 11.2 %collective-permute-done.2 = bf16[2048,256]{1,0:T(8,128)(2,1)S(1)} collective-permute-done((bf16[2048,256]{1,0:T(8,128)(2,1)S(1)}, bf16[2048,256]{1,0:T(8,128)(2,1)S(1)}, u32[]{:S(2)}, u32[]{:S(2)}) %collective-permute-start.2) | collective-permute-done | bytes 1048608 | tf_op jit(solution)/shard_map/ppermute | solution.py:761
  213.3 1.9 pad_maximum_fusion.win_ref.refs_19_
  215.2 28.6 %attend.1 = (bf16[1024,1280]{1,0:T(8,128)(2,1)}, bf16[5,1024,2304]{2,1,0:T(8,128)(2,1)}) custom-call(s32[1]{0:T(128)} %bitcast.place_ref, bf16[1024,1280]{1,0:T(8,128)(2,1)} %multiply_convert_fusion.q_ref.refs_18_, bf16[3072,512]{1,0:T(8,128)(2,1)} %pad_maximum_fusion.win_ref.refs_19_), custom_call_target="tpu_custom_call" | custom-call | tf_op jit(solution)/shard_map/attend/pallas_call | solution.py:66
  243.8 11.4 %product.3.refs_1_ = bf16[1024,2560]{1,0:T(8,128)(2,1)} custom-call(bf16[1024,1280]{1,0:T(8,128)(2,1)} %get-tuple-element.33.refs_0_.refs_17_, bf16[2560,3200]{1,0:T(8,128)(2,1)} %all-gather.5.cloned.1.call-done.refs_1_.refs_6_), custom_call_target="tpu_custom_call" | custom-call | tf_op jit(solution)/shard_map/product/pallas_call | solution.py:133
  255.2 1.5 collective-permute-start.3
  256.7 112.4 %collective-permute-done.3.refs_2_ = bf16[1024,2560]{1,0:T(8,128)(2,1)} collective-permute-done((bf16[1024,2560]{1,0:T(8,128)(2,1)}, bf16[1024,2560]{1,0:T(8,128)(2,1)}, u32[]{:S(2)}, u32[]{:S(2)}) %collective-permute-start.3) | collective-permute-done | bytes 5242912 | tf_op jit(solution)/shard_map/ppermute | solution.py:761
  369.0 12.0 %by_rows.1 = (bf16[1024,2560]{1,0:T(8,128)(2,1)}, bf16[1024,2560]{1,0:T(8,128)(2,1)}, f32[1024,128]{1,0:T(8,128)}) custom-call(bf16[1024,2560]{1,0:T(8,128)(2,1)} %refs_12_.1, bf16[1024,2560]{1,0:T(8,128)(2,1)} %product.3.refs_1_, bf16[1024,2560]{1,0:T(8,128)(2,1)} %collective-permute-done.3.refs_2_, f32[1,2560]{1,0:T(1,128)} %get-tuple-element.68.refs_3_.refs_16_), custom_call_target="tpu_custom_call" | custom-call | tf_op jit(solution)/shard_map/by_rows/pallas_call | solution.py:149
  381.0 26.9 %product.4.refs_2_ = f32[1024,3840]{1,0:T(8,128)} custom-call(bf16[1024,2560]{1,0:T(8,128)(2,1)} %get-tuple-element.34.refs_0_.refs_10_, bf16[2560,3840]{1,0:T(8,128)(2,1)} %all-gather.9.cloned.1.call-done.refs_1_.refs_4_), custom_call_target="tpu_custom_call" | custom-call | tf_op jit(solution)/shard_map/product/pallas_call | solution.py:133
  408.0 36.5 %product.5 = (bf16[1024,3840]{1,0:T(8,128)(2,1)}, bf16[1024,3840]{1,0:T(8,128)(2,1)}, bf16[1024,3840]{1,0:T(8,128)(2,1)}) custom-call(bf16[1024,2560]{1,0:T(8,128)(2,1)} %get-tuple-element.34.refs_0_.refs_10_, bf16[2560,3840]{1,0:T(8,128)(2,1)} %all-gather.7.cloned.1.call-done.refs_1_.refs_5_, f32[1024,3840]{1,0:T(8,128)} %product.4.refs_2_), custom_call_target="tpu_custom_call" | custom-call | tf_op jit(solution)/shard_map/product/pallas_call | solution.py:133
  444.5 53.6 %down_start.1 = (bf16[1280,3840]{1,0:T(8,128)(2,1)}, bf16[1280,3840]{1,0:T(8,128)(2,1)}, bf16[4,320,3840]{2,1,0:T(8,128)(2,1)}) custom-call(bf16[1024,2560]{1,0:T(8,128)(2,1)} %refs_1_.1, bf16[1024,3840]{1,0:T(8,128)(2,1)} %get-tuple-element.35.refs_1_.refs_2_), custom_call_target="tpu_custom_call" | custom-call | tf_op jit(solution)/shard_map/down_start/pallas_call | solution.py:906
  498.1 4.2 all-gather.11.cloned.1.call-done.refs_3_
  502.3 1.0 broadcast_in_dim.2.refs_13_
  503.3 537.9 %backward.1 = (bf16[1024,3840]{1,0:T(8,128)(2,1)}, bf16[1024,3840]{1,0:T(8,128)(2,1)}, bf16[1024,2560]{1,0:T(8,128)(2,1)}, bf16[1024,2560]{1,0:T(8,128)(2,1)}, b...) custom-call(bf16[4,320,3840]{2,1,0:T(8,128)(2,1)} %get-tuple-element, ...), custom_call_target="tpu_custom_call" | custom-call | tf_op jit(solution)/shard_map/backward/pallas_call | solution.py:922
  1041.2 2.2 multiply_reduce_fusion.2
  1043.4 3.7 multiply_reduce_fusion.1
  1047.6 4.2 multiply_reduce_fusion
  1051.8 1.3 collective-permute-start.4
  1056.7 2.7 copy.34
  1059.3 1.4 slice-done
  1061.0 2.4 copy.35
  (67 shorter events, 9.1 us)
Async XLA Ops:
  7.2 131.0 %all-gather.5.cloned.1.call-start = ((), (), s32[]{:S(2)}) async-start(), calls=%async_computation | async-start | bytes 17408000 | tf_op jit(solution)/shard_map/all_gather | solution.py:765
  11.0 370.0 %all-gather.9.cloned.1.call-start = ((), (), s32[]{:S(2)}) async-start(), calls=%async_computation.2 | async-start | bytes 20889600 | tf_op jit(solution)/shard_map/all_gather | solution.py:765
  11.7 396.2 %all-gather.7.cloned.1.call-start = ((), (), s32[]{:S(2)}) async-start(), calls=%async_computation.1 | async-start | bytes 20889600 | tf_op jit(solution)/shard_map/all_gather | solution.py:765
  12.5 489.9 %all-gather.11.cloned.1.call-start = ((), (), s32[]{:S(2)}) async-start(), calls=%async_computation.3 | async-start | bytes 20889600 | tf_op jit(solution)/shard_map/all_gather | solution.py:765
  144.1 6.5 copy-start
  150.7 21.3 %collective-permute-start = (bf16[1024,256]{1,0:T(8,128)(2,1)S(1)}, bf16[1024,256]{1,0:T(8,128)(2,1)S(1)}, u32[]{:S(2)}, u32[]{:S(2)}) collective-permute-start(bf16[1024,256]{1,0:T(8,128)(2,1)S(1)} %slice_select_fusion), channel_id=1, source_target_pairs={{0,4},{2,6},{1,5},{3,7},{8,12},{10,14},{9,13},{11,15},{16,20},{18,... | collective-permute-start | bytes 1572872 | tf_op jit(solution)/shard_map/ppermute | solution.py:757
  154.2 34.3 %collective-permute-start.1 = (bf16[1024,256]{1,0:T(8,128)(2,1)S(1)}, bf16[1024,256]{1,0:T(8,128)(2,1)S(1)}, u32[]{:S(2)}, u32[]{:S(2)}) collective-permute-start(bf16[1024,256]{1,0:T(8,128)(2,1)S(1)} %slice_select_fusion), channel_id=1, source_target_pairs={{0,2},{2,4},{4,6},{1,3},{3,5},{5,7},{8,10},{10,12},{12,14},{9,11},... | collective-permute-start | bytes 1572872 | tf_op jit(solution)/shard_map/ppermute | solution.py:757
  188.6 24.6 %collective-permute-start.2 = (bf16[2048,256]{1,0:T(8,128)(2,1)S(1)}, bf16[2048,256]{1,0:T(8,128)(2,1)S(1)}, u32[]{:S(2)}, u32[]{:S(2)}) collective-permute-start(bf16[2048,256]{1,0:T(8,128)(2,1)S(1)} %constant_dynamic-update-slice_fusion), channel_id=1, source_target_pairs={{0,1},{1,0},{2,3},{3,2},{4,5},{5,4},{6,7},{7,6},{8,9},{9,8},{10,11... | collective-permute-start | bytes 3145736 | tf_op jit(solution)/shard_map/ppermute | solution.py:761
  255.2 113.8 %collective-permute-start.3 = (bf16[1024,2560]{1,0:T(8,128)(2,1)}, bf16[1024,2560]{1,0:T(8,128)(2,1)}, u32[]{:S(2)}, u32[]{:S(2)}) collective-permute-start(bf16[1024,2560]{1,0:T(8,128)(2,1)} %product.3.refs_1_), channel_id=1, source_target_pairs={{0,1},{1,0},{2,3},{3,2},{4,5},{5,4},{6,7},{7,6},{8,9},{9,8},{10,11... | collective-permute-start | bytes 15728648 | tf_op jit(solution)/shard_map/ppermute | solution.py:761
  503.3 537.9 %copy-start.3 = (bf16[160,1280]{1,0:T(8,128)(2,1)S(1)}, bf16[160,1280]{1,0:T(8,128)(2,1)}, u32[]{:S(2)}) copy-start(bf16[160,1280]{1,0:T(8,128)(2,1)} %param.11) | copy-start | bytes 1228804
  503.3 540.1 %copy-start.1 = (bf16[160,3840]{1,0:T(8,128)(2,1)S(1)}, bf16[160,3840]{1,0:T(8,128)(2,1)}, u32[]{:S(2)}) copy-start(bf16[160,3840]{1,0:T(8,128)(2,1)} %param.14) | copy-start | bytes 3686404
  1043.4 3.8 copy-start.2
  1043.4 3.8 copy-start.4
  1043.4 3.8 copy-start.5
  1043.4 4.1 copy-start.7
  1047.1 9.5 slice-start.2
  1047.5 5.6 copy-start.8
  1047.5 5.6 copy-start.9
  1047.5 6.5 copy-start.6
  1047.5 6.5 copy-start.10
  1047.5 6.5 copy-start.11
  1047.6 7.9 copy-start.12
  1047.6 8.5 copy-start.13
  1047.6 9.1 slice-start.3
  1051.8 3.6 collective-permute-start.4
  1056.6 4.1 slice-start
  1056.7 4.4 slice-start.1
Sparse Core Ops, SparseCore 0:
  11.1 127.0 all-gather.4
  139.7 128.5 all-gather.8
  269.9 118.6 all-gather.6
  390.0 112.3 all-gather.10

commit v6 on v5

--- a/solution.py
+++ b/solution.py
@@ -632,7 +632,6 @@
             {"ctx": lax.rem(place + count - by, count)},
         )
 
-    down.halve(0)
     job(
         "nn",
         [(r["cotangent"], r["down_full"])],
@@ -644,6 +643,7 @@
         finish=finish_hidden,
     )
     gate.away()
+    down.halve(0)
     second0 = second(parts[0])
     gate.far()
     gate.cross()
@@ -677,22 +677,21 @@
             move.start()
 
         windows.append(move)
-    out.away()
-    out.far()
     gate.add(0)
     if len(bits) > 1:
         gate.halve(1)
     job("nt", [(r["query_back"], r["small_full"].at[:, pl.ds(0, width)])], [r["share"]], bm=rows, bn=512)
-    share0 = share(0)
-    up.near()
-    up.halve(0)
-    out.cross()
+    share1 = share(1)
+    feed1.wait_recv()
+    finish_output(1)
+    out.away()
     query.away()
     query.far()
     query.cross()
-    if len(bits) > 1:
-        down.rest(1)
-    down.cross()
+    up.near()
+    up.halve(0)
+    out.far()
+    out.cross()
     for by in range(1, hops + 1):
 
         @pl.when(links.place + by < count)
@@ -707,38 +706,39 @@
         block,
     )
     swap = links.send(r["keyval_own"], r["keyval_other"], links.tp)
-    out.near()
-    out.halve(0)
+    query.near()
+    query.halve(0)
+    share0 = share(0)
+    swap.wait_recv()
+    rows_job(pair_sum, [r["keyval_own"], r["keyval_other"]], [], [r["keyval_back"]], block)
     up.add(0)
     if len(bits) > 1:
         up.halve(1)
-    swap.wait_recv()
-    rows_job(pair_sum, [r["keyval_own"], r["keyval_other"]], [], [r["keyval_back"]], block)
-    share0.wait_recv()
-    finish_source(0)
-    share1 = share(1)
-    feed0.wait_recv()
-    finish_output(0)
-    query.near()
-    query.halve(0)
+    out.near()
+    out.halve(0)
     keyval.away()
-    feed1.wait_recv()
-    finish_output(1)
     keyval.far()
+    keyval.cross()
+    share1.wait_recv()
+    finish_source(1)
+    query.add(0)
+    if len(bits) > 1:
+        query.halve(1)
+    if len(bits) > 1:
+        down.rest(1)
+    down.cross()
+    keyval.near()
+    keyval.halve(0)
     out.add(0)
     if len(bits) > 1:
         out.halve(1)
-    keyval.cross()
-    query.add(0)
-    if len(bits) > 1:
-        query.halve(1)
-    keyval.near()
-    keyval.halve(0)
+    share0.wait_recv()
+    finish_source(0)
     keyval.add(0)
     if len(bits) > 1:
         keyval.halve(1)
-    share1.wait_recv()
-    finish_source(1)
+    feed0.wait_recv()
+    finish_output(0)
     if len(bits) > 1:
         for each in (gate, up, out, query, keyval):
             each.rest(1)
@@ -787,7 +787,8 @@
     place = lax.axis_index("ctx")
     block = min(256, rows)
 
-    gains = jnp.pad(jnp.stack([first_gain, second_gain], axis=1), ((0, 0), (0, 126)))
+    spare = units - 2 * width - 2 * HD - 2
+    gains = jnp.pad(jnp.stack([first_gain, second_gain], axis=1), ((0, 0), (0, spare)))
     small_full = gathered(jnp.concatenate([query_weight, out_weight, keyval_weight, gains], axis=1))
     gate_full = gathered(gate_weight)
     up_full = gathered(up_weight)

time: 1080 us -> 1110 us (1.028)
  Pallas kernels: 707 us -> 745 us
  waiting for transfers between devices: 284 us -> 266 us
    pallas_call x2, Pallas kernels: 591 us -> 630 us  [on_device(): done |= zip(writes, call(*[done[key] for key in reads]))]
    all_gather x4, waiting for transfers between devices: 126 us -> 112 us  [gathered(): return lax.all_gather(shard, ('fsdp', 'ctx'), axis=0, tiled=True)]
  transfers between devices with their start and end apart: 9 -> 9, of which waited for: 7 -> 6; matrix products, arithmetic and copies ran while one was open for 3% -> 3% of each run, Pallas kernels for 16% -> 15%
where the time goes in v6:
time: 1110 us; the launch traced here: 1090 us
  Pallas kernels  745 us (67%)
  waiting for transfers between devices  266 us (24%)
  other arithmetic  26.1 us (2%)
  matrix products  18.5 us (2%)
  between operations  14.2 us (1%)
  starting transfers between devices  13 us (1%)
    pallas_call x2, Pallas kernels, on_device(): done |= zip(writes, call(*[done[key] for key in reads]))  630 us
    ppermute x3, waiting for transfers between devices, swap_tp(): return lax.ppermute(array, 'tp', [(0, 1), (1, 0)])  122 us
    all_gather x4, waiting for transfers between devices, gathered(): return lax.all_gather(shard, ('fsdp', 'ctx'), axis=0, tiled=True)  112 us
    pallas_call x3, Pallas kernels, product(): pl.pallas_call(products_body(kind, 1, len(extras), finish, sub, keep_bloc...  74.8 us
    ppermute x2, waiting for transfers between devices, from_place(): lax.ppermute(array, 'ctx', [(i, i + by) for i in range(count) if i + by <...  30.4 us
    pallas_call x1, Pallas kernels, attend(): pl.pallas_call(functools.partial(attend_kernel, heads=heads, hops=hops, r...  28.6 us
  transfers between devices with their start and end apart: 9, of which 6 were waited for; matrix products, arithmetic and copies ran while one was open for 3% of the time, Pallas kernels for 15%

profile of v6, /device:TPU:0, one launch (start us, length us, event | category | flops | bytes accessed | tf_op | source)
XLA Modules:
  0.0 1092.4 jit_solution(7169771744069777767)
XLA Ops:
  8.7 2.3 fusion.13
  13.1 3.6 fusion
  16.7 105.3 %all-gather.5.cloned.1.call-done.refs_1_.refs_6_ = bf16[2560,3840]{1,0:T(8,128)(2,1)} async-done(((bf16[160,3840]{1,0:T(8,128)(2,1)}), bf16[2560,3840]{1,0:T(8,128)(2,1)}) %all-gather.5.cloned.1.call-update) | async-done | bytes 19660816 | tf_op jit(solution)/shard_map/all_gather | solution.py:765
  122.1 1.2 convert_add_fusion.1
  124.3 3.7 fusion.2.refs_9_
  128.0 6.5 fusion.10
  134.7 4.3 collective-permute-start
  139.0 3.6 collective-permute-start.1
  142.6 14.3 %collective-permute-done = bf16[1024,256]{1,0:T(8,128)(2,1)S(1)} collective-permute-done((bf16[1024,256]{1,0:T(8,128)(2,1)S(1)}, bf16[1024,256]{1,0:T(8,128)(2,1)S(1)}, u32[]{:S(2)}, u32[]{:S(2)}) %collective-permute-start) | collective-permute-done | bytes 524320 | tf_op jit(solution)/shard_map/ppermute | solution.py:757
  156.9 16.1 %collective-permute-done.1 = bf16[1024,256]{1,0:T(8,128)(2,1)S(1)} collective-permute-done((bf16[1024,256]{1,0:T(8,128)(2,1)S(1)}, bf16[1024,256]{1,0:T(8,128)(2,1)S(1)}, u32[]{:S(2)}, u32[]{:S(2)}) %collective-permute-start.1) | collective-permute-done | bytes 524320 | tf_op jit(solution)/shard_map/ppermute | solution.py:757
  173.1 1.5 collective-permute-start.2
  174.6 12.0 %multiply_convert_fusion.q_ref.refs_18_ = bf16[1024,1280]{1,0:T(8,128)(2,1)} fusion(bf16[1024,2560]{1,0:T(8,128)(2,1)} %copy-done, bf16[2560,3840]{1,0:T(8,128)(2,1)} %all-gather.5.cloned.1.call-done.refs_1_.refs_6_), kind=kOutput, calls=%fused_computation.7 | convolution fusion | flops 6713507840 | bytes 14417920 | tf_op jit(solution)/shard_map/dot_general | solution.py:22
  186.6 10.4 collective-permute-done.2
  197.1 1.9 pad_maximum_fusion.win_ref.refs_19_
  198.9 28.6 %attend.1 = (bf16[1024,1280]{1,0:T(8,128)(2,1)}, bf16[5,1024,2304]{2,1,0:T(8,128)(2,1)}) custom-call(s32[1]{0:T(128)} %bitcast.place_ref, bf16[1024,1280]{1,0:T(8,128)(2,1)} %multiply_convert_fusion.q_ref.refs_18_, bf16[3072,512]{1,0:T(8,128)(2,1)} %pad_maximum_fusion.win_ref.refs_19_), custom_call_target="tpu_custom_call" | custom-call | tf_op jit(solution)/shard_map/attend/pallas_call | solution.py:66
  227.5 11.3 %product.3.refs_1_ = bf16[1024,2560]{1,0:T(8,128)(2,1)} custom-call(bf16[1024,1280]{1,0:T(8,128)(2,1)} %get-tuple-element.33.refs_0_.refs_17_, bf16[2560,3840]{1,0:T(8,128)(2,1)} %all-gather.5.cloned.1.call-done.refs_1_.refs_6_), custom_call_target="tpu_custom_call" | custom-call | tf_op jit(solution)/shard_map/product/pallas_call | solution.py:133
  238.8 1.5 collective-permute-start.3
  240.3 111.7 %collective-permute-done.3.refs_2_ = bf16[1024,2560]{1,0:T(8,128)(2,1)} collective-permute-done((bf16[1024,2560]{1,0:T(8,128)(2,1)}, bf16[1024,2560]{1,0:T(8,128)(2,1)}, u32[]{:S(2)}, u32[]{:S(2)}) %collective-permute-start.3) | collective-permute-done | bytes 5242912 | tf_op jit(solution)/shard_map/ppermute | solution.py:761
  352.0 11.9 %by_rows.1 = (bf16[1024,2560]{1,0:T(8,128)(2,1)}, bf16[1024,2560]{1,0:T(8,128)(2,1)}, f32[1024,128]{1,0:T(8,128)}) custom-call(bf16[1024,2560]{1,0:T(8,128)(2,1)} %refs_12_.1, bf16[1024,2560]{1,0:T(8,128)(2,1)} %product.3.refs_1_, bf16[1024,2560]{1,0:T(8,128)(2,1)} %collective-permute-done.3.refs_2_, f32[1,2560]{1,0:T(1,128)} %get-tuple-element.68.refs_3_.refs_16_), custom_call_target="tpu_custom_call" | custom-call | tf_op jit(solution)/shard_map/by_rows/pallas_call | solution.py:149
  363.9 26.9 %product.4.refs_2_ = f32[1024,3840]{1,0:T(8,128)} custom-call(bf16[1024,2560]{1,0:T(8,128)(2,1)} %get-tuple-element.34.refs_0_.refs_10_, bf16[2560,3840]{1,0:T(8,128)(2,1)} %all-gather.9.cloned.1.call-done.refs_1_.refs_4_), custom_call_target="tpu_custom_call" | custom-call | tf_op jit(solution)/shard_map/product/pallas_call | solution.py:133
  390.8 36.6 %product.5 = (bf16[1024,3840]{1,0:T(8,128)(2,1)}, bf16[1024,3840]{1,0:T(8,128)(2,1)}, bf16[1024,3840]{1,0:T(8,128)(2,1)}) custom-call(bf16[1024,2560]{1,0:T(8,128)(2,1)} %get-tuple-element.34.refs_0_.refs_10_, bf16[2560,3840]{1,0:T(8,128)(2,1)} %all-gather.7.cloned.1.call-done.refs_1_.refs_5_, f32[1024,3840]{1,0:T(8,128)} %product.4.refs_2_), custom_call_target="tpu_custom_call" | custom-call | tf_op jit(solution)/shard_map/product/pallas_call | solution.py:133
  427.5 53.3 %down_start.1 = (bf16[1280,3840]{1,0:T(8,128)(2,1)}, bf16[1280,3840]{1,0:T(8,128)(2,1)}, bf16[4,320,3840]{2,1,0:T(8,128)(2,1)}) custom-call(bf16[1024,2560]{1,0:T(8,128)(2,1)} %refs_1_.1, bf16[1024,3840]{1,0:T(8,128)(2,1)} %get-tuple-element.35.refs_1_.refs_2_), custom_call_target="tpu_custom_call" | custom-call | tf_op jit(solution)/shard_map/down_start/pallas_call | solution.py:907
  480.7 6.8 all-gather.11.cloned.1.call-done.refs_3_
  487.5 1.0 broadcast_in_dim.2.refs_13_
  488.5 576.8 %backward.1 = (bf16[1024,3840]{1,0:T(8,128)(2,1)}, bf16[1024,3840]{1,0:T(8,128)(2,1)}, bf16[1024,2560]{1,0:T(8,128)(2,1)}, bf16[1024,2560]{1,0:T(8,128)(2,1)}, b...) custom-call(bf16[4,320,3840]{2,1,0:T(8,128)(2,1)} %get-tuple-element, ...), custom_call_target="tpu_custom_call" | custom-call | tf_op jit(solution)/shard_map/backward/pallas_call | solution.py:923
  1065.4 2.3 multiply_reduce_fusion.2
  1067.7 3.7 multiply_reduce_fusion.1
  1071.8 4.2 multiply_reduce_fusion
  1076.0 1.9 collective-permute-start.4
  1077.9 1.0 add_bitcast_fusion.2
  1080.9 2.4 copy.34
  1083.3 2.4 copy.35
  (67 shorter events, 7.2 us)
Async XLA Ops:
  7.2 114.9 %all-gather.5.cloned.1.call-start = ((), (), s32[]{:S(2)}) async-start(), calls=%async_computation | async-start | bytes 20889600 | tf_op jit(solution)/shard_map/all_gather | solution.py:765
  11.1 352.8 %all-gather.9.cloned.1.call-start = ((), (), s32[]{:S(2)}) async-start(), calls=%async_computation.2 | async-start | bytes 20889600 | tf_op jit(solution)/shard_map/all_gather | solution.py:765
  11.8 379.0 %all-gather.7.cloned.1.call-start = ((), (), s32[]{:S(2)}) async-start(), calls=%async_computation.1 | async-start | bytes 20889600 | tf_op jit(solution)/shard_map/all_gather | solution.py:765
  12.5 475.0 %all-gather.11.cloned.1.call-start = ((), (), s32[]{:S(2)}) async-start(), calls=%async_computation.3 | async-start | bytes 20889600 | tf_op jit(solution)/shard_map/all_gather | solution.py:765
  128.0 6.6 copy-start
  134.7 22.2 %collective-permute-start = (bf16[1024,256]{1,0:T(8,128)(2,1)S(1)}, bf16[1024,256]{1,0:T(8,128)(2,1)S(1)}, u32[]{:S(2)}, u32[]{:S(2)}) collective-permute-start(bf16[1024,256]{1,0:T(8,128)(2,1)S(1)} %slice_select_fusion), channel_id=1, source_target_pairs={{0,4},{2,6},{1,5},{3,7},{8,12},{10,14},{9,13},{11,15},{16,20},{18,... | collective-permute-start | bytes 1572872 | tf_op jit(solution)/shard_map/ppermute | solution.py:757
  139.0 34.0 %collective-permute-start.1 = (bf16[1024,256]{1,0:T(8,128)(2,1)S(1)}, bf16[1024,256]{1,0:T(8,128)(2,1)S(1)}, u32[]{:S(2)}, u32[]{:S(2)}) collective-permute-start(bf16[1024,256]{1,0:T(8,128)(2,1)S(1)} %slice_select_fusion), channel_id=1, source_target_pairs={{0,2},{2,4},{4,6},{1,3},{3,5},{5,7},{8,10},{10,12},{12,14},{9,11},... | collective-permute-start | bytes 1572872 | tf_op jit(solution)/shard_map/ppermute | solution.py:757
  173.1 23.8 %collective-permute-start.2 = (bf16[2048,256]{1,0:T(8,128)(2,1)S(1)}, bf16[2048,256]{1,0:T(8,128)(2,1)S(1)}, u32[]{:S(2)}, u32[]{:S(2)}) collective-permute-start(bf16[2048,256]{1,0:T(8,128)(2,1)S(1)} %constant_dynamic-update-slice_fusion), channel_id=1, source_target_pairs={{0,1},{1,0},{2,3},{3,2},{4,5},{5,4},{6,7},{7,6},{8,9},{9,8},{10,11... | collective-permute-start | bytes 3145736 | tf_op jit(solution)/shard_map/ppermute | solution.py:761
  238.8 113.2 %collective-permute-start.3 = (bf16[1024,2560]{1,0:T(8,128)(2,1)}, bf16[1024,2560]{1,0:T(8,128)(2,1)}, u32[]{:S(2)}, u32[]{:S(2)}) collective-permute-start(bf16[1024,2560]{1,0:T(8,128)(2,1)} %product.3.refs_1_), channel_id=1, source_target_pairs={{0,1},{1,0},{2,3},{3,2},{4,5},{5,4},{6,7},{7,6},{8,9},{9,8},{10,11... | collective-permute-start | bytes 15728648 | tf_op jit(solution)/shard_map/ppermute | solution.py:761
  488.5 576.9 %copy-start.3 = (bf16[160,1280]{1,0:T(8,128)(2,1)S(1)}, bf16[160,1280]{1,0:T(8,128)(2,1)}, u32[]{:S(2)}) copy-start(bf16[160,1280]{1,0:T(8,128)(2,1)} %param.11) | copy-start | bytes 1228804
  1065.3 2.3 copy-start.1
  1067.6 3.8 copy-start.2
  1067.6 3.8 copy-start.4
  1067.6 3.8 copy-start.5
  1067.6 4.1 copy-start.7
  1071.4 9.5 slice-start.2
  1071.8 6.2 copy-start.8
  1071.8 6.2 copy-start.9
  1071.8 7.2 copy-start.6
  1071.8 7.2 copy-start.10
  1071.8 7.2 copy-start.11
  1071.8 8.0 copy-start.12
  1071.8 8.6 copy-start.13
  1071.8 9.1 slice-start.3
  1076.0 3.7 collective-permute-start.4
  1078.9 4.4 slice-start
  1080.9 2.4 slice-start.1
Sparse Core Ops, SparseCore 0:
  11.2 110.8 all-gather.4
  123.6 130.3 all-gather.8
  255.6 118.6 all-gather.6
  375.7 111.7 all-gather.10

commit v7 on v5

--- a/solution.py
+++ b/solution.py
@@ -787,7 +787,8 @@
     place = lax.axis_index("ctx")
     block = min(256, rows)
 
-    gains = jnp.pad(jnp.stack([first_gain, second_gain], axis=1), ((0, 0), (0, 126)))
+    spare = units - 2 * width - 2 * HD - 2
+    gains = jnp.pad(jnp.stack([first_gain, second_gain], axis=1), ((0, 0), (0, spare)))
     small_full = gathered(jnp.concatenate([query_weight, out_weight, keyval_weight, gains], axis=1))
     gate_full = gathered(gate_weight)
     up_full = gathered(up_weight)

time: 1080 us -> 1060 us (0.981)
  waiting for transfers between devices: 284 us -> 266 us
    all_gather x4, waiting for transfers between devices: 126 us -> 112 us  [gathered(): return lax.all_gather(shard, ('fsdp', 'ctx'), axis=0, tiled=True)]
  transfers between devices with their start and end apart: 9 -> 9, of which waited for: 7 -> 6; matrix products, arithmetic and copies ran while one was open for 3% -> 3% of each run, Pallas kernels for 16% -> 16%
where the time goes in v7:
time: 1060 us; the launch traced here: 1050 us
  Pallas kernels  705 us (67%)
  waiting for transfers between devices  266 us (25%)
  other arithmetic  26.1 us (2%)
  matrix products  18.5 us (2%)
  between operations  14.2 us (1%)
  starting transfers between devices  13.7 us (1%)
    pallas_call x2, Pallas kernels, on_device(): done |= zip(writes, call(*[done[key] for key in reads]))  590 us
    ppermute x3, waiting for transfers between devices, swap_tp(): return lax.ppermute(array, 'tp', [(0, 1), (1, 0)])  122 us
    all_gather x4, waiting for transfers between devices, gathered(): return lax.all_gather(shard, ('fsdp', 'ctx'), axis=0, tiled=True)  112 us
    pallas_call x3, Pallas kernels, product(): pl.pallas_call(products_body(kind, 1, len(extras), finish, sub, keep_bloc...  74.8 us
    ppermute x2, waiting for transfers between devices, from_place(): lax.ppermute(array, 'ctx', [(i, i + by) for i in range(count) if i + by <...  30.4 us
    pallas_call x1, Pallas kernels, attend(): pl.pallas_call(functools.partial(attend_kernel, heads=heads, hops=hops, r...  28.6 us
  transfers between devices with their start and end apart: 9, of which 6 were waited for; matrix products, arithmetic and copies ran while one was open for 3% of the time, Pallas kernels for 16%

profile of v7, /device:TPU:0, one launch (start us, length us, event | category | flops | bytes accessed | tf_op | source)
XLA Modules:
  0.0 1052.7 jit_solution(15487027472369431145)
XLA Ops:
  8.7 2.3 fusion.13
  13.1 3.6 fusion
  16.7 105.3 %all-gather.5.cloned.1.call-done.refs_1_.refs_6_ = bf16[2560,3840]{1,0:T(8,128)(2,1)} async-done(((bf16[160,3840]{1,0:T(8,128)(2,1)}), bf16[2560,3840]{1,0:T(8,128)(2,1)}) %all-gather.5.cloned.1.call-update) | async-done | bytes 19660816 | tf_op jit(solution)/shard_map/all_gather | solution.py:765
  122.1 1.2 convert_add_fusion.1
  124.3 3.7 fusion.2.refs_9_
  128.0 6.5 fusion.10
  134.7 4.3 collective-permute-start
  139.0 3.6 collective-permute-start.1
  142.6 14.3 %collective-permute-done = bf16[1024,256]{1,0:T(8,128)(2,1)S(1)} collective-permute-done((bf16[1024,256]{1,0:T(8,128)(2,1)S(1)}, bf16[1024,256]{1,0:T(8,128)(2,1)S(1)}, u32[]{:S(2)}, u32[]{:S(2)}) %collective-permute-start) | collective-permute-done | bytes 524320 | tf_op jit(solution)/shard_map/ppermute | solution.py:757
  156.9 16.1 %collective-permute-done.1 = bf16[1024,256]{1,0:T(8,128)(2,1)S(1)} collective-permute-done((bf16[1024,256]{1,0:T(8,128)(2,1)S(1)}, bf16[1024,256]{1,0:T(8,128)(2,1)S(1)}, u32[]{:S(2)}, u32[]{:S(2)}) %collective-permute-start.1) | collective-permute-done | bytes 524320 | tf_op jit(solution)/shard_map/ppermute | solution.py:757
  173.1 1.5 collective-permute-start.2
  174.6 12.0 %multiply_convert_fusion.q_ref.refs_18_ = bf16[1024,1280]{1,0:T(8,128)(2,1)} fusion(bf16[1024,2560]{1,0:T(8,128)(2,1)} %copy-done, bf16[2560,3840]{1,0:T(8,128)(2,1)} %all-gather.5.cloned.1.call-done.refs_1_.refs_6_), kind=kOutput, calls=%fused_computation.7 | convolution fusion | flops 6713507840 | bytes 14417920 | tf_op jit(solution)/shard_map/dot_general | solution.py:22
  186.6 10.4 collective-permute-done.2
  197.1 1.9 pad_maximum_fusion.win_ref.refs_19_
  198.9 28.6 %attend.1 = (bf16[1024,1280]{1,0:T(8,128)(2,1)}, bf16[5,1024,2304]{2,1,0:T(8,128)(2,1)}) custom-call(s32[1]{0:T(128)} %bitcast.place_ref, bf16[1024,1280]{1,0:T(8,128)(2,1)} %multiply_convert_fusion.q_ref.refs_18_, bf16[3072,512]{1,0:T(8,128)(2,1)} %pad_maximum_fusion.win_ref.refs_19_), custom_call_target="tpu_custom_call" | custom-call | tf_op jit(solution)/shard_map/attend/pallas_call | solution.py:66
  227.5 11.3 %product.3.refs_1_ = bf16[1024,2560]{1,0:T(8,128)(2,1)} custom-call(bf16[1024,1280]{1,0:T(8,128)(2,1)} %get-tuple-element.33.refs_0_.refs_17_, bf16[2560,3840]{1,0:T(8,128)(2,1)} %all-gather.5.cloned.1.call-done.refs_1_.refs_6_), custom_call_target="tpu_custom_call" | custom-call | tf_op jit(solution)/shard_map/product/pallas_call | solution.py:133
  238.8 1.5 collective-permute-start.3
  240.3 111.7 %collective-permute-done.3.refs_2_ = bf16[1024,2560]{1,0:T(8,128)(2,1)} collective-permute-done((bf16[1024,2560]{1,0:T(8,128)(2,1)}, bf16[1024,2560]{1,0:T(8,128)(2,1)}, u32[]{:S(2)}, u32[]{:S(2)}) %collective-permute-start.3) | collective-permute-done | bytes 5242912 | tf_op jit(solution)/shard_map/ppermute | solution.py:761
  352.0 11.9 %by_rows.1 = (bf16[1024,2560]{1,0:T(8,128)(2,1)}, bf16[1024,2560]{1,0:T(8,128)(2,1)}, f32[1024,128]{1,0:T(8,128)}) custom-call(bf16[1024,2560]{1,0:T(8,128)(2,1)} %refs_12_.1, bf16[1024,2560]{1,0:T(8,128)(2,1)} %product.3.refs_1_, bf16[1024,2560]{1,0:T(8,128)(2,1)} %collective-permute-done.3.refs_2_, f32[1,2560]{1,0:T(1,128)} %get-tuple-element.68.refs_3_.refs_16_), custom_call_target="tpu_custom_call" | custom-call | tf_op jit(solution)/shard_map/by_rows/pallas_call | solution.py:149
  363.9 26.9 %product.4.refs_2_ = f32[1024,3840]{1,0:T(8,128)} custom-call(bf16[1024,2560]{1,0:T(8,128)(2,1)} %get-tuple-element.34.refs_0_.refs_10_, bf16[2560,3840]{1,0:T(8,128)(2,1)} %all-gather.9.cloned.1.call-done.refs_1_.refs_4_), custom_call_target="tpu_custom_call" | custom-call | tf_op jit(solution)/shard_map/product/pallas_call | solution.py:133
  390.8 36.6 %product.5 = (bf16[1024,3840]{1,0:T(8,128)(2,1)}, bf16[1024,3840]{1,0:T(8,128)(2,1)}, bf16[1024,3840]{1,0:T(8,128)(2,1)}) custom-call(bf16[1024,2560]{1,0:T(8,128)(2,1)} %get-tuple-element.34.refs_0_.refs_10_, bf16[2560,3840]{1,0:T(8,128)(2,1)} %all-gather.7.cloned.1.call-done.refs_1_.refs_5_, f32[1024,3840]{1,0:T(8,128)} %product.4.refs_2_), custom_call_target="tpu_custom_call" | custom-call | tf_op jit(solution)/shard_map/product/pallas_call | solution.py:133
  427.5 53.3 %down_start.1 = (bf16[1280,3840]{1,0:T(8,128)(2,1)}, bf16[1280,3840]{1,0:T(8,128)(2,1)}, bf16[4,320,3840]{2,1,0:T(8,128)(2,1)}) custom-call(bf16[1024,2560]{1,0:T(8,128)(2,1)} %refs_1_.1, bf16[1024,3840]{1,0:T(8,128)(2,1)} %get-tuple-element.35.refs_1_.refs_2_), custom_call_target="tpu_custom_call" | custom-call | tf_op jit(solution)/shard_map/down_start/pallas_call | solution.py:907
  480.7 6.8 all-gather.11.cloned.1.call-done.refs_3_
  487.5 1.0 broadcast_in_dim.2.refs_13_
  488.5 536.4 %backward.1 = (bf16[1024,3840]{1,0:T(8,128)(2,1)}, bf16[1024,3840]{1,0:T(8,128)(2,1)}, bf16[1024,2560]{1,0:T(8,128)(2,1)}, bf16[1024,2560]{1,0:T(8,128)(2,1)}, b...) custom-call(bf16[4,320,3840]{2,1,0:T(8,128)(2,1)} %get-tuple-element, ...), custom_call_target="tpu_custom_call" | custom-call | tf_op jit(solution)/shard_map/backward/pallas_call | solution.py:923
  1025.0 2.3 multiply_reduce_fusion.2
  1027.3 3.7 multiply_reduce_fusion.1
  1031.4 4.2 multiply_reduce_fusion
  1035.6 2.6 collective-permute-start.4
  1038.3 1.0 add_bitcast_fusion.2
  1041.3 2.4 copy.34
  1043.6 2.4 copy.35
  (67 shorter events, 7.2 us)
Async XLA Ops:
  7.2 114.9 %all-gather.5.cloned.1.call-start = ((), (), s32[]{:S(2)}) async-start(), calls=%async_computation | async-start | bytes 20889600 | tf_op jit(solution)/shard_map/all_gather | solution.py:765
  11.1 352.8 %all-gather.9.cloned.1.call-start = ((), (), s32[]{:S(2)}) async-start(), calls=%async_computation.2 | async-start | bytes 20889600 | tf_op jit(solution)/shard_map/all_gather | solution.py:765
  11.8 379.0 %all-gather.7.cloned.1.call-start = ((), (), s32[]{:S(2)}) async-start(), calls=%async_computation.1 | async-start | bytes 20889600 | tf_op jit(solution)/shard_map/all_gather | solution.py:765
  12.5 475.0 %all-gather.11.cloned.1.call-start = ((), (), s32[]{:S(2)}) async-start(), calls=%async_computation.3 | async-start | bytes 20889600 | tf_op jit(solution)/shard_map/all_gather | solution.py:765
  128.0 6.6 copy-start
  134.7 22.2 %collective-permute-start = (bf16[1024,256]{1,0:T(8,128)(2,1)S(1)}, bf16[1024,256]{1,0:T(8,128)(2,1)S(1)}, u32[]{:S(2)}, u32[]{:S(2)}) collective-permute-start(bf16[1024,256]{1,0:T(8,128)(2,1)S(1)} %slice_select_fusion), channel_id=1, source_target_pairs={{0,4},{2,6},{1,5},{3,7},{8,12},{10,14},{9,13},{11,15},{16,20},{18,... | collective-permute-start | bytes 1572872 | tf_op jit(solution)/shard_map/ppermute | solution.py:757
  139.0 34.0 %collective-permute-start.1 = (bf16[1024,256]{1,0:T(8,128)(2,1)S(1)}, bf16[1024,256]{1,0:T(8,128)(2,1)S(1)}, u32[]{:S(2)}, u32[]{:S(2)}) collective-permute-start(bf16[1024,256]{1,0:T(8,128)(2,1)S(1)} %slice_select_fusion), channel_id=1, source_target_pairs={{0,2},{2,4},{4,6},{1,3},{3,5},{5,7},{8,10},{10,12},{12,14},{9,11},... | collective-permute-start | bytes 1572872 | tf_op jit(solution)/shard_map/ppermute | solution.py:757
  173.1 23.8 %collective-permute-start.2 = (bf16[2048,256]{1,0:T(8,128)(2,1)S(1)}, bf16[2048,256]{1,0:T(8,128)(2,1)S(1)}, u32[]{:S(2)}, u32[]{:S(2)}) collective-permute-start(bf16[2048,256]{1,0:T(8,128)(2,1)S(1)} %constant_dynamic-update-slice_fusion), channel_id=1, source_target_pairs={{0,1},{1,0},{2,3},{3,2},{4,5},{5,4},{6,7},{7,6},{8,9},{9,8},{10,11... | collective-permute-start | bytes 3145736 | tf_op jit(solution)/shard_map/ppermute | solution.py:761
  238.8 113.2 %collective-permute-start.3 = (bf16[1024,2560]{1,0:T(8,128)(2,1)}, bf16[1024,2560]{1,0:T(8,128)(2,1)}, u32[]{:S(2)}, u32[]{:S(2)}) collective-permute-start(bf16[1024,2560]{1,0:T(8,128)(2,1)} %product.3.refs_1_), channel_id=1, source_target_pairs={{0,1},{1,0},{2,3},{3,2},{4,5},{5,4},{6,7},{7,6},{8,9},{9,8},{10,11... | collective-permute-start | bytes 15728648 | tf_op jit(solution)/shard_map/ppermute | solution.py:761
  488.5 536.5 %copy-start.3 = (bf16[160,1280]{1,0:T(8,128)(2,1)S(1)}, bf16[160,1280]{1,0:T(8,128)(2,1)}, u32[]{:S(2)}) copy-start(bf16[160,1280]{1,0:T(8,128)(2,1)} %param.11) | copy-start | bytes 1228804
  1024.9 2.3 copy-start.1
  1027.2 3.8 copy-start.2
  1027.2 3.8 copy-start.4
  1027.2 3.8 copy-start.5
  1027.3 4.1 copy-start.7
  1031.0 10.3 slice-start.2
  1031.4 6.9 copy-start.8
  1031.4 6.9 copy-start.9
  1031.4 7.9 copy-start.6
  1031.4 7.9 copy-start.10
  1031.4 7.9 copy-start.11
  1031.4 8.7 copy-start.12
  1031.4 9.3 copy-start.13
  1031.4 9.9 slice-start.3
  1035.6 4.4 collective-permute-start.4
  1039.3 4.4 slice-start
  1041.3 2.4 slice-start.1
Sparse Core Ops, SparseCore 0:
  11.2 110.8 all-gather.4
  123.6 130.3 all-gather.8
  255.6 118.6 all-gather.6
  375.7 111.7 all-gather.10
